TPU v7x, 32 devices: a whole 2x2x4 slice. The times are simulated.
32 devices in a mesh: grp: 8 (over z, x), rep: 4 (over y, core).
Axes of the slice: x: 2, y: 2, z: 4, core: 2. Of those that a mesh axis runs over, the one named last changes fastest.
Arguments:
- activations: bfloat16 [32, 192, 6144], P(('grp', 'rep')), may hold values from -3 to 3
- cotangent: bfloat16 [32, 192, 6144], P(('grp', 'rep')), may hold values from -6 to 6
- documents: int32 [32, 192], P(('grp', 'rep')), may hold values from 0 to 3, never falling along the last dimension, each value on 1 to 96 neighbouring positions
- weight_copy: bfloat16 [6144, 256], P('grp'), may hold values from -0.078125 to 0.078125
- primary: float32 [6144, 256], P(('grp', 'rep')), may hold values from -0.0014648438 to 0.0014648438
- first_moment: float32 [6144, 256], P(('grp', 'rep')), may hold values from -1.5 to 1.5
- second_moment: float32 [6144, 256], P(('grp', 'rep')), may hold values from 0.001 to 0.1
Outputs:
- primary_new: float32 [6144, 256], P(('grp', 'rep'))
- first_new: float32 [6144, 256], P(('grp', 'rep'))
- second_new: float32 [6144, 256], P(('grp', 'rep'))
- copy_new: bfloat16 [6144, 256], P('grp')
Inputs may be any that keep to these rules, and one draw needn't show every extreme that they name: Within each row of 192 tokens the document numbers never fall; each of the 4 documents has 1 to 96 tokens, and one has exactly 96.
All inputs are finite; a program needn't handle non-finite values.
Results may differ from a plain program's by a relative error of at most 0.015.
Values may be sent and summed in bfloat16 or wider, within the bound.
No kernel may reach another device: no remote copies, remote signals or barrier semaphores. Data moves between devices by JAX's collectives and lax.ppermute only.
A program may use at most 64 MiB of HBM per device.

v0:
```python
import math

import jax
import jax.numpy as jnp
from jax import lax
from jax.sharding import PartitionSpec as P

BETA_FIRST = 0.9
BETA_SECOND = 0.95
LEARN_RATE = 6e-05
DECAY_RATE = 0.1
EPSILON = 1e-08
STEP_COUNT = 10.0


def term_block(feature_cols, cotan_cols, back_projected, context, grad_scale):
    left_part = jnp.einsum(
        "tr,tc->rc", feature_cols, back_projected, preferred_element_type=jnp.float32
    )
    right_part = jnp.einsum("tr,tc->rc", cotan_cols, context, preferred_element_type=jnp.float32)
    return jnp.concatenate([left_part, right_part], axis=1) * grad_scale


def body(activations, cotangent, documents, weight_copy, primary, first_moment, second_moment):
    features = activations[0]
    cotan_rows = cotangent[0]
    doc_row = documents[0]
    head_size = weight_copy.shape[1] // 4
    groups = lax.axis_size("grp")
    replicas = lax.axis_size("rep")
    token_count = features.shape[0]
    grad_scale = 1.0 / math.sqrt(groups * replicas * token_count)
    scale_value = 1.0 / math.sqrt(head_size)
    weight_piece = lax.all_gather(weight_copy, "grp", axis=0, tiled=True)
    feature_cols = features
    cotan_cols = cotan_rows
    front_part = jnp.dot(
        feature_cols, weight_piece[:, : 3 * head_size], preferred_element_type=jnp.float32
    )
    back_part = jnp.dot(
        cotan_cols, weight_piece[:, 3 * head_size :], preferred_element_type=jnp.float32
    )
    projected = front_part.astype(jnp.bfloat16)
    back_context = back_part.astype(jnp.bfloat16)
    queries = projected[:, :head_size]
    key_rows = projected[:, head_size : 2 * head_size]
    value_rows = projected[:, 2 * head_size :]
    scores = jnp.dot(queries, key_rows.T, preferred_element_type=jnp.float32) * scale_value
    position = jnp.arange(token_count, dtype=jnp.int32)
    allowed = (position[None, :] <= position[:, None]) & (doc_row[None, :] == doc_row[:, None])
    exp_scores = jnp.where(allowed, jnp.exp(jnp.where(allowed, scores, 0.0)), 0.0)
    attention = exp_scores / jnp.sum(exp_scores, axis=1, keepdims=True)
    attention_low = attention.astype(jnp.bfloat16)
    context = jnp.dot(attention_low, value_rows, preferred_element_type=jnp.float32).astype(
        jnp.bfloat16
    )
    back_attention = jnp.dot(back_context, value_rows.T, preferred_element_type=jnp.float32)
    back_values = jnp.dot(attention_low.T, back_context, preferred_element_type=jnp.float32).astype(
        jnp.bfloat16
    )
    inner_sum = jnp.sum(attention * back_attention, axis=1, keepdims=True)
    back_scores = (attention * (back_attention - inner_sum) * scale_value).astype(jnp.bfloat16)
    back_queries = jnp.dot(back_scores, key_rows, preferred_element_type=jnp.float32).astype(
        jnp.bfloat16
    )
    back_keys = jnp.dot(back_scores.T, queries, preferred_element_type=jnp.float32).astype(
        jnp.bfloat16
    )
    back_projected = jnp.concatenate([back_queries, back_keys, back_values], axis=1)
    feature_cols = features
    cotan_cols = cotan_rows
    partial_sum = lax.psum_scatter(
        term_block(feature_cols, cotan_cols, back_projected, context, grad_scale).astype(
            jnp.bfloat16
        ),
        "grp",
        scatter_dimension=0,
        tiled=True,
    )
    gradient = lax.psum_scatter(partial_sum, "rep", scatter_dimension=0, tiled=True).astype(
        jnp.float32
    )
    first_new = BETA_FIRST * first_moment + (1.0 - BETA_FIRST) * gradient
    second_new = BETA_SECOND * second_moment + (1.0 - BETA_SECOND) * gradient * gradient
    correct_first = 1.0 - BETA_FIRST**STEP_COUNT
    correct_second = 1.0 - BETA_SECOND**STEP_COUNT
    update = first_new / correct_first / (jnp.sqrt(second_new / correct_second) + EPSILON)
    primary_new = primary - LEARN_RATE * (update + DECAY_RATE * primary)
    copy_new = lax.all_gather(primary_new.astype(jnp.bfloat16), "rep", axis=0, tiled=True)
    return (primary_new, first_new, second_new, copy_new)


def solution(mesh):
    in_specs = (
        P(("grp", "rep"), None, None),
        P(("grp", "rep"), None, None),
        P(("grp", "rep"), None),
        P("grp", None),
        P(("grp", "rep"), None),
        P(("grp", "rep"), None),
        P(("grp", "rep"), None),
    )
    out_specs = (
        P(("grp", "rep"), None),
        P(("grp", "rep"), None),
        P(("grp", "rep"), None),
        P("grp", None),
    )
    return jax.shard_map(body, mesh=mesh, in_specs=in_specs, out_specs=out_specs, check_vma=False)
```

profile of v0, /device:TPU:0, one launch (start us, length us, event | category | flops | bytes accessed | tf_op | source)
XLA Modules:
  0.0 198.0 jit_solution(5090982162962548125)
XLA Ops:
  7.2 0.0 copy-start
  7.2 0.0 all-gather.2.cloned.1.call-start
  7.2 0.7 all-gather.2.cloned.1.call-update
  7.9 0.0 copy-start.7
  7.9 0.0 reduce-scatter.5.cloned.1.call-start
  8.0 65.4 %all-gather.2.cloned.1.call-done = bf16[6144,256]{1,0:T(8,128)(2,1)} async-done(((bf16[768,256]{1,0:T(8,128)(2,1)}), bf16[6144,256]{1,0:T(8,128)(2,1)}) %all-gather.2.cloned.1.call-update) | async-done | bytes 3145744 | tf_op jit(solution)/shard_map/all_gather | solution.py:34
  73.4 0.0 copy-done
  73.4 0.0 copy-start.1
  73.4 0.0 copy-start.3
  73.4 3.2 %fusion.12 = bf16[192,192]{0,1:T(8,128)(2,1)S(1)} fusion(bf16[6144,256]{1,0:T(8,128)(2,1)} %all-gather.2.cloned.1.call-done, bf16[1,192,6144]{2,1,0:T(8,128)(2,1)S(1)} %copy-done), kind=kOutput, calls=%fused_computation.16 | convolution fusion | flops 453021696 | bytes 5578752 | tf_op jit(solution)/shard_map/dot_general | solution.py:37
  76.6 0.0 copy-done.7
  76.6 0.3 fusion.45
  76.9 0.0 copy-done.1
  76.9 0.0 copy-done.3
  76.9 1.6 fusion.17
  78.5 0.1 convolution_convert_fusion.2
  78.7 0.3 multiply_reduce_fusion
  79.0 0.1 convolution_convert_fusion.3
  79.2 0.2 convolution_convert_fusion.1
  79.3 3.5 %convolution_bitcast_fusion.1 = f32[6144,64]{0,1:T(8,128)} fusion(bf16[1,192,6144]{2,1,0:T(8,128)(2,1)} %param.8, bf16[192,192]{0,1:T(8,128)(2,1)S(1)} %fusion.12, f32[192,192]{0,1:T(8,128)S(1)} %get-tuple-element.17, f32[192]{0:T(256)S(1)} %get-tuple-element.16), kind=kOutput, calls=%fused_computation.1 | convolution fusion | flops 155799552 | bytes 4162560 | tf_op jit(solution)/shard_map/tr,tc->rc/dot_general | solution.py:20
  82.9 0.0 copy-start.2
  82.9 0.8 convolution_bitcast_fusion
  83.7 0.6 copy-done.2
  84.3 2.2 %fusion = bf16[6144,256]{0,1:T(8,128)(2,1)} fusion(f32[6144,64]{0,1:T(8,128)S(1)} %copy-done.2, f32[6144,192]{0,1:T(8,128)S(1)} %convolution_bitcast_fusion), kind=kLoop, calls=%fused_computation.3 | loop fusion | flops 4718592 | bytes 9437184 | tf_op jit(solution)/shard_map/convert_element_type | solution.py:73
  86.5 0.0 copy-start.4
  86.5 0.0 copy-start.5
  86.5 0.0 copy-start.6
  86.5 0.0 reduce-scatter.5.cloned.1.call-update
  86.5 0.0 reduce-scatter.7.cloned.1.call-start
  86.6 73.2 %reduce-scatter.5.cloned.1.call-done = bf16[768,256]{0,1:T(8,128)(2,1)} async-done(((bf16[6144,256]{0,1:T(8,128)(2,1)}), bf16[768,256]{0,1:T(8,128)(2,1)}) %reduce-scatter.5.cloned.1.call-update) | async-done | bytes 393232 | tf_op jit(solution)/shard_map/reduce_scatter | solution.py:72
  159.7 1.9 copy.28
  161.7 0.0 reduce-scatter.7.cloned.1.call-update
  161.7 21.1 %reduce-scatter.7.cloned.1.call-done = bf16[192,256]{1,0:T(8,128)(2,1)} async-done(((bf16[768,256]{1,0:T(8,128)(2,1)}), bf16[192,256]{1,0:T(8,128)(2,1)}) %reduce-scatter.7.cloned.1.call-update) | async-done | bytes 98320 | tf_op jit(solution)/shard_map/reduce_scatter | solution.py:80
  182.8 0.0 copy-done.4
  182.8 0.0 copy-done.5
  182.8 0.0 copy-done.6
  182.8 1.8 fusion.42
  184.6 6.1 %all_gather.7 = bf16[768,256]{1,0:T(8,128)(2,1)S(1)} all-gather(bf16[192,256]{1,0:T(8,128)(2,1)S(1)} %get-tuple-element.12), channel_id=1, replica_groups=mesh['grp'=8,'rep'=4] {'rep'}, dimensions={0}, use_global_device_ids=true | all-gather | bytes 491520 | tf_op jit(solution)/shard_map/all_gather | solution.py:89
  190.7 0.7 copy.31
  (1 shorter events, 0.0 us)
Async XLA Ops:
  7.2 66.2 %copy-start = (bf16[1,192,6144]{2,1,0:T(8,128)(2,1)S(1)}, bf16[1,192,6144]{2,1,0:T(8,128)(2,1)}, u32[]{:S(2)}) copy-start(bf16[1,192,6144]{2,1,0:T(8,128)(2,1)} %param.7) | copy-start | bytes 7077892
  7.2 66.2 %all-gather.2.cloned.1.call-start = ((), (), s32[]{:S(2)}) async-start(), calls=%async_computation.2 | async-start | bytes 3538944 | tf_op jit(solution)/shard_map/all_gather | solution.py:34
  7.9 68.7 %copy-start.7 = (s32[1,192]{1,0:T(1,128)S(1)}, s32[1,192]{1,0:T(1,128)}, u32[]{:S(2)}) copy-start(s32[1,192]{1,0:T(1,128)} %param.9) | copy-start | bytes 2308
  7.9 151.8 %reduce-scatter.5.cloned.1.call-start = ((), (), s32[]{:S(2)}) async-start(), calls=%async_computation.3 | async-start | bytes 3538944 | tf_op jit(solution)/shard_map/reduce_scatter | solution.py:72
  73.4 3.5 %copy-start.1 = (bf16[1,192,6144]{2,1,0:T(8,128)(2,1)S(1)}, bf16[1,192,6144]{2,1,0:T(8,128)(2,1)}, u32[]{:S(2)}) copy-start(bf16[1,192,6144]{2,1,0:T(8,128)(2,1)} %param.8) | copy-start | bytes 7077892
  73.4 3.5 %copy-start.3 = (bf16[6144,256]{1,0:T(8,128)(2,1)S(1)}, bf16[6144,256]{1,0:T(8,128)(2,1)}, u32[]{:S(2)}) copy-start(bf16[6144,256]{1,0:T(8,128)(2,1)} %all-gather.2.cloned.1.call-done) | copy-start | bytes 9437188
  82.9 1.4 copy-start.2
  86.5 96.3 %copy-start.4 = (f32[192,256]{1,0:T(8,128)S(1)}, f32[192,256]{1,0:T(8,128)}, u32[]{:S(2)}) copy-start(f32[192,256]{1,0:T(8,128)} %param.11) | copy-start | bytes 589828
  86.5 96.3 %copy-start.5 = (f32[192,256]{1,0:T(8,128)S(1)}, f32[192,256]{1,0:T(8,128)}, u32[]{:S(2)}) copy-start(f32[192,256]{1,0:T(8,128)} %param.12) | copy-start | bytes 589828
  86.5 96.3 %copy-start.6 = (f32[192,256]{1,0:T(8,128)S(1)}, f32[192,256]{1,0:T(8,128)}, u32[]{:S(2)}) copy-start(f32[192,256]{1,0:T(8,128)} %param.13) | copy-start | bytes 589828
  86.5 96.3 %reduce-scatter.7.cloned.1.call-start = ((), (), s32[]{:S(2)}) async-start(), calls=%async_computation.4 | async-start | bytes 491520 | tf_op jit(solution)/shard_map/reduce_scatter | solution.py:80
Sparse Core Ops, SparseCore 0:
  10.2 63.1 all-gather.1
  86.6 73.0 reduce-scatter.4
  162.8 19.9 reduce-scatter.6
where the time goes:
time: 198 us
  waiting for transfers between devices  160 us (81%)
  between operations  13.8 us (7%)
  matrix products  10.1 us (5%)
  blocking collectives  6.13 us (3%)
  other arithmetic  4.04 us (2%)
  local copies, waits for them, and re-layouts  3.35 us (2%)
    reduce_scatter x1, waiting for transfers between devices, body(): lax.psum_scatter(term_block(feature_cols, cotan_cols, back_projected, con...  73.2 us
    all_gather x1, waiting for transfers between devices, body(): weight_piece = lax.all_gather(weight_copy, 'grp', axis=0, tiled=True)  65.4 us
    reduce_scatter x1, waiting for transfers between devices, body(): lax.psum_scatter(partial_sum, 'rep', scatter_dimension=0, tiled=True)  21.1 us
    all_gather x1, blocking collectives, body(): lax.all_gather(primary_new.astype(jnp.bfloat16), 'rep', axis=0, tiled=True)  6.13 us
  transfers between devices with their start and end apart: 3, of which 3 were waited for; matrix products, arithmetic and copies ran while one was open for 0% of the time, Pallas kernels for 0%

commit v1 on v0

v1 whole, which is shorter than its diff:
```python
import functools
import math

import jax
import jax.numpy as jnp
from jax import lax
from jax.experimental import pallas as pl
from jax.experimental.pallas import tpu as pltpu
from jax.sharding import PartitionSpec as P

BETA_FIRST = 0.9
BETA_SECOND = 0.95
LEARN_RATE = 6e-05
DECAY_RATE = 0.1
EPSILON = 1e-08
STEP_COUNT = 10.0

AXES = ("grp", "rep")
MIB = 1024 * 1024


def adam(gradient, primary, first_moment, second_moment):
    first_new = BETA_FIRST * first_moment + (1.0 - BETA_FIRST) * gradient
    second_new = BETA_SECOND * second_moment + (1.0 - BETA_SECOND) * gradient * gradient
    correct_first = 1.0 - BETA_FIRST**STEP_COUNT
    correct_second = 1.0 - BETA_SECOND**STEP_COUNT
    update = first_new / correct_first / (jnp.sqrt(second_new / correct_second) + EPSILON)
    primary_new = primary - LEARN_RATE * (update + DECAY_RATE * primary)
    return primary_new, first_new, second_new


def plain_body(activations, cotangent, documents, weight_copy, primary, first_moment, second_moment):
    features = activations[0]
    cotan_rows = cotangent[0]
    doc_row = documents[0]
    head = weight_copy.shape[1] // 4
    token_count = features.shape[0]
    grad_scale = 1.0 / math.sqrt(lax.axis_size("grp") * lax.axis_size("rep") * token_count)
    scale_value = 1.0 / math.sqrt(head)
    dot = functools.partial(jnp.dot, preferred_element_type=jnp.float32)
    weights = lax.all_gather(weight_copy, "grp", axis=0, tiled=True)
    projected = dot(features, weights[:, : 3 * head]).astype(jnp.bfloat16)
    back_context = dot(cotan_rows, weights[:, 3 * head :]).astype(jnp.bfloat16)
    queries, key_rows, value_rows = jnp.split(projected, 3, axis=1)
    scores = dot(queries, key_rows.T) * scale_value
    position = jnp.arange(token_count, dtype=jnp.int32)
    allowed = (position[None, :] <= position[:, None]) & (doc_row[None, :] == doc_row[:, None])
    exp_scores = jnp.where(allowed, jnp.exp(jnp.where(allowed, scores, 0.0)), 0.0)
    attention = exp_scores / jnp.sum(exp_scores, axis=1, keepdims=True)
    attention_low = attention.astype(jnp.bfloat16)
    context = dot(attention_low, value_rows).astype(jnp.bfloat16)
    back_attention = dot(back_context, value_rows.T)
    back_values = dot(attention_low.T, back_context).astype(jnp.bfloat16)
    inner_sum = jnp.sum(attention * back_attention, axis=1, keepdims=True)
    back_scores = (attention * (back_attention - inner_sum) * scale_value).astype(jnp.bfloat16)
    back_queries = dot(back_scores, key_rows).astype(jnp.bfloat16)
    back_keys = dot(back_scores.T, queries).astype(jnp.bfloat16)
    back_projected = jnp.concatenate([back_queries, back_keys, back_values], axis=1)
    term = jnp.concatenate([dot(features.T, back_projected), dot(cotan_rows.T, context)], axis=1)
    term = (term * grad_scale).astype(jnp.bfloat16)
    partial_sum = lax.psum_scatter(term, "grp", scatter_dimension=0, tiled=True)
    gradient = lax.psum_scatter(partial_sum, "rep", scatter_dimension=0, tiled=True)
    primary_new, first_new, second_new = adam(
        gradient.astype(jnp.float32), primary, first_moment, second_moment
    )
    copy_new = lax.all_gather(primary_new.astype(jnp.bfloat16), "rep", axis=0, tiled=True)
    return primary_new, first_new, second_new, copy_new


def hop(value, kz, kx, ky, kc):
    offset = (kz * 2 + kx) * 4 + ky * 2 + kc
    return lax.ppermute(value, AXES, [(i, i ^ offset) for i in range(32)])


def join(*parts):
    return jnp.concatenate(parts, axis=0)


def block_start(kz, kx, ky, kc, rows):
    me = lax.axis_index("grp") * 4 + lax.axis_index("rep")
    offset = (kz * 2 + kx) * 4 + ky * 2 + kc
    return pl.multiple_of(lax.bitwise_xor(me, jnp.int32(offset)) * rows, rows)


def turn_kernel(a_ref, b_ref, at_ref, bt_ref, *, step):
    for source, target in ((a_ref, at_ref), (b_ref, bt_ref)):
        for start in range(0, source.shape[1], step):
            target[start : start + step, :] = source[:, start : start + step].T


def fdot(a, b, dims):
    return lax.dot_general(a, b, (dims, ((), ())), preferred_element_type=jnp.float32)


MM = ((1,), (0,))
MT = ((1,), (1,))
TM = ((0,), (0,))


def attend_kernel(places, rows, head, grad_scale, *refs):
    count = len(places)
    pieces = refs[:count]
    acts, cots, doc_row, doc_col, acts_t, cots_t = refs[count : count + 6]
    other_ref, left_ref, right_ref = refs[count + 6 : count + 9]
    weights = refs[count + 9]
    for piece, place in zip(pieces, places):
        for index, where in enumerate(place):
            if where is None:
                size = piece.shape[0]
                start = pl.multiple_of(lax.axis_index("grp") * size, size)
                weights[pl.ds(start, size), :] = piece[...]
            else:
                weights[pl.ds(block_start(*where, rows), rows), :] = piece[
                    index * rows : (index + 1) * rows, :
                ]
    projected = fdot(acts[...], weights[:, : 3 * head], MM).astype(jnp.bfloat16)
    back_context = fdot(cots[...], weights[:, 3 * head :], MM).astype(jnp.bfloat16)
    queries = projected[:, :head]
    key_rows = projected[:, head : 2 * head]
    value_rows = projected[:, 2 * head :]
    scale_value = 1.0 / math.sqrt(head)
    scores = fdot(queries, key_rows, MT) * scale_value
    tokens = scores.shape[0]
    here = lax.broadcasted_iota(jnp.int32, (tokens, tokens), 0)
    there = lax.broadcasted_iota(jnp.int32, (tokens, tokens), 1)
    allowed = (there <= here) & (doc_row[...] == doc_col[...])
    exp_scores = jnp.where(allowed, jnp.exp(jnp.where(allowed, scores, 0.0)), 0.0)
    attention = exp_scores / jnp.sum(exp_scores, axis=1, keepdims=True)
    attention_low = attention.astype(jnp.bfloat16)
    context = fdot(attention_low, value_rows, MM).astype(jnp.bfloat16)
    back_attention = fdot(back_context, value_rows, MT)
    back_values = fdot(attention_low, back_context, TM).astype(jnp.bfloat16)
    inner_sum = jnp.sum(attention * back_attention, axis=1, keepdims=True)
    back_scores = (attention * (back_attention - inner_sum) * scale_value).astype(jnp.bfloat16)
    back_queries = fdot(back_scores, key_rows, MM).astype(jnp.bfloat16)
    back_keys = fdot(back_scores, queries, TM).astype(jnp.bfloat16)
    none = jnp.zeros((tokens, head), jnp.bfloat16)
    left = jnp.concatenate([back_queries, back_keys, back_values, none], axis=1)
    right = jnp.concatenate([none, none, none, context], axis=1)
    left_ref[...] = left
    right_ref[...] = right
    write_terms(acts_t, cots_t, left, right, other_ref, 1, rows, grad_scale)


def write_terms(acts_t, cots_t, left, right, out_ref, kc, rows, grad_scale):
    for index in range(16):
        start = block_start(index // 4, index // 2 % 2, index % 2, kc, rows)
        term = fdot(acts_t[pl.ds(start, rows), :], left, MM)
        term += fdot(cots_t[pl.ds(start, rows), :], right, MM)
        out_ref[index * rows : (index + 1) * rows, :] = (term * grad_scale).astype(out_ref.dtype)


def mine_kernel(rows, grad_scale, acts_t, cots_t, left_ref, right_ref, out_ref):
    write_terms(acts_t, cots_t, left_ref[...], right_ref[...], out_ref, 0, rows, grad_scale)


def vmem(count):
    return [pl.BlockSpec(memory_space=pltpu.VMEM)] * count


def kernel_call(body, outs, name, args, scratch=(), flops=0, limit=24):
    return pl.pallas_call(
        body,
        out_shape=outs,
        in_specs=vmem(len(args)),
        out_specs=vmem(len(outs)),
        scratch_shapes=scratch,
        name=name,
        compiler_params=pltpu.CompilerParams(vmem_limit_bytes=limit * MIB),
        cost_estimate=pl.CostEstimate(flops=flops, bytes_accessed=4 * MIB, transcendentals=0),
    )(*args)


def gather(weight_copy, rows):
    rep = lax.axis_index("rep")
    own = lax.dynamic_slice_in_dim(weight_copy, rep * rows, rows, 0)
    half = lax.dynamic_slice_in_dim(weight_copy, jnp.bitwise_xor(rep, 2) * rows, rows, 0)
    z2 = hop(own, 2, 0, 0, 0)
    z1 = hop(own, 1, 0, 0, 0)
    x0 = hop(join(own, half), 0, 1, 0, 0)
    z12 = join(z1, z2)
    z3 = hop(z2, 1, 0, 0, 0)
    x12 = hop(z12, 0, 1, 0, 0)
    y12 = hop(z12, 0, 0, 1, 0)
    c0 = hop(join(z12, x0), 0, 0, 0, 1)
    x3 = hop(z3, 0, 1, 0, 0)
    ya = hop(join(z3, x12), 0, 0, 1, 0)
    c1 = hop(join(z3, x12, y12), 0, 0, 0, 1)
    yb = hop(x3, 0, 0, 1, 0)
    c2 = hop(join(x3, ya, yb), 0, 0, 0, 1)
    z12_at = [(1, 0, 0), (2, 0, 0)]
    x0_at = [(0, 1, 0), (0, 1, 1)]
    x12_at = [(1, 1, 0), (2, 1, 0)]
    y12_at = [(1, 0, 1), (2, 0, 1)]
    z3_at, x3_at, yb_at = [(3, 0, 0)], [(3, 1, 0)], [(3, 1, 1)]
    ya_at = [(3, 0, 1), (1, 1, 1), (2, 1, 1)]

    def core(kc, *lists):
        return [(*at, kc) for one in lists for at in one]

    return [
        (weight_copy, [None]),
        (z12, core(0, z12_at)),
        (x0, core(0, x0_at)),
        (z3, core(0, z3_at)),
        (x12, core(0, x12_at)),
        (y12, core(0, y12_at)),
        (x3, core(0, x3_at)),
        (ya, core(0, ya_at)),
        (yb, core(0, yb_at)),
        (c0, core(1, z12_at, x0_at)),
        (c1, core(1, z3_at, x12_at, y12_at)),
        (c2, core(1, x3_at, ya_at, yb_at)),
    ]


def scatter(mine, other, rows):
    received = hop(other, 0, 0, 0, 1)

    def block(kz, kx, ky):
        start = ((kz * 2 + kx) * 2 + ky) * rows
        both = mine[start : start + rows] + received[start : start + rows].astype(jnp.float32)
        return both

    def send(at, kz, kx, ky):
        return hop(join(*[block(*one).astype(jnp.bfloat16) for one in at]), kz, kx, ky, 0)

    got = {}
    for pair in ((3, 2), (1, 0)):
        for kx, ky in ((1, 1), (1, 0), (0, 1)):
            came = send([(kz, kx, ky) for kz in pair], 0, kx, ky)
            for index, kz in enumerate(pair):
                got.setdefault(kz, []).append(came[index * rows : (index + 1) * rows])
    totals = {kz: block(kz, 0, 0) + sum(one.astype(jnp.float32) for one in got[kz]) for kz in got}
    gradient = totals[0]
    for kz in (3, 2, 1):
        gradient += hop(totals[kz].astype(jnp.bfloat16), kz, 0, 0, 0).astype(jnp.float32)
    return gradient


def block_body(activations, cotangent, documents, weight_copy, primary, first_moment, second_moment):
    acts, cots = activations[0], cotangent[0]
    tokens, depth = acts.shape
    columns = weight_copy.shape[1]
    rows = primary.shape[0]
    head = columns // 4
    grad_scale = 1.0 / math.sqrt(32 * tokens)
    turned = jax.ShapeDtypeStruct((depth, tokens), jnp.bfloat16)
    acts_t, cots_t = kernel_call(
        functools.partial(turn_kernel, step=512), [turned, turned], "turn", (acts, cots)
    )
    pieces = gather(weight_copy, rows)
    places = [place for _, place in pieces]
    side = jax.ShapeDtypeStruct((tokens, columns), jnp.bfloat16)
    other, left, right = kernel_call(
        functools.partial(attend_kernel, places, rows, head, grad_scale),
        [jax.ShapeDtypeStruct((16 * rows, columns), jnp.bfloat16), side, side],
        "attend",
        (
            *[piece for piece, _ in pieces],
            acts,
            cots,
            documents,
            documents.reshape(tokens, 1),
            acts_t,
            cots_t,
        ),
        scratch=[pltpu.VMEM((depth, columns), jnp.bfloat16)],
        flops=4 * tokens * depth * columns,
        limit=32,
    )
    (mine,) = kernel_call(
        functools.partial(mine_kernel, rows, grad_scale),
        [jax.ShapeDtypeStruct((16 * rows, columns), jnp.float32)],
        "mine",
        (acts_t, cots_t, left, right),
        flops=2 * tokens * depth * columns,
    )
    gradient = scatter(mine, other, rows)
    primary_new, first_new, second_new = adam(gradient, primary, first_moment, second_moment)
    copy_new = lax.all_gather(primary_new.astype(jnp.bfloat16), "rep", axis=0, tiled=True)
    return primary_new, first_new, second_new, copy_new


def chosen_body(activations, cotangent, documents, weight_copy, primary, first_moment, second_moment):
    blocks = lax.axis_size("grp") == 8 and lax.axis_size("rep") == 4
    tiled = primary.shape[0] % 16 == 0 and activations.shape[1] % 16 == 0
    args = (activations, cotangent, documents, weight_copy, primary, first_moment, second_moment)
    return block_body(*args) if blocks and tiled else plain_body(*args)


def solution(mesh):
    in_specs = (
        P(("grp", "rep"), None, None),
        P(("grp", "rep"), None, None),
        P(("grp", "rep"), None),
        P("grp", None),
        P(("grp", "rep"), None),
        P(("grp", "rep"), None),
        P(("grp", "rep"), None),
    )
    out_specs = (
        P(("grp", "rep"), None),
        P(("grp", "rep"), None),
        P(("grp", "rep"), None),
        P("grp", None),
    )
    return jax.shard_map(chosen_body, mesh=mesh, in_specs=in_specs, out_specs=out_specs, check_vma=False)
```

time: 198 us -> 83.5 us (0.42)
  waiting for transfers between devices: 160 us -> 34.8 us
  starting transfers between devices: 0.12 us -> 25.8 us
  between operations: 13.8 us -> 0.91 us
  matrix products: 10.1 us -> 0 us
  Pallas kernels: 0 us -> 7.26 us
    reduce_scatter x2 -> x0, waiting for transfers between devices: 94.3 us -> none  [the longest x1 73.2 us: body(): lax.psum_scatter(term_block(feature_cols, cotan_cols, back_projected, con...]
    all_gather x1 -> x0, waiting for transfers between devices: 65.4 us -> none  [body(): weight_piece = lax.all_gather(weight_copy, 'grp', axis=0, tiled=True)]
    ppermute x0 -> x22, waiting for transfers between devices: none -> 34.8 us  [hop(): return lax.ppermute(value, AXES, [(i, i ^ offset) for i in range(32)])]
    ppermute x0 -> x22, starting transfers between devices: none -> 25.8 us  [hop(): return lax.ppermute(value, AXES, [(i, i ^ offset) for i in range(32)])]
    dot_general x9 -> x0, matrix products: 10.1 us -> none  [the longest x1 3.54 us: term_block(): jnp.einsum('tr,tc->rc', cotan_cols, context, preferred_element_type=jnp.f...]
    pallas_call x0 -> x3, Pallas kernels: none -> 7.26 us  [kernel_call(): pl.pallas_call(body, out_shape=outs, in_specs=vmem(len(args)), out_specs=...]
    convert_element_type x3 -> x4, other arithmetic: 4.04 us -> 1.46 us  [the longest x1 1 us: block_body(): primary_new.astype(jnp.bfloat16)]
    concatenate x0 -> x11, other arithmetic: none -> 2.54 us  [join(): return jnp.concatenate(parts, axis=0)]
  transfers between devices with their start and end apart: 3 -> 22, of which waited for: 3 -> 12; matrix products, arithmetic and copies ran while one was open for 0% -> 4% of each run, Pallas kernels for 0% -> 3%
where the time goes in v1:
time: 83.5 us; the launch traced here: 83.3 us
  waiting for transfers between devices  34.8 us (42%)
  starting transfers between devices  25.8 us (31%)
  Pallas kernels  7.26 us (9%)
  blocking collectives  6.19 us (7%)
  local copies, waits for them, and re-layouts  4.36 us (5%)
  other arithmetic  4 us (5%)
  between operations  0.91 us (1%)
    ppermute x22, waiting for transfers between devices, hop(): return lax.ppermute(value, AXES, [(i, i ^ offset) for i in range(32)])  34.8 us
    ppermute x22, starting transfers between devices, hop(): return lax.ppermute(value, AXES, [(i, i ^ offset) for i in range(32)])  25.8 us
    pallas_call x3, Pallas kernels, kernel_call(): pl.pallas_call(body, out_shape=outs, in_specs=vmem(len(args)), out_specs=...  7.26 us
    all_gather x1, blocking collectives, block_body(): lax.all_gather(primary_new.astype(jnp.bfloat16), 'rep', axis=0, tiled=True)  6.19 us
    concatenate x11, other arithmetic, join(): return jnp.concatenate(parts, axis=0)  2.54 us
    unnamed x28, local copies, waits for them, and re-layouts  2.47 us
  transfers between devices with their start and end apart: 22, of which 12 were waited for; matrix products, arithmetic and copies ran while one was open for 4% of the time, Pallas kernels for 3%

profile of v1, /device:TPU:0, one launch (start us, length us, event | category | flops | bytes accessed | tf_op | source)
XLA Modules:
  0.0 83.3 jit_solution(603604611468526619)
XLA Ops:
  0.7 1.1 %constant_dynamic-slice_fusion = (bf16[192,256]{1,0:T(8,128)(2,1)S(1)}, bf16[192,256]{1,0:T(8,128)(2,1)S(1)}) fusion(bf16[768,256]{1,0:T(8,128)(2,1)} %refs_0_.1, s32[]{:T(128)S(6)} %select_n.7, s32[]{:T(128)S(6)} %select_n.6), kind=kLoop, calls=%fused_computation.55 | loop fusion | bytes 393224 | tf_op jit(solution)/shard_map/dynamic_slice | solution.py:177
  1.8 3.1 %collective-permute-start = (bf16[192,256]{1,0:T(8,128)(2,1)S(1)}, bf16[192,256]{1,0:T(8,128)(2,1)S(1)}, u32[]{:S(2)}, u32[]{:S(2)}) collective-permute-start(bf16[192,256]{1,0:T(8,128)(2,1)S(1)} %get-tuple-element.34), channel_id=1, source_target_pairs={{0,8},{1,9},{2,10},{3,11},{4,12},{5,13},{6,14},{7,15},{8,0},{9,1},... | collective-permute-start | bytes 294920 | tf_op jit(solution)/shard_map/ppermute | solution.py:72
  4.9 2.6 %collective-permute-start.1 = (bf16[192,256]{1,0:T(8,128)(2,1)S(1)}, bf16[192,256]{1,0:T(8,128)(2,1)S(1)}, u32[]{:S(2)}, u32[]{:S(2)}) collective-permute-start(bf16[192,256]{1,0:T(8,128)(2,1)S(1)} %get-tuple-element.34), channel_id=1, source_target_pairs={{0,16},{1,17},{2,18},{3,19},{4,20},{5,21},{6,22},{7,23},{8,24},{9,... | collective-permute-start | bytes 294920 | tf_op jit(solution)/shard_map/ppermute | solution.py:72
  7.5 0.2 collective-permute-done
  7.7 4.5 %collective-permute-done.1 = bf16[192,256]{1,0:T(8,128)(2,1)S(1)} collective-permute-done((bf16[192,256]{1,0:T(8,128)(2,1)S(1)}, bf16[192,256]{1,0:T(8,128)(2,1)S(1)}, u32[]{:S(2)}, u32[]{:S(2)}) %collective-permute-start.1) | collective-permute-done | bytes 98336 | tf_op jit(solution)/shard_map/ppermute | solution.py:72
  12.2 1.6 %collective-permute-start.4 = (bf16[384,256]{1,0:T(8,128)(2,1)S(1)}, bf16[384,256]{1,0:T(8,128)(2,1)S(1)}, u32[]{:S(2)}, u32[]{:S(2)}) collective-permute-start(bf16[384,256]{1,0:T(8,128)(2,1)S(1)} %constant_dynamic-update-slice_fusion.refs_1_), channel_id=1, source_target_pairs={{0,4},{1,5},{2,6},{3,7},{4,0},{5,1},{6,2},{7,3},{8,12},{9,13},{10,... | collective-permute-start | bytes 589832 | tf_op jit(solution)/shard_map/ppermute | solution.py:72
  13.7 0.3 collective-permute-start.3
  14.1 1.5 %collective-permute-start.5 = (bf16[384,256]{1,0:T(8,128)(2,1)S(1)}, bf16[384,256]{1,0:T(8,128)(2,1)S(1)}, u32[]{:S(2)}, u32[]{:S(2)}) collective-permute-start(bf16[384,256]{1,0:T(8,128)(2,1)S(1)} %constant_dynamic-update-slice_fusion.refs_1_), channel_id=1, source_target_pairs={{0,2},{1,3},{2,0},{3,1},{4,6},{5,7},{6,4},{7,5},{8,10},{9,11},{10,... | collective-permute-start | bytes 589832 | tf_op jit(solution)/shard_map/ppermute | solution.py:72
  15.6 2.8 %collective-permute-done.3.refs_3_ = bf16[192,256]{1,0:T(8,128)(2,1)S(1)} collective-permute-done((bf16[192,256]{1,0:T(8,128)(2,1)S(1)}, bf16[192,256]{1,0:T(8,128)(2,1)S(1)}, u32[]{:S(2)}, u32[]{:S(2)}) %collective-permute-start.3) | collective-permute-done | bytes 98336 | tf_op jit(solution)/shard_map/ppermute | solution.py:72
  18.4 0.0 collective-permute-done.4.refs_4_
  18.4 1.9 %collective-permute-start.7 = (bf16[576,256]{1,0:T(8,128)(2,1)S(1)}, bf16[576,256]{1,0:T(8,128)(2,1)S(1)}, u32[]{:S(2)}, u32[]{:S(2)}) collective-permute-start(bf16[576,256]{1,0:T(8,128)(2,1)S(1)} %pad_maximum_fusion.3), channel_id=1, source_target_pairs={{0,2},{1,3},{2,0},{3,1},{4,6},{5,7},{6,4},{7,5},{8,10},{9,11},{10,... | collective-permute-start | bytes 884744 | tf_op jit(solution)/shard_map/ppermute | solution.py:72
  20.3 2.1 %collective-permute-start.6 = (bf16[192,256]{1,0:T(8,128)(2,1)S(1)}, bf16[192,256]{1,0:T(8,128)(2,1)S(1)}, u32[]{:S(2)}, u32[]{:S(2)}) collective-permute-start(bf16[192,256]{1,0:T(8,128)(2,1)S(1)} %collective-permute-done.3.refs_3_), channel_id=1, source_target_pairs={{0,4},{1,5},{2,6},{3,7},{4,0},{5,1},{6,2},{7,3},{8,12},{9,13},{10,... | collective-permute-start | bytes 294920 | tf_op jit(solution)/shard_map/ppermute | solution.py:72
  22.4 0.1 collective-permute-start.2
  22.5 2.5 %collective-permute-done.6.refs_6_ = bf16[192,256]{1,0:T(8,128)(2,1)S(1)} collective-permute-done((bf16[192,256]{1,0:T(8,128)(2,1)S(1)}, bf16[192,256]{1,0:T(8,128)(2,1)S(1)}, u32[]{:S(2)}, u32[]{:S(2)}) %collective-permute-start.6) | collective-permute-done | bytes 98336 | tf_op jit(solution)/shard_map/ppermute | solution.py:72
  25.0 0.1 collective-permute-start.8
  25.1 0.0 collective-permute-done.5.refs_5_
  25.1 0.8 pad_maximum_fusion
  25.9 0.0 collective-permute-start.10
  25.9 3.7 %collective-permute-done.8.refs_8_ = bf16[192,256]{1,0:T(8,128)(2,1)S(1)} collective-permute-done((bf16[192,256]{1,0:T(8,128)(2,1)S(1)}, bf16[192,256]{1,0:T(8,128)(2,1)S(1)}, u32[]{:S(2)}, u32[]{:S(2)}) %collective-permute-start.8) | collective-permute-done | bytes 98336 | tf_op jit(solution)/shard_map/ppermute | solution.py:72
  29.6 0.0 collective-permute-done.7.refs_7_
  29.6 0.8 pad_maximum_fusion.1
  30.5 0.0 collective-permute-start.11
  30.5 0.0 collective-permute-done.2.refs_2_
  30.5 0.8 pad_maximum_fusion.2
  31.2 0.5 collective-permute-start.9
  31.7 0.0 copy-done.9
  31.8 0.8 copy.11.refs_15_
  32.5 1.7 %copy-done.1 = bf16[1,192,6144]{2,1,0:T(8,128)(2,1)S(1)} copy-done((bf16[1,192,6144]{2,1,0:T(8,128)(2,1)S(1)}, bf16[1,192,6144]{2,1,0:T(8,128)(2,1)}, u32[]{:S(2)}) %copy-start.1) | copy-done | bytes 2359320
  34.2 0.0 copy-start.8
  34.2 1.7 %turn.1 = (bf16[6144,192]{1,0:T(8,128)(2,1)S(1)}, bf16[6144,192]{1,0:T(8,128)(2,1)S(1)}) custom-call(bf16[192,6144]{1,0:T(8,128)(2,1)S(1)} %bitcast.3, bf16[192,6144]{1,0:T(8,128)(2,1)S(1)} %bitcast.5), custom_call_target="tpu_custom_call" | custom-call | bytes 4194304 | tf_op jit(solution)/shard_map/turn/pallas_call | solution.py:162
  35.9 0.0 collective-permute-done.9.refs_9_
  35.9 0.0 collective-permute-done.10.refs_10_
  35.9 0.0 collective-permute-done.11.refs_11_
  36.0 4.6 %attend.1 = (bf16[3072,256]{1,0:T(8,128)(2,1)S(1)}, bf16[192,256]{1,0:T(8,128)(2,1)S(1)}, bf16[192,256]{1,0:T(8,128)(2,1)S(1)}) custom-call(bf16[768,256]{1,0:T(8,128)(2,1)S(1)} %copy-done.3, bf16[384,256]{1,0:T(8,128)(2,1)S(1)} %constant_dynamic-update-slice_fusion.refs_1_, bf16[384,256]{1,0:T(8,128)(2,1)S(1)} %collective-permute-done.2.refs_2_, ...), custom_call_target="tpu_custom_call" | custom-call | flops 1207959552 | bytes 4194304 | tf_op jit(solution)/shard_map/attend/pallas_call | solution.py:162
  40.6 0.1 collective-permute-start.12
  40.7 1.0 %mine.1 = f32[3072,256]{1,0:T(8,128)S(1)} custom-call(bf16[6144,192]{1,0:T(8,128)(2,1)S(1)} %get-tuple-element.9.refs_16_.acts_t, bf16[6144,192]{1,0:T(8,128)(2,1)S(1)} %get-tuple-element.10.refs_17_.cots_t, bf16[192,256]{1,0:T(8,128)(2,1)S(1)} %get-tuple-element.11.left_ref, bf16[192,256]{1,0:T(8,128)(2,1)S(1)} %get-tuple-element.12.right_ref), custom_call_target="tpu_custom_call" | custom-call | flops 603979776 | bytes 4194304 | tf_op jit(solution)/shard_map/mine/pallas_call | solution.py:162
  41.7 2.4 %collective-permute-done.12 = bf16[3072,256]{1,0:T(8,128)(2,1)S(1)} collective-permute-done((bf16[3072,256]{1,0:T(8,128)(2,1)S(1)}, bf16[3072,256]{1,0:T(8,128)(2,1)S(1)}, u32[]{:S(2)}, u32[]{:S(2)}) %collective-permute-start.12) | collective-permute-done | bytes 1572896 | tf_op jit(solution)/shard_map/ppermute | solution.py:72
  44.1 0.1 fusion.18
  44.2 1.6 %collective-permute-start.13 = (bf16[384,256]{1,0:T(8,128)(2,1)S(1)}, bf16[384,256]{1,0:T(8,128)(2,1)S(1)}, u32[]{:S(2)}, u32[]{:S(2)}) collective-permute-start(bf16[384,256]{1,0:T(8,128)(2,1)S(1)} %pad_maximum_fusion.5), channel_id=1, source_target_pairs={{0,6},{1,7},{2,4},{3,5},{4,2},{5,3},{6,0},{7,1},{8,14},{9,15},{10,... | collective-permute-start | bytes 589832 | tf_op jit(solution)/shard_map/ppermute | solution.py:72
  45.8 0.2 fusion.10
  46.0 0.0 copy-start.10
  46.0 0.0 copy-start.11
  46.0 0.0 copy-start.12
  46.0 2.0 %collective-permute-start.15 = (bf16[384,256]{1,0:T(8,128)(2,1)S(1)}, bf16[384,256]{1,0:T(8,128)(2,1)S(1)}, u32[]{:S(2)}, u32[]{:S(2)}) collective-permute-start(bf16[384,256]{1,0:T(8,128)(2,1)S(1)} %pad_maximum_fusion.7), channel_id=1, source_target_pairs={{0,2},{1,3},{2,0},{3,1},{4,6},{5,7},{6,4},{7,5},{8,10},{9,11},{10,... | collective-permute-start | bytes 589832 | tf_op jit(solution)/shard_map/ppermute | solution.py:72
  48.1 0.1 collective-permute-start.17
  48.2 0.6 collective-permute-start.18
  48.8 1.6 %collective-permute-start.14 = (bf16[384,256]{1,0:T(8,128)(2,1)S(1)}, bf16[384,256]{1,0:T(8,128)(2,1)S(1)}, u32[]{:S(2)}, u32[]{:S(2)}) collective-permute-start(bf16[384,256]{1,0:T(8,128)(2,1)S(1)} %pad_maximum_fusion.6), channel_id=1, source_target_pairs={{0,4},{1,5},{2,6},{3,7},{4,0},{5,1},{6,2},{7,3},{8,12},{9,13},{10,... | collective-permute-start | bytes 589832 | tf_op jit(solution)/shard_map/ppermute | solution.py:72
  50.4 2.5 %collective-permute-done.13 = bf16[384,256]{1,0:T(8,128)(2,1)S(1)} collective-permute-done((bf16[384,256]{1,0:T(8,128)(2,1)S(1)}, bf16[384,256]{1,0:T(8,128)(2,1)S(1)}, u32[]{:S(2)}, u32[]{:S(2)}) %collective-permute-start.13) | collective-permute-done | bytes 196640 | tf_op jit(solution)/shard_map/ppermute | solution.py:72
  52.9 1.5 %collective-permute-start.16 = (bf16[384,256]{1,0:T(8,128)(2,1)S(1)}, bf16[384,256]{1,0:T(8,128)(2,1)S(1)}, u32[]{:S(2)}, u32[]{:S(2)}) collective-permute-start(bf16[384,256]{1,0:T(8,128)(2,1)S(1)} %pad_maximum_fusion.8), channel_id=1, source_target_pairs={{0,6},{1,7},{2,4},{3,5},{4,2},{5,3},{6,0},{7,1},{8,14},{9,15},{10,... | collective-permute-start | bytes 589832 | tf_op jit(solution)/shard_map/ppermute | solution.py:72
  54.5 1.9 %collective-permute-done.15 = bf16[384,256]{1,0:T(8,128)(2,1)S(1)} collective-permute-done((bf16[384,256]{1,0:T(8,128)(2,1)S(1)}, bf16[384,256]{1,0:T(8,128)(2,1)S(1)}, u32[]{:S(2)}, u32[]{:S(2)}) %collective-permute-start.15) | collective-permute-done | bytes 196640 | tf_op jit(solution)/shard_map/ppermute | solution.py:72
  56.4 0.0 collective-permute-done.17
  56.4 4.9 %collective-permute-done.18 = bf16[384,256]{1,0:T(8,128)(2,1)S(1)} collective-permute-done((bf16[384,256]{1,0:T(8,128)(2,1)S(1)}, bf16[384,256]{1,0:T(8,128)(2,1)S(1)}, u32[]{:S(2)}, u32[]{:S(2)}) %collective-permute-start.18) | collective-permute-done | bytes 196640 | tf_op jit(solution)/shard_map/ppermute | solution.py:72
  61.3 0.0 collective-permute-done.14
  61.3 3.5 %collective-permute-done.16 = bf16[384,256]{1,0:T(8,128)(2,1)S(1)} collective-permute-done((bf16[384,256]{1,0:T(8,128)(2,1)S(1)}, bf16[384,256]{1,0:T(8,128)(2,1)S(1)}, u32[]{:S(2)}, u32[]{:S(2)}) %collective-permute-start.16) | collective-permute-done | bytes 196640 | tf_op jit(solution)/shard_map/ppermute | solution.py:72
  64.7 0.2 fusion.12
  64.9 3.0 %collective-permute-start.19 = (bf16[192,256]{1,0:T(8,128)(2,1)S(1)}, bf16[192,256]{1,0:T(8,128)(2,1)S(1)}, u32[]{:S(2)}, u32[]{:S(2)}) collective-permute-start(bf16[192,256]{1,0:T(8,128)(2,1)S(1)} %get-tuple-element.18), channel_id=1, source_target_pairs={{0,24},{1,25},{2,26},{3,27},{4,28},{5,29},{6,30},{7,31},{8,16},{9,... | collective-permute-start | bytes 294920 | tf_op jit(solution)/shard_map/ppermute | solution.py:72
  67.9 0.0 collective-permute-start.20
  67.9 1.5 %collective-permute-start.21 = (bf16[192,256]{1,0:T(8,128)(2,1)S(1)}, bf16[192,256]{1,0:T(8,128)(2,1)S(1)}, u32[]{:S(2)}, u32[]{:S(2)}) collective-permute-start(bf16[192,256]{1,0:T(8,128)(2,1)S(1)} %get-tuple-element.20), channel_id=1, source_target_pairs={{0,8},{1,9},{2,10},{3,11},{4,12},{5,13},{6,14},{7,15},{8,0},{9,1},... | collective-permute-start | bytes 294920 | tf_op jit(solution)/shard_map/ppermute | solution.py:72
  69.4 2.8 %collective-permute-done.19 = bf16[192,256]{1,0:T(8,128)(2,1)S(1)} collective-permute-done((bf16[192,256]{1,0:T(8,128)(2,1)S(1)}, bf16[192,256]{1,0:T(8,128)(2,1)S(1)}, u32[]{:S(2)}, u32[]{:S(2)}) %collective-permute-start.19) | collective-permute-done | bytes 98336 | tf_op jit(solution)/shard_map/ppermute | solution.py:72
  72.2 3.1 %collective-permute-done.20 = bf16[192,256]{1,0:T(8,128)(2,1)S(1)} collective-permute-done((bf16[192,256]{1,0:T(8,128)(2,1)S(1)}, bf16[192,256]{1,0:T(8,128)(2,1)S(1)}, u32[]{:S(2)}, u32[]{:S(2)}) %collective-permute-start.20) | collective-permute-done | bytes 98336 | tf_op jit(solution)/shard_map/ppermute | solution.py:72
  75.3 0.0 collective-permute-done.21
  75.3 1.0 %fusion.23 = (bf16[192,256]{1,0:T(8,128)(2,1)S(1)}, f32[192,256]{1,0:T(8,128)}, f32[192,256]{1,0:T(8,128)}, f32[192,256]{1,0:T(8,128)}) fusion(f32[192,256]{1,0:T(8,128)S(1)} %copy-done.10, f32[192,256]{1,0:T(8,128)S(1)} %copy-done.11, f32[192,256]{1,0:T(8,128)S(1)} %copy-done.12, bf16[192,256]{1,0:T(8,128)(2,1)S(1)} %collective-permute-done.21, ...), kind=kLoop, calls=%fused_computation.57 | loop fusion | flops 1474560 | bytes 2162688 | tf_op jit(solution)/shard_map/convert_element_type | solution.py:281
  76.3 6.2 %all_gather.3 = bf16[768,256]{1,0:T(8,128)(2,1)S(1)} all-gather(bf16[192,256]{1,0:T(8,128)(2,1)S(1)} %get-tuple-element.14), channel_id=1, replica_groups=mesh['grp'=8,'rep'=4] {'rep'}, dimensions={0}, use_global_device_ids=true | all-gather | bytes 491520 | tf_op jit(solution)/shard_map/all_gather | solution.py:281
  82.5 0.7 copy.14
  (30 shorter events, 0.2 us)
Async XLA Ops:
  0.6 31.1 %copy-start.9 = (s32[1,192]{1,0:T(1,128)S(1)}, s32[1,192]{1,0:T(1,128)}, u32[]{:S(2)}) copy-start(s32[1,192]{1,0:T(1,128)} %refs_14_.1) | copy-start | bytes 2308
  0.6 31.9 %copy-start = (bf16[1,192,6144]{2,1,0:T(8,128)(2,1)S(1)}, bf16[1,192,6144]{2,1,0:T(8,128)(2,1)}, u32[]{:S(2)}) copy-start(bf16[1,192,6144]{2,1,0:T(8,128)(2,1)} %param.7) | copy-start | bytes 7077892
  1.8 5.9 %collective-permute-start = (bf16[192,256]{1,0:T(8,128)(2,1)S(1)}, bf16[192,256]{1,0:T(8,128)(2,1)S(1)}, u32[]{:S(2)}, u32[]{:S(2)}) collective-permute-start(bf16[192,256]{1,0:T(8,128)(2,1)S(1)} %get-tuple-element.34), channel_id=1, source_target_pairs={{0,8},{1,9},{2,10},{3,11},{4,12},{5,13},{6,14},{7,15},{8,0},{9,1},... | collective-permute-start | bytes 294920 | tf_op jit(solution)/shard_map/ppermute | solution.py:72
  4.9 7.3 %collective-permute-start.1 = (bf16[192,256]{1,0:T(8,128)(2,1)S(1)}, bf16[192,256]{1,0:T(8,128)(2,1)S(1)}, u32[]{:S(2)}, u32[]{:S(2)}) collective-permute-start(bf16[192,256]{1,0:T(8,128)(2,1)S(1)} %get-tuple-element.34), channel_id=1, source_target_pairs={{0,16},{1,17},{2,18},{3,19},{4,20},{5,21},{6,22},{7,23},{8,24},{9,... | collective-permute-start | bytes 294920 | tf_op jit(solution)/shard_map/ppermute | solution.py:72
  12.2 6.2 %collective-permute-start.4 = (bf16[384,256]{1,0:T(8,128)(2,1)S(1)}, bf16[384,256]{1,0:T(8,128)(2,1)S(1)}, u32[]{:S(2)}, u32[]{:S(2)}) collective-permute-start(bf16[384,256]{1,0:T(8,128)(2,1)S(1)} %constant_dynamic-update-slice_fusion.refs_1_), channel_id=1, source_target_pairs={{0,4},{1,5},{2,6},{3,7},{4,0},{5,1},{6,2},{7,3},{8,12},{9,13},{10,... | collective-permute-start | bytes 589832 | tf_op jit(solution)/shard_map/ppermute | solution.py:72
  13.7 4.6 %collective-permute-start.3 = (bf16[192,256]{1,0:T(8,128)(2,1)S(1)}, bf16[192,256]{1,0:T(8,128)(2,1)S(1)}, u32[]{:S(2)}, u32[]{:S(2)}) collective-permute-start(bf16[192,256]{1,0:T(8,128)(2,1)S(1)} %collective-permute-done.1), channel_id=1, source_target_pairs={{0,8},{1,9},{2,10},{3,11},{4,12},{5,13},{6,14},{7,15},{8,0},{9,1},... | collective-permute-start | bytes 294920 | tf_op jit(solution)/shard_map/ppermute | solution.py:72
  14.1 11.0 %collective-permute-start.5 = (bf16[384,256]{1,0:T(8,128)(2,1)S(1)}, bf16[384,256]{1,0:T(8,128)(2,1)S(1)}, u32[]{:S(2)}, u32[]{:S(2)}) collective-permute-start(bf16[384,256]{1,0:T(8,128)(2,1)S(1)} %constant_dynamic-update-slice_fusion.refs_1_), channel_id=1, source_target_pairs={{0,2},{1,3},{2,0},{3,1},{4,6},{5,7},{6,4},{7,5},{8,10},{9,11},{10,... | collective-permute-start | bytes 589832 | tf_op jit(solution)/shard_map/ppermute | solution.py:72
  18.4 11.3 %collective-permute-start.7 = (bf16[576,256]{1,0:T(8,128)(2,1)S(1)}, bf16[576,256]{1,0:T(8,128)(2,1)S(1)}, u32[]{:S(2)}, u32[]{:S(2)}) collective-permute-start(bf16[576,256]{1,0:T(8,128)(2,1)S(1)} %pad_maximum_fusion.3), channel_id=1, source_target_pairs={{0,2},{1,3},{2,0},{3,1},{4,6},{5,7},{6,4},{7,5},{8,10},{9,11},{10,... | collective-permute-start | bytes 884744 | tf_op jit(solution)/shard_map/ppermute | solution.py:72
  20.3 4.7 %collective-permute-start.6 = (bf16[192,256]{1,0:T(8,128)(2,1)S(1)}, bf16[192,256]{1,0:T(8,128)(2,1)S(1)}, u32[]{:S(2)}, u32[]{:S(2)}) collective-permute-start(bf16[192,256]{1,0:T(8,128)(2,1)S(1)} %collective-permute-done.3.refs_3_), channel_id=1, source_target_pairs={{0,4},{1,5},{2,6},{3,7},{4,0},{5,1},{6,2},{7,3},{8,12},{9,13},{10,... | collective-permute-start | bytes 294920 | tf_op jit(solution)/shard_map/ppermute | solution.py:72
  22.4 8.0 %collective-permute-start.2 = (bf16[384,256]{1,0:T(8,128)(2,1)S(1)}, bf16[384,256]{1,0:T(8,128)(2,1)S(1)}, u32[]{:S(2)}, u32[]{:S(2)}) collective-permute-start(bf16[384,256]{1,0:T(8,128)(2,1)S(1)} %pad_maximum_fusion.4), channel_id=1, source_target_pairs={{0,4},{1,5},{2,6},{3,7},{4,0},{5,1},{6,2},{7,3},{8,12},{9,13},{10,... | collective-permute-start | bytes 589832 | tf_op jit(solution)/shard_map/ppermute | solution.py:72
  25.0 5.5 %copy-start.5 = (bf16[192,256]{1,0:T(8,128)(2,1)}, bf16[192,256]{1,0:T(8,128)(2,1)S(1)}, u32[]{:S(2)}) copy-start(bf16[192,256]{1,0:T(8,128)(2,1)S(1)} %collective-permute-done.6.refs_6_) | copy-start | bytes 294916
  25.0 4.6 %collective-permute-start.8 = (bf16[192,256]{1,0:T(8,128)(2,1)S(1)}, bf16[192,256]{1,0:T(8,128)(2,1)S(1)}, u32[]{:S(2)}, u32[]{:S(2)}) collective-permute-start(bf16[192,256]{1,0:T(8,128)(2,1)S(1)} %collective-permute-done.6.refs_6_), channel_id=1, source_target_pairs={{0,2},{1,3},{2,0},{3,1},{4,6},{5,7},{6,4},{7,5},{8,10},{9,11},{10,... | collective-permute-start | bytes 294920 | tf_op jit(solution)/shard_map/ppermute | solution.py:72
  25.9 10.0 %collective-permute-start.10 = (bf16[960,256]{1,0:T(8,128)(2,1)}, bf16[960,256]{1,0:T(8,128)(2,1)}, u32[]{:S(2)}, u32[]{:S(2)}) collective-permute-start(bf16[960,256]{1,0:T(8,128)(2,1)} %pad_maximum_fusion), channel_id=1, source_target_pairs={{0,1},{1,0},{2,3},{3,2},{4,5},{5,4},{6,7},{7,6},{8,9},{9,8},{10,11... | collective-permute-start | bytes 1474568 | tf_op jit(solution)/shard_map/ppermute | solution.py:72
  29.6 1.6 %copy-start.7 = (bf16[192,256]{1,0:T(8,128)(2,1)}, bf16[192,256]{1,0:T(8,128)(2,1)S(1)}, u32[]{:S(2)}) copy-start(bf16[192,256]{1,0:T(8,128)(2,1)S(1)} %collective-permute-done.8.refs_8_) | copy-start | bytes 294916
  30.5 5.5 %collective-permute-start.11 = (bf16[960,256]{1,0:T(8,128)(2,1)}, bf16[960,256]{1,0:T(8,128)(2,1)}, u32[]{:S(2)}, u32[]{:S(2)}) collective-permute-start(bf16[960,256]{1,0:T(8,128)(2,1)} %pad_maximum_fusion.1), channel_id=1, source_target_pairs={{0,1},{1,0},{2,3},{3,2},{4,5},{5,4},{6,7},{7,6},{8,9},{9,8},{10,11... | collective-permute-start | bytes 1474568 | tf_op jit(solution)/shard_map/ppermute | solution.py:72
  31.2 4.7 %collective-permute-start.9 = (bf16[768,256]{1,0:T(8,128)(2,1)}, bf16[768,256]{1,0:T(8,128)(2,1)}, u32[]{:S(2)}, u32[]{:S(2)}) collective-permute-start(bf16[768,256]{1,0:T(8,128)(2,1)} %pad_maximum_fusion.2), channel_id=1, source_target_pairs={{0,1},{1,0},{2,3},{3,2},{4,5},{5,4},{6,7},{7,6},{8,9},{9,8},{10,11... | collective-permute-start | bytes 1179656 | tf_op jit(solution)/shard_map/ppermute | solution.py:72
  32.5 1.7 %copy-start.1 = (bf16[1,192,6144]{2,1,0:T(8,128)(2,1)S(1)}, bf16[1,192,6144]{2,1,0:T(8,128)(2,1)}, u32[]{:S(2)}) copy-start(bf16[1,192,6144]{2,1,0:T(8,128)(2,1)} %param.8) | copy-start | bytes 7077892
  34.2 1.8 %copy-start.2 = (bf16[1,192,6144]{2,1,0:T(8,128)(2,1)S(1)}, bf16[1,192,6144]{2,1,0:T(8,128)(2,1)}, u32[]{:S(2)}) copy-start(bf16[1,192,6144]{2,1,0:T(8,128)(2,1)} %param.8) | copy-start | bytes 7077892
  34.2 1.8 %copy-start.3 = (bf16[768,256]{1,0:T(8,128)(2,1)S(1)}, bf16[768,256]{1,0:T(8,128)(2,1)}, u32[]{:S(2)}) copy-start(bf16[768,256]{1,0:T(8,128)(2,1)} %refs_0_.1) | copy-start | bytes 1179652
  34.2 1.8 %copy-start.4 = (s32[192,1]{1,0:T(8,128)S(1)}, s32[192,1]{1,0:T(8,128)}, u32[]{:S(2)}) copy-start(s32[192,1]{1,0:T(8,128)} %copy.11.refs_15_) | copy-start | bytes 2308
  34.2 1.8 %copy-start.6 = (bf16[192,256]{1,0:T(8,128)(2,1)S(1)}, bf16[192,256]{1,0:T(8,128)(2,1)}, u32[]{:S(2)}) copy-start(bf16[192,256]{1,0:T(8,128)(2,1)} %copy-done.5) | copy-start | bytes 294916
  34.2 1.8 %copy-start.8 = (bf16[192,256]{1,0:T(8,128)(2,1)S(1)}, bf16[192,256]{1,0:T(8,128)(2,1)}, u32[]{:S(2)}) copy-start(bf16[192,256]{1,0:T(8,128)(2,1)} %copy-done.7) | copy-start | bytes 294916
  40.6 3.5 %collective-permute-start.12 = (bf16[3072,256]{1,0:T(8,128)(2,1)S(1)}, bf16[3072,256]{1,0:T(8,128)(2,1)S(1)}, u32[]{:S(2)}, u32[]{:S(2)}) collective-permute-start(bf16[3072,256]{1,0:T(8,128)(2,1)S(1)} %get-tuple-element.13), channel_id=1, source_target_pairs={{0,1},{1,0},{2,3},{3,2},{4,5},{5,4},{6,7},{7,6},{8,9},{9,8},{10,11... | collective-permute-start | bytes 4718600 | tf_op jit(solution)/shard_map/ppermute | solution.py:72
  44.2 8.8 %collective-permute-start.13 = (bf16[384,256]{1,0:T(8,128)(2,1)S(1)}, bf16[384,256]{1,0:T(8,128)(2,1)S(1)}, u32[]{:S(2)}, u32[]{:S(2)}) collective-permute-start(bf16[384,256]{1,0:T(8,128)(2,1)S(1)} %pad_maximum_fusion.5), channel_id=1, source_target_pairs={{0,6},{1,7},{2,4},{3,5},{4,2},{5,3},{6,0},{7,1},{8,14},{9,15},{10,... | collective-permute-start | bytes 589832 | tf_op jit(solution)/shard_map/ppermute | solution.py:72
  46.0 29.3 %copy-start.10 = (f32[192,256]{1,0:T(8,128)S(1)}, f32[192,256]{1,0:T(8,128)}, u32[]{:S(2)}) copy-start(f32[192,256]{1,0:T(8,128)} %param.11) | copy-start | bytes 589828
  46.0 29.3 %copy-start.11 = (f32[192,256]{1,0:T(8,128)S(1)}, f32[192,256]{1,0:T(8,128)}, u32[]{:S(2)}) copy-start(f32[192,256]{1,0:T(8,128)} %param.12) | copy-start | bytes 589828
  46.0 29.3 %copy-start.12 = (f32[192,256]{1,0:T(8,128)S(1)}, f32[192,256]{1,0:T(8,128)}, u32[]{:S(2)}) copy-start(f32[192,256]{1,0:T(8,128)} %param.13) | copy-start | bytes 589828
  46.0 10.3 %collective-permute-start.15 = (bf16[384,256]{1,0:T(8,128)(2,1)S(1)}, bf16[384,256]{1,0:T(8,128)(2,1)S(1)}, u32[]{:S(2)}, u32[]{:S(2)}) collective-permute-start(bf16[384,256]{1,0:T(8,128)(2,1)S(1)} %pad_maximum_fusion.7), channel_id=1, source_target_pairs={{0,2},{1,3},{2,0},{3,1},{4,6},{5,7},{6,4},{7,5},{8,10},{9,11},{10,... | collective-permute-start | bytes 589832 | tf_op jit(solution)/shard_map/ppermute | solution.py:72
  48.1 8.3 %collective-permute-start.17 = (bf16[384,256]{1,0:T(8,128)(2,1)S(1)}, bf16[384,256]{1,0:T(8,128)(2,1)S(1)}, u32[]{:S(2)}, u32[]{:S(2)}) collective-permute-start(bf16[384,256]{1,0:T(8,128)(2,1)S(1)} %pad_maximum_fusion.9), channel_id=1, source_target_pairs={{0,4},{1,5},{2,6},{3,7},{4,0},{5,1},{6,2},{7,3},{8,12},{9,13},{10,... | collective-permute-start | bytes 589832 | tf_op jit(solution)/shard_map/ppermute | solution.py:72
  48.2 13.1 %collective-permute-start.18 = (bf16[384,256]{1,0:T(8,128)(2,1)S(1)}, bf16[384,256]{1,0:T(8,128)(2,1)S(1)}, u32[]{:S(2)}, u32[]{:S(2)}) collective-permute-start(bf16[384,256]{1,0:T(8,128)(2,1)S(1)} %pad_maximum_fusion.10), channel_id=1, source_target_pairs={{0,2},{1,3},{2,0},{3,1},{4,6},{5,7},{6,4},{7,5},{8,10},{9,11},{10,... | collective-permute-start | bytes 589832 | tf_op jit(solution)/shard_map/ppermute | solution.py:72
  48.8 12.4 %collective-permute-start.14 = (bf16[384,256]{1,0:T(8,128)(2,1)S(1)}, bf16[384,256]{1,0:T(8,128)(2,1)S(1)}, u32[]{:S(2)}, u32[]{:S(2)}) collective-permute-start(bf16[384,256]{1,0:T(8,128)(2,1)S(1)} %pad_maximum_fusion.6), channel_id=1, source_target_pairs={{0,4},{1,5},{2,6},{3,7},{4,0},{5,1},{6,2},{7,3},{8,12},{9,13},{10,... | collective-permute-start | bytes 589832 | tf_op jit(solution)/shard_map/ppermute | solution.py:72
  52.9 11.8 %collective-permute-start.16 = (bf16[384,256]{1,0:T(8,128)(2,1)S(1)}, bf16[384,256]{1,0:T(8,128)(2,1)S(1)}, u32[]{:S(2)}, u32[]{:S(2)}) collective-permute-start(bf16[384,256]{1,0:T(8,128)(2,1)S(1)} %pad_maximum_fusion.8), channel_id=1, source_target_pairs={{0,6},{1,7},{2,4},{3,5},{4,2},{5,3},{6,0},{7,1},{8,14},{9,15},{10,... | collective-permute-start | bytes 589832 | tf_op jit(solution)/shard_map/ppermute | solution.py:72
  64.9 7.2 %collective-permute-start.19 = (bf16[192,256]{1,0:T(8,128)(2,1)S(1)}, bf16[192,256]{1,0:T(8,128)(2,1)S(1)}, u32[]{:S(2)}, u32[]{:S(2)}) collective-permute-start(bf16[192,256]{1,0:T(8,128)(2,1)S(1)} %get-tuple-element.18), channel_id=1, source_target_pairs={{0,24},{1,25},{2,26},{3,27},{4,28},{5,29},{6,30},{7,31},{8,16},{9,... | collective-permute-start | bytes 294920 | tf_op jit(solution)/shard_map/ppermute | solution.py:72
  67.9 7.4 %collective-permute-start.20 = (bf16[192,256]{1,0:T(8,128)(2,1)S(1)}, bf16[192,256]{1,0:T(8,128)(2,1)S(1)}, u32[]{:S(2)}, u32[]{:S(2)}) collective-permute-start(bf16[192,256]{1,0:T(8,128)(2,1)S(1)} %get-tuple-element.19), channel_id=1, source_target_pairs={{0,16},{1,17},{2,18},{3,19},{4,20},{5,21},{6,22},{7,23},{8,24},{9,... | collective-permute-start | bytes 294920 | tf_op jit(solution)/shard_map/ppermute | solution.py:72
  67.9 7.4 %collective-permute-start.21 = (bf16[192,256]{1,0:T(8,128)(2,1)S(1)}, bf16[192,256]{1,0:T(8,128)(2,1)S(1)}, u32[]{:S(2)}, u32[]{:S(2)}) collective-permute-start(bf16[192,256]{1,0:T(8,128)(2,1)S(1)} %get-tuple-element.20), channel_id=1, source_target_pairs={{0,8},{1,9},{2,10},{3,11},{4,12},{5,13},{6,14},{7,15},{8,0},{9,1},... | collective-permute-start | bytes 294920 | tf_op jit(solution)/shard_map/ppermute | solution.py:72

commit v2 on v1

--- a/solution.py
+++ b/solution.py
@@ -17,6 +17,8 @@
 
 AXES = ("grp", "rep")
 MIB = 1024 * 1024
+FAR = (2, 3)
+NEAR = (1, 0)
 
 
 def adam(gradient, primary, first_moment, second_moment):
@@ -100,9 +102,8 @@
 def attend_kernel(places, rows, head, grad_scale, *refs):
     count = len(places)
     pieces = refs[:count]
-    acts, cots, doc_row, doc_col, acts_t, cots_t = refs[count : count + 6]
-    other_ref, left_ref, right_ref = refs[count + 6 : count + 9]
-    weights = refs[count + 9]
+    acts, cots, docs, acts_t, cots_t = refs[count : count + 5]
+    far_ref, near_ref, left_ref, right_ref, weights = refs[count + 5 :]
     for piece, place in zip(pieces, places):
         for index, where in enumerate(place):
             if where is None:
@@ -123,7 +124,8 @@
     tokens = scores.shape[0]
     here = lax.broadcasted_iota(jnp.int32, (tokens, tokens), 0)
     there = lax.broadcasted_iota(jnp.int32, (tokens, tokens), 1)
-    allowed = (there <= here) & (doc_row[...] == doc_col[...])
+    document = jnp.broadcast_to(docs[...], (tokens, tokens))
+    allowed = (there <= here) & (document == document.T)
     exp_scores = jnp.where(allowed, jnp.exp(jnp.where(allowed, scores, 0.0)), 0.0)
     attention = exp_scores / jnp.sum(exp_scores, axis=1, keepdims=True)
     attention_low = attention.astype(jnp.bfloat16)
@@ -139,26 +141,27 @@
     right = jnp.concatenate([none, none, none, context], axis=1)
     left_ref[...] = left
     right_ref[...] = right
-    write_terms(acts_t, cots_t, left, right, other_ref, 1, rows, grad_scale)
-
-
-def write_terms(acts_t, cots_t, left, right, out_ref, kc, rows, grad_scale):
-    for index in range(16):
-        start = block_start(index // 4, index // 2 % 2, index % 2, kc, rows)
+    write_terms(acts_t, cots_t, left, right, far_ref, FAR, 1, rows, grad_scale)
+    write_terms(acts_t, cots_t, left, right, near_ref, NEAR, 1, rows, grad_scale)
+
+
+def write_terms(acts_t, cots_t, left, right, out_ref, kzs, kc, rows, grad_scale):
+    for index, (kz, kx, ky) in enumerate((kz, kx, ky) for kz in kzs for kx in (0, 1) for ky in (0, 1)):
+        start = block_start(kz, kx, ky, kc, rows)
         term = fdot(acts_t[pl.ds(start, rows), :], left, MM)
         term += fdot(cots_t[pl.ds(start, rows), :], right, MM)
         out_ref[index * rows : (index + 1) * rows, :] = (term * grad_scale).astype(out_ref.dtype)
 
 
-def mine_kernel(rows, grad_scale, acts_t, cots_t, left_ref, right_ref, out_ref):
-    write_terms(acts_t, cots_t, left_ref[...], right_ref[...], out_ref, 0, rows, grad_scale)
+def mine_kernel(kzs, rows, grad_scale, acts_t, cots_t, left_ref, right_ref, out_ref):
+    write_terms(acts_t, cots_t, left_ref[...], right_ref[...], out_ref, kzs, 0, rows, grad_scale)
 
 
 def vmem(count):
     return [pl.BlockSpec(memory_space=pltpu.VMEM)] * count
 
 
-def kernel_call(body, outs, name, args, scratch=(), flops=0, limit=24):
+def kernel_call(body, outs, name, args, scratch=(), flops=0, limit=16):
     return pl.pallas_call(
         body,
         out_shape=outs,
@@ -171,71 +174,65 @@
     )(*args)
 
 
-def gather(weight_copy, rows):
+def gather(weight_copy, rows, beside):
     rep = lax.axis_index("rep")
     own = lax.dynamic_slice_in_dim(weight_copy, rep * rows, rows, 0)
     half = lax.dynamic_slice_in_dim(weight_copy, jnp.bitwise_xor(rep, 2) * rows, rows, 0)
+    both = join(own, half)
     z2 = hop(own, 2, 0, 0, 0)
-    z1 = hop(own, 1, 0, 0, 0)
-    x0 = hop(join(own, half), 0, 1, 0, 0)
-    z12 = join(z1, z2)
+    z1 = hop(both, 1, 0, 0, 0)
+    x0 = hop(both, 0, 1, 0, 0)
+    zx = hop(both, 1, 1, 0, 0)
+    z2, *beside = lax.optimization_barrier((z2, *beside))
     z3 = hop(z2, 1, 0, 0, 0)
-    x12 = hop(z12, 0, 1, 0, 0)
-    y12 = hop(z12, 0, 0, 1, 0)
-    c0 = hop(join(z12, x0), 0, 0, 0, 1)
+    x2 = hop(z2, 0, 1, 0, 0)
+    y2 = hop(z2, 0, 0, 1, 0)
     x3 = hop(z3, 0, 1, 0, 0)
-    ya = hop(join(z3, x12), 0, 0, 1, 0)
-    c1 = hop(join(z3, x12, y12), 0, 0, 0, 1)
+    ya = hop(join(z3, x2), 0, 0, 1, 0)
     yb = hop(x3, 0, 0, 1, 0)
+    c0 = hop(join(z1, x0, zx), 0, 0, 0, 1)
+    c1 = hop(join(z2, z3, x2, y2), 0, 0, 0, 1)
     c2 = hop(join(x3, ya, yb), 0, 0, 0, 1)
-    z12_at = [(1, 0, 0), (2, 0, 0)]
+    z1_at = [(1, 0, 0), (1, 0, 1)]
     x0_at = [(0, 1, 0), (0, 1, 1)]
-    x12_at = [(1, 1, 0), (2, 1, 0)]
-    y12_at = [(1, 0, 1), (2, 0, 1)]
-    z3_at, x3_at, yb_at = [(3, 0, 0)], [(3, 1, 0)], [(3, 1, 1)]
-    ya_at = [(3, 0, 1), (1, 1, 1), (2, 1, 1)]
+    zx_at = [(1, 1, 0), (1, 1, 1)]
+    z2_at, z3_at, x2_at, y2_at = [(2, 0, 0)], [(3, 0, 0)], [(2, 1, 0)], [(2, 0, 1)]
+    x3_at, yb_at = [(3, 1, 0)], [(3, 1, 1)]
+    ya_at = [(3, 0, 1), (2, 1, 1)]
 
     def core(kc, *lists):
         return [(*at, kc) for one in lists for at in one]
 
-    return [
+    pieces = [
         (weight_copy, [None]),
-        (z12, core(0, z12_at)),
+        (z1, core(0, z1_at)),
         (x0, core(0, x0_at)),
+        (zx, core(0, zx_at)),
+        (z2, core(0, z2_at)),
         (z3, core(0, z3_at)),
-        (x12, core(0, x12_at)),
-        (y12, core(0, y12_at)),
+        (x2, core(0, x2_at)),
+        (y2, core(0, y2_at)),
         (x3, core(0, x3_at)),
         (ya, core(0, ya_at)),
         (yb, core(0, yb_at)),
-        (c0, core(1, z12_at, x0_at)),
-        (c1, core(1, z3_at, x12_at, y12_at)),
+        (c0, core(1, z1_at, x0_at, zx_at)),
+        (c1, core(1, z2_at, z3_at, x2_at, y2_at)),
         (c2, core(1, x3_at, ya_at, yb_at)),
     ]
-
-
-def scatter(mine, other, rows):
-    received = hop(other, 0, 0, 0, 1)
-
+    return pieces, beside
+
+
+def plane_sum(mine, received, kzs, rows):
     def block(kz, kx, ky):
-        start = ((kz * 2 + kx) * 2 + ky) * rows
-        both = mine[start : start + rows] + received[start : start + rows].astype(jnp.float32)
-        return both
-
-    def send(at, kz, kx, ky):
-        return hop(join(*[block(*one).astype(jnp.bfloat16) for one in at]), kz, kx, ky, 0)
-
-    got = {}
-    for pair in ((3, 2), (1, 0)):
-        for kx, ky in ((1, 1), (1, 0), (0, 1)):
-            came = send([(kz, kx, ky) for kz in pair], 0, kx, ky)
-            for index, kz in enumerate(pair):
-                got.setdefault(kz, []).append(came[index * rows : (index + 1) * rows])
-    totals = {kz: block(kz, 0, 0) + sum(one.astype(jnp.float32) for one in got[kz]) for kz in got}
-    gradient = totals[0]
-    for kz in (3, 2, 1):
-        gradient += hop(totals[kz].astype(jnp.bfloat16), kz, 0, 0, 0).astype(jnp.float32)
-    return gradient
+        start = ((kzs.index(kz) * 2 + kx) * 2 + ky) * rows
+        return mine[start : start + rows] + received[start : start + rows].astype(jnp.float32)
+
+    totals = [block(kz, 0, 0) for kz in kzs]
+    for kx, ky in ((1, 1), (1, 0), (0, 1)):
+        came = hop(join(*[block(kz, kx, ky).astype(jnp.bfloat16) for kz in kzs]), 0, kx, ky, 0)
+        for index in range(len(kzs)):
+            totals[index] += came[index * rows : (index + 1) * rows].astype(jnp.float32)
+    return totals
 
 
 def block_body(activations, cotangent, documents, weight_copy, primary, first_moment, second_moment):
@@ -249,34 +246,32 @@
     acts_t, cots_t = kernel_call(
         functools.partial(turn_kernel, step=512), [turned, turned], "turn", (acts, cots)
     )
-    pieces = gather(weight_copy, rows)
+    pieces, (acts_t, cots_t) = gather(weight_copy, rows, (acts_t, cots_t))
     places = [place for _, place in pieces]
     side = jax.ShapeDtypeStruct((tokens, columns), jnp.bfloat16)
-    other, left, right = kernel_call(
+    other = jax.ShapeDtypeStruct((8 * rows, columns), jnp.bfloat16)
+    far, near, left, right = kernel_call(
         functools.partial(attend_kernel, places, rows, head, grad_scale),
-        [jax.ShapeDtypeStruct((16 * rows, columns), jnp.bfloat16), side, side],
+        [other, other, side, side],
         "attend",
-        (
-            *[piece for piece, _ in pieces],
-            acts,
-            cots,
-            documents,
-            documents.reshape(tokens, 1),
-            acts_t,
-            cots_t,
-        ),
+        (*[piece for piece, _ in pieces], acts, cots, documents, acts_t, cots_t),
         scratch=[pltpu.VMEM((depth, columns), jnp.bfloat16)],
         flops=4 * tokens * depth * columns,
-        limit=32,
-    )
-    (mine,) = kernel_call(
-        functools.partial(mine_kernel, rows, grad_scale),
-        [jax.ShapeDtypeStruct((16 * rows, columns), jnp.float32)],
-        "mine",
-        (acts_t, cots_t, left, right),
-        flops=2 * tokens * depth * columns,
-    )
-    gradient = scatter(mine, other, rows)
+    )
+    totals = {}
+    for kzs, sent in ((FAR, far), (NEAR, near)):
+        received = hop(sent, 0, 0, 0, 1)
+        (mine,) = kernel_call(
+            functools.partial(mine_kernel, kzs, rows, grad_scale),
+            [jax.ShapeDtypeStruct((8 * rows, columns), jnp.float32)],
+            "mine",
+            (acts_t, cots_t, left, right),
+            flops=tokens * depth * columns,
+        )
+        totals.update(zip(kzs, plane_sum(mine, received, kzs, rows)))
+    gradient = totals[0]
+    for kz in (2, 3, 1):
+        gradient += hop(totals[kz].astype(jnp.bfloat16), kz, 0, 0, 0).astype(jnp.float32)
     primary_new, first_new, second_new = adam(gradient, primary, first_moment, second_moment)
     copy_new = lax.all_gather(primary_new.astype(jnp.bfloat16), "rep", axis=0, tiled=True)
     return primary_new, first_new, second_new, copy_new

time: 83.5 us -> 73.5 us (0.88)
  waiting for transfers between devices: 34.8 us -> 25 us
  other arithmetic: 4 us -> 1.63 us
  starting transfers between devices: 25.8 us -> 28.1 us
  Pallas kernels: 7.26 us -> 6.13 us
    ppermute x22 -> x24, waiting for transfers between devices: 34.8 us -> 25 us  [hop(): return lax.ppermute(value, AXES, [(i, i ^ offset) for i in range(32)])]
    concatenate x11, other arithmetic: 2.54 us -> 0.2 us  [join(): return jnp.concatenate(parts, axis=0)]
    ppermute x22 -> x24, starting transfers between devices: 25.8 us -> 28.1 us  [hop(): return lax.ppermute(value, AXES, [(i, i ^ offset) for i in range(32)])]
    unnamed x28 -> x15, local copies, waits for them, and re-layouts: 2.47 us -> 4.11 us
    pallas_call x3 -> x4, Pallas kernels: 7.26 us -> 6.13 us  [kernel_call(): pl.pallas_call(body, out_shape=outs, in_specs=vmem(len(args)), out_specs=...]
  transfers between devices with their start and end apart: 22 -> 24, of which waited for: 12 -> 12; matrix products, arithmetic and copies ran while one was open for 4% -> 1% of each run, Pallas kernels for 3% -> 4%
where the time goes in v2:
time: 73.5 us; the launch traced here: 73.2 us
  starting transfers between devices  28.1 us (38%)
  waiting for transfers between devices  25 us (34%)
  blocking collectives  6.46 us (9%)
  Pallas kernels  6.13 us (8%)
  local copies, waits for them, and re-layouts  5.07 us (7%)
  other arithmetic  1.63 us (2%)
  between operations  0.85 us (1%)
    ppermute x24, starting transfers between devices, hop(): return lax.ppermute(value, AXES, [(i, i ^ offset) for i in range(32)])  28.1 us
    ppermute x24, waiting for transfers between devices, hop(): return lax.ppermute(value, AXES, [(i, i ^ offset) for i in range(32)])  25 us
    all_gather x1, blocking collectives, block_body(): lax.all_gather(primary_new.astype(jnp.bfloat16), 'rep', axis=0, tiled=True)  6.46 us
    pallas_call x4, Pallas kernels, kernel_call(): pl.pallas_call(body, out_shape=outs, in_specs=vmem(len(args)), out_specs=...  6.13 us
    unnamed x15, local copies, waits for them, and re-layouts  4.11 us
  transfers between devices with their start and end apart: 24, of which 12 were waited for; matrix products, arithmetic and copies ran while one was open for 1% of the time, Pallas kernels for 4%

profile of v2, /device:TPU:0, one launch (start us, length us, event | category | flops | bytes accessed | tf_op | source)
XLA Modules:
  0.0 73.2 jit_solution(7161590326709552980)
XLA Ops:
  0.6 1.0 %constant_dynamic-slice_fusion = (bf16[192,256]{1,0:T(8,128)(2,1)S(1)}, bf16[192,256]{1,0:T(8,128)(2,1)S(1)}) fusion(bf16[768,256]{1,0:T(8,128)(2,1)} %refs_0_.1, s32[]{:T(128)S(6)} %select_n.7, s32[]{:T(128)S(6)} %select_n.6), kind=kLoop, calls=%fused_computation.61 | loop fusion | bytes 393224 | tf_op jit(solution)/shard_map/dynamic_slice | solution.py:180
  1.6 4.1 %collective-permute-start = (bf16[192,256]{1,0:T(8,128)(2,1)S(1)}, bf16[192,256]{1,0:T(8,128)(2,1)S(1)}, u32[]{:S(2)}, u32[]{:S(2)}) collective-permute-start(bf16[192,256]{1,0:T(8,128)(2,1)S(1)} %get-tuple-element.41), channel_id=1, source_target_pairs={{0,16},{1,17},{2,18},{3,19},{4,20},{5,21},{6,22},{7,23},{8,24},{9,... | collective-permute-start | bytes 294920 | tf_op jit(solution)/shard_map/ppermute | solution.py:74
  5.7 1.7 %copy-done = bf16[1,192,6144]{2,1,0:T(8,128)(2,1)S(1)} copy-done((bf16[1,192,6144]{2,1,0:T(8,128)(2,1)S(1)}, bf16[1,192,6144]{2,1,0:T(8,128)(2,1)}, u32[]{:S(2)}) %copy-start) | copy-done | bytes 2359320
  7.4 1.7 %copy-done.1 = bf16[1,192,6144]{2,1,0:T(8,128)(2,1)S(1)} copy-done((bf16[1,192,6144]{2,1,0:T(8,128)(2,1)S(1)}, bf16[1,192,6144]{2,1,0:T(8,128)(2,1)}, u32[]{:S(2)}) %copy-start.1) | copy-done | bytes 2359320
  9.0 1.7 %turn.1 = (bf16[6144,192]{1,0:T(8,128)(2,1)S(1)}, bf16[6144,192]{1,0:T(8,128)(2,1)S(1)}) custom-call(bf16[192,6144]{1,0:T(8,128)(2,1)S(1)} %bitcast.2, bf16[192,6144]{1,0:T(8,128)(2,1)S(1)} %bitcast.4), custom_call_target="tpu_custom_call" | custom-call | bytes 4194304 | tf_op jit(solution)/shard_map/turn/pallas_call | solution.py:165
  10.8 1.6 %collective-permute-start.4 = (bf16[192,256]{1,0:T(8,128)(2,1)S(1)}, bf16[192,256]{1,0:T(8,128)(2,1)S(1)}, u32[]{:S(2)}, u32[]{:S(2)}) collective-permute-start(bf16[192,256]{1,0:T(8,128)(2,1)S(1)} %collective-permute-done.refs_4_), channel_id=1, source_target_pairs={{0,8},{1,9},{2,10},{3,11},{4,12},{5,13},{6,14},{7,15},{8,0},{9,1},... | collective-permute-start | bytes 294920 | tf_op jit(solution)/shard_map/ppermute | solution.py:74
  12.4 1.5 %collective-permute-start.5 = (bf16[192,256]{1,0:T(8,128)(2,1)S(1)}, bf16[192,256]{1,0:T(8,128)(2,1)S(1)}, u32[]{:S(2)}, u32[]{:S(2)}) collective-permute-start(bf16[192,256]{1,0:T(8,128)(2,1)S(1)} %collective-permute-done.refs_4_), channel_id=1, source_target_pairs={{0,4},{1,5},{2,6},{3,7},{4,0},{5,1},{6,2},{7,3},{8,12},{9,13},{10,... | collective-permute-start | bytes 294920 | tf_op jit(solution)/shard_map/ppermute | solution.py:74
  13.9 0.0 copy-start.2
  13.9 0.0 copy-start.3
  13.9 0.5 collective-permute-start.1
  14.4 0.5 collective-permute-start.2
  15.0 2.5 %collective-permute-start.3 = (bf16[384,256]{1,0:T(8,128)(2,1)S(1)}, bf16[384,256]{1,0:T(8,128)(2,1)S(1)}, u32[]{:S(2)}, u32[]{:S(2)}) collective-permute-start(bf16[384,256]{1,0:T(8,128)(2,1)S(1)} %pad_maximum_fusion.3), channel_id=1, source_target_pairs={{0,12},{1,13},{2,14},{3,15},{4,8},{5,9},{6,10},{7,11},{8,4},{9,5},... | collective-permute-start | bytes 589832 | tf_op jit(solution)/shard_map/ppermute | solution.py:74
  17.5 1.5 %collective-permute-start.6 = (bf16[192,256]{1,0:T(8,128)(2,1)S(1)}, bf16[192,256]{1,0:T(8,128)(2,1)S(1)}, u32[]{:S(2)}, u32[]{:S(2)}) collective-permute-start(bf16[192,256]{1,0:T(8,128)(2,1)S(1)} %collective-permute-done.refs_4_), channel_id=1, source_target_pairs={{0,2},{1,3},{2,0},{3,1},{4,6},{5,7},{6,4},{7,5},{8,10},{9,11},{10,... | collective-permute-start | bytes 294920 | tf_op jit(solution)/shard_map/ppermute | solution.py:74
  19.0 0.0 collective-permute-done.5.refs_6_
  19.0 0.6 collective-permute-start.8
  19.7 2.2 %collective-permute-done.1.refs_1_ = bf16[384,256]{1,0:T(8,128)(2,1)S(1)} collective-permute-done((bf16[384,256]{1,0:T(8,128)(2,1)S(1)}, bf16[384,256]{1,0:T(8,128)(2,1)S(1)}, u32[]{:S(2)}, u32[]{:S(2)}) %collective-permute-start.1) | collective-permute-done | bytes 196640 | tf_op jit(solution)/shard_map/ppermute | solution.py:74
  21.8 0.5 collective-permute-start.7
  22.4 3.7 %collective-permute-done.2.refs_2_ = bf16[384,256]{1,0:T(8,128)(2,1)S(1)} collective-permute-done((bf16[384,256]{1,0:T(8,128)(2,1)S(1)}, bf16[384,256]{1,0:T(8,128)(2,1)S(1)}, u32[]{:S(2)}, u32[]{:S(2)}) %collective-permute-start.2) | collective-permute-done | bytes 196640 | tf_op jit(solution)/shard_map/ppermute | solution.py:74
  26.1 0.0 collective-permute-done.3.refs_3_
  26.1 0.1 collective-permute-start.10
  26.2 1.1 %collective-permute-done.7.refs_8_ = bf16[192,256]{1,0:T(8,128)(2,1)S(1)} collective-permute-done((bf16[192,256]{1,0:T(8,128)(2,1)S(1)}, bf16[192,256]{1,0:T(8,128)(2,1)S(1)}, u32[]{:S(2)}, u32[]{:S(2)}) %collective-permute-start.7) | collective-permute-done | bytes 98336 | tf_op jit(solution)/shard_map/ppermute | solution.py:74
  27.3 1.5 %collective-permute-start.9 = (bf16[192,256]{1,0:T(8,128)(2,1)S(1)}, bf16[192,256]{1,0:T(8,128)(2,1)S(1)}, u32[]{:S(2)}, u32[]{:S(2)}) collective-permute-start(bf16[192,256]{1,0:T(8,128)(2,1)S(1)} %collective-permute-done.7.refs_8_), channel_id=1, source_target_pairs={{0,2},{1,3},{2,0},{3,1},{4,6},{5,7},{6,4},{7,5},{8,10},{9,11},{10,... | collective-permute-start | bytes 294920 | tf_op jit(solution)/shard_map/ppermute | solution.py:74
  28.9 0.0 collective-permute-done.6.refs_7_
  28.9 0.1 collective-permute-start.11
  29.0 0.0 collective-permute-done.8.refs_9_
  29.0 3.0 %collective-permute-done.9.refs_10_ = bf16[192,256]{1,0:T(8,128)(2,1)S(1)} collective-permute-done((bf16[192,256]{1,0:T(8,128)(2,1)S(1)}, bf16[192,256]{1,0:T(8,128)(2,1)S(1)}, u32[]{:S(2)}, u32[]{:S(2)}) %collective-permute-start.9) | collective-permute-done | bytes 98336 | tf_op jit(solution)/shard_map/ppermute | solution.py:74
  32.0 0.1 collective-permute-start.12
  32.1 0.0 collective-permute-done.11.refs_12_
  32.1 1.7 %collective-permute-done.12.refs_13_ = bf16[768,256]{1,0:T(8,128)(2,1)S(1)} collective-permute-done((bf16[768,256]{1,0:T(8,128)(2,1)S(1)}, bf16[768,256]{1,0:T(8,128)(2,1)S(1)}, u32[]{:S(2)}, u32[]{:S(2)}) %collective-permute-start.12) | collective-permute-done | bytes 393248 | tf_op jit(solution)/shard_map/ppermute | solution.py:74
  33.8 0.0 collective-permute-done.10.refs_11_
  33.8 3.3 %attend.1 = (bf16[1536,256]{1,0:T(8,128)(2,1)S(1)}, bf16[1536,256]{1,0:T(8,128)(2,1)S(1)}, bf16[192,256]{1,0:T(8,128)(2,1)S(1)}, bf16[192,256]{1,0:T(8,128)(2,1)S(1)}) custom-call(bf16[768,256]{1,0:T(8,128)(2,1)S(1)} %copy-done.2, bf16[384,256]{1,0:T(8,128)(2,1)S(1)} %collective-permute-done.1.refs_1_, bf16[384,256]{1,0:T(8,128)(2,1)S(1)} %collective-permute-done.2.refs_2_, ...), custom_call_target="tpu_custom_call" | custom-call | flops 1207959552 | bytes 4194304 | tf_op jit(solution)/shard_map/attend/pallas_call | solution.py:165
  37.1 0.2 collective-permute-start.17
  37.3 0.4 collective-permute-start.13
  37.7 0.6 mine.3
  38.2 0.6 mine.2
  38.8 0.6 collective-permute-done.17
  39.4 0.1 fusion.14
  39.6 2.1 %collective-permute-start.18 = (bf16[384,256]{1,0:T(8,128)(2,1)S(1)}, bf16[384,256]{1,0:T(8,128)(2,1)S(1)}, u32[]{:S(2)}, u32[]{:S(2)}) collective-permute-start(bf16[384,256]{1,0:T(8,128)(2,1)S(1)} %pad_maximum_fusion.8), channel_id=1, source_target_pairs={{0,6},{1,7},{2,4},{3,5},{4,2},{5,3},{6,0},{7,1},{8,14},{9,15},{10,... | collective-permute-start | bytes 589832 | tf_op jit(solution)/shard_map/ppermute | solution.py:74
  41.7 1.0 %collective-permute-start.19 = (bf16[384,256]{1,0:T(8,128)(2,1)S(1)}, bf16[384,256]{1,0:T(8,128)(2,1)S(1)}, u32[]{:S(2)}, u32[]{:S(2)}) collective-permute-start(bf16[384,256]{1,0:T(8,128)(2,1)S(1)} %pad_maximum_fusion.9), channel_id=1, source_target_pairs={{0,4},{1,5},{2,6},{3,7},{4,0},{5,1},{6,2},{7,3},{8,12},{9,13},{10,... | collective-permute-start | bytes 589832 | tf_op jit(solution)/shard_map/ppermute | solution.py:74
  42.7 0.6 collective-permute-start.20
  43.3 0.0 collective-permute-done.13
  43.3 0.1 fusion.24
  43.5 0.0 copy-start.4
  43.5 0.0 copy-start.5
  43.5 0.0 copy-start.6
  43.5 2.1 %collective-permute-start.14 = (bf16[384,256]{1,0:T(8,128)(2,1)S(1)}, bf16[384,256]{1,0:T(8,128)(2,1)S(1)}, u32[]{:S(2)}, u32[]{:S(2)}) collective-permute-start(bf16[384,256]{1,0:T(8,128)(2,1)S(1)} %pad_maximum_fusion.5), channel_id=1, source_target_pairs={{0,6},{1,7},{2,4},{3,5},{4,2},{5,3},{6,0},{7,1},{8,14},{9,15},{10,... | collective-permute-start | bytes 589832 | tf_op jit(solution)/shard_map/ppermute | solution.py:74
  45.6 1.0 %collective-permute-start.15 = (bf16[384,256]{1,0:T(8,128)(2,1)S(1)}, bf16[384,256]{1,0:T(8,128)(2,1)S(1)}, u32[]{:S(2)}, u32[]{:S(2)}) collective-permute-start(bf16[384,256]{1,0:T(8,128)(2,1)S(1)} %pad_maximum_fusion.6), channel_id=1, source_target_pairs={{0,4},{1,5},{2,6},{3,7},{4,0},{5,1},{6,2},{7,3},{8,12},{9,13},{10,... | collective-permute-start | bytes 589832 | tf_op jit(solution)/shard_map/ppermute | solution.py:74
  46.7 1.7 %collective-permute-done.18 = bf16[384,256]{1,0:T(8,128)(2,1)S(1)} collective-permute-done((bf16[384,256]{1,0:T(8,128)(2,1)S(1)}, bf16[384,256]{1,0:T(8,128)(2,1)S(1)}, u32[]{:S(2)}, u32[]{:S(2)}) %collective-permute-start.18) | collective-permute-done | bytes 196640 | tf_op jit(solution)/shard_map/ppermute | solution.py:74
  48.3 1.5 %collective-permute-start.16 = (bf16[384,256]{1,0:T(8,128)(2,1)S(1)}, bf16[384,256]{1,0:T(8,128)(2,1)S(1)}, u32[]{:S(2)}, u32[]{:S(2)}) collective-permute-start(bf16[384,256]{1,0:T(8,128)(2,1)S(1)} %pad_maximum_fusion.7), channel_id=1, source_target_pairs={{0,2},{1,3},{2,0},{3,1},{4,6},{5,7},{6,4},{7,5},{8,10},{9,11},{10,... | collective-permute-start | bytes 589832 | tf_op jit(solution)/shard_map/ppermute | solution.py:74
  49.9 2.7 %collective-permute-done.19 = bf16[384,256]{1,0:T(8,128)(2,1)S(1)} collective-permute-done((bf16[384,256]{1,0:T(8,128)(2,1)S(1)}, bf16[384,256]{1,0:T(8,128)(2,1)S(1)}, u32[]{:S(2)}, u32[]{:S(2)}) %collective-permute-start.19) | collective-permute-done | bytes 196640 | tf_op jit(solution)/shard_map/ppermute | solution.py:74
  52.6 0.0 collective-permute-done.20
  52.6 0.1 fusion.18
  52.7 2.6 %collective-permute-start.21 = (bf16[192,256]{1,0:T(8,128)(2,1)S(1)}, bf16[192,256]{1,0:T(8,128)(2,1)S(1)}, u32[]{:S(2)}, u32[]{:S(2)}) collective-permute-start(bf16[192,256]{1,0:T(8,128)(2,1)S(1)} %get-tuple-element.26), channel_id=1, source_target_pairs={{0,16},{1,17},{2,18},{3,19},{4,20},{5,21},{6,22},{7,23},{8,24},{9,... | collective-permute-start | bytes 294920 | tf_op jit(solution)/shard_map/ppermute | solution.py:74
  55.3 0.6 collective-permute-start.22
  56.0 0.8 %collective-permute-done.14 = bf16[384,256]{1,0:T(8,128)(2,1)S(1)} collective-permute-done((bf16[384,256]{1,0:T(8,128)(2,1)S(1)}, bf16[384,256]{1,0:T(8,128)(2,1)S(1)}, u32[]{:S(2)}, u32[]{:S(2)}) %collective-permute-start.14) | collective-permute-done | bytes 196640 | tf_op jit(solution)/shard_map/ppermute | solution.py:74
  56.8 3.5 %collective-permute-done.15 = bf16[384,256]{1,0:T(8,128)(2,1)S(1)} collective-permute-done((bf16[384,256]{1,0:T(8,128)(2,1)S(1)}, bf16[384,256]{1,0:T(8,128)(2,1)S(1)}, u32[]{:S(2)}, u32[]{:S(2)}) %collective-permute-start.15) | collective-permute-done | bytes 196640 | tf_op jit(solution)/shard_map/ppermute | solution.py:74
  60.3 0.0 collective-permute-done.16
  60.3 0.1 fusion.4
  60.4 0.7 %collective-permute-start.23 = (bf16[192,256]{1,0:T(8,128)(2,1)S(1)}, bf16[192,256]{1,0:T(8,128)(2,1)S(1)}, u32[]{:S(2)}, u32[]{:S(2)}) collective-permute-start(bf16[192,256]{1,0:T(8,128)(2,1)S(1)} %fusion.4), channel_id=1, source_target_pairs={{0,8},{1,9},{2,10},{3,11},{4,12},{5,13},{6,14},{7,15},{8,0},{9,1},... | collective-permute-start | bytes 294920 | tf_op jit(solution)/shard_map/ppermute | solution.py:74
  61.1 1.9 %collective-permute-done.21 = bf16[192,256]{1,0:T(8,128)(2,1)S(1)} collective-permute-done((bf16[192,256]{1,0:T(8,128)(2,1)S(1)}, bf16[192,256]{1,0:T(8,128)(2,1)S(1)}, u32[]{:S(2)}, u32[]{:S(2)}) %collective-permute-start.21) | collective-permute-done | bytes 98336 | tf_op jit(solution)/shard_map/ppermute | solution.py:74
  63.0 2.1 %collective-permute-done.23 = bf16[192,256]{1,0:T(8,128)(2,1)S(1)} collective-permute-done((bf16[192,256]{1,0:T(8,128)(2,1)S(1)}, bf16[192,256]{1,0:T(8,128)(2,1)S(1)}, u32[]{:S(2)}, u32[]{:S(2)}) %collective-permute-start.23) | collective-permute-done | bytes 98336 | tf_op jit(solution)/shard_map/ppermute | solution.py:74
  65.1 1.0 %fusion.31 = (bf16[192,256]{1,0:T(8,128)(2,1)S(1)}, f32[192,256]{1,0:T(8,128)}, f32[192,256]{1,0:T(8,128)}, f32[192,256]{1,0:T(8,128)}) fusion(f32[192,256]{1,0:T(8,128)S(1)} %copy-done.4, f32[192,256]{1,0:T(8,128)S(1)} %copy-done.5, f32[192,256]{1,0:T(8,128)S(1)} %copy-done.6, bf16[192,256]{1,0:T(8,128)(2,1)S(1)} %collective-permute-done.23, ...), kind=kLoop, calls=%fused_computation.63 | loop fusion | flops 1474560 | bytes 2162688 | tf_op jit(solution)/shard_map/convert_element_type | solution.py:276
  66.0 6.5 %all_gather.3 = bf16[768,256]{1,0:T(8,128)(2,1)S(1)} all-gather(bf16[192,256]{1,0:T(8,128)(2,1)S(1)} %get-tuple-element.22), channel_id=1, replica_groups=mesh['grp'=8,'rep'=4] {'rep'}, dimensions={0}, use_global_device_ids=true | all-gather | bytes 491520 | tf_op jit(solution)/shard_map/all_gather | solution.py:276
  72.5 0.7 %copy.12 = bf16[768,256]{1,0:T(8,128)(2,1)} copy(bf16[768,256]{1,0:T(8,128)(2,1)S(1)} %all_gather.3) | data formatting | bytes 786432
  (21 shorter events, 0.2 us)
Async XLA Ops:
  1.6 9.1 %collective-permute-start = (bf16[192,256]{1,0:T(8,128)(2,1)S(1)}, bf16[192,256]{1,0:T(8,128)(2,1)S(1)}, u32[]{:S(2)}, u32[]{:S(2)}) collective-permute-start(bf16[192,256]{1,0:T(8,128)(2,1)S(1)} %get-tuple-element.41), channel_id=1, source_target_pairs={{0,16},{1,17},{2,18},{3,19},{4,20},{5,21},{6,22},{7,23},{8,24},{9,... | collective-permute-start | bytes 294920 | tf_op jit(solution)/shard_map/ppermute | solution.py:74
  5.7 1.7 %copy-start = (bf16[1,192,6144]{2,1,0:T(8,128)(2,1)S(1)}, bf16[1,192,6144]{2,1,0:T(8,128)(2,1)}, u32[]{:S(2)}) copy-start(bf16[1,192,6144]{2,1,0:T(8,128)(2,1)} %param.7) | copy-start | bytes 7077892
  7.4 1.7 %copy-start.1 = (bf16[1,192,6144]{2,1,0:T(8,128)(2,1)S(1)}, bf16[1,192,6144]{2,1,0:T(8,128)(2,1)}, u32[]{:S(2)}) copy-start(bf16[1,192,6144]{2,1,0:T(8,128)(2,1)} %param.8) | copy-start | bytes 7077892
  10.8 6.7 %collective-permute-start.4 = (bf16[192,256]{1,0:T(8,128)(2,1)S(1)}, bf16[192,256]{1,0:T(8,128)(2,1)S(1)}, u32[]{:S(2)}, u32[]{:S(2)}) collective-permute-start(bf16[192,256]{1,0:T(8,128)(2,1)S(1)} %collective-permute-done.refs_4_), channel_id=1, source_target_pairs={{0,8},{1,9},{2,10},{3,11},{4,12},{5,13},{6,14},{7,15},{8,0},{9,1},... | collective-permute-start | bytes 294920 | tf_op jit(solution)/shard_map/ppermute | solution.py:74
  12.4 6.6 %collective-permute-start.5 = (bf16[192,256]{1,0:T(8,128)(2,1)S(1)}, bf16[192,256]{1,0:T(8,128)(2,1)S(1)}, u32[]{:S(2)}, u32[]{:S(2)}) collective-permute-start(bf16[192,256]{1,0:T(8,128)(2,1)S(1)} %collective-permute-done.refs_4_), channel_id=1, source_target_pairs={{0,4},{1,5},{2,6},{3,7},{4,0},{5,1},{6,2},{7,3},{8,12},{9,13},{10,... | collective-permute-start | bytes 294920 | tf_op jit(solution)/shard_map/ppermute | solution.py:74
  13.9 19.9 %copy-start.2 = (bf16[768,256]{1,0:T(8,128)(2,1)S(1)}, bf16[768,256]{1,0:T(8,128)(2,1)}, u32[]{:S(2)}) copy-start(bf16[768,256]{1,0:T(8,128)(2,1)} %refs_0_.1) | copy-start | bytes 1179652
  13.9 19.9 %copy-start.3 = (s32[1,192]{1,0:T(1,128)S(1)}, s32[1,192]{1,0:T(1,128)}, u32[]{:S(2)}) copy-start(s32[1,192]{1,0:T(1,128)} %refs_16_.1) | copy-start | bytes 2308
  13.9 7.9 %collective-permute-start.1 = (bf16[384,256]{1,0:T(8,128)(2,1)S(1)}, bf16[384,256]{1,0:T(8,128)(2,1)S(1)}, u32[]{:S(2)}, u32[]{:S(2)}) collective-permute-start(bf16[384,256]{1,0:T(8,128)(2,1)S(1)} %pad_maximum_fusion.3), channel_id=1, source_target_pairs={{0,8},{1,9},{2,10},{3,11},{4,12},{5,13},{6,14},{7,15},{8,0},{9,1},... | collective-permute-start | bytes 589832 | tf_op jit(solution)/shard_map/ppermute | solution.py:74
  14.4 11.6 %collective-permute-start.2 = (bf16[384,256]{1,0:T(8,128)(2,1)S(1)}, bf16[384,256]{1,0:T(8,128)(2,1)S(1)}, u32[]{:S(2)}, u32[]{:S(2)}) collective-permute-start(bf16[384,256]{1,0:T(8,128)(2,1)S(1)} %pad_maximum_fusion.3), channel_id=1, source_target_pairs={{0,4},{1,5},{2,6},{3,7},{4,0},{5,1},{6,2},{7,3},{8,12},{9,13},{10,... | collective-permute-start | bytes 589832 | tf_op jit(solution)/shard_map/ppermute | solution.py:74
  15.0 11.1 %collective-permute-start.3 = (bf16[384,256]{1,0:T(8,128)(2,1)S(1)}, bf16[384,256]{1,0:T(8,128)(2,1)S(1)}, u32[]{:S(2)}, u32[]{:S(2)}) collective-permute-start(bf16[384,256]{1,0:T(8,128)(2,1)S(1)} %pad_maximum_fusion.3), channel_id=1, source_target_pairs={{0,12},{1,13},{2,14},{3,15},{4,8},{5,9},{6,10},{7,11},{8,4},{9,5},... | collective-permute-start | bytes 589832 | tf_op jit(solution)/shard_map/ppermute | solution.py:74
  17.5 11.4 %collective-permute-start.6 = (bf16[192,256]{1,0:T(8,128)(2,1)S(1)}, bf16[192,256]{1,0:T(8,128)(2,1)S(1)}, u32[]{:S(2)}, u32[]{:S(2)}) collective-permute-start(bf16[192,256]{1,0:T(8,128)(2,1)S(1)} %collective-permute-done.refs_4_), channel_id=1, source_target_pairs={{0,2},{1,3},{2,0},{3,1},{4,6},{5,7},{6,4},{7,5},{8,10},{9,11},{10,... | collective-permute-start | bytes 294920 | tf_op jit(solution)/shard_map/ppermute | solution.py:74
  19.0 9.9 %collective-permute-start.8 = (bf16[384,256]{1,0:T(8,128)(2,1)S(1)}, bf16[384,256]{1,0:T(8,128)(2,1)S(1)}, u32[]{:S(2)}, u32[]{:S(2)}) collective-permute-start(bf16[384,256]{1,0:T(8,128)(2,1)S(1)} %pad_maximum_fusion.4), channel_id=1, source_target_pairs={{0,2},{1,3},{2,0},{3,1},{4,6},{5,7},{6,4},{7,5},{8,10},{9,11},{10,... | collective-permute-start | bytes 589832 | tf_op jit(solution)/shard_map/ppermute | solution.py:74
  21.8 5.5 %collective-permute-start.7 = (bf16[192,256]{1,0:T(8,128)(2,1)S(1)}, bf16[192,256]{1,0:T(8,128)(2,1)S(1)}, u32[]{:S(2)}, u32[]{:S(2)}) collective-permute-start(bf16[192,256]{1,0:T(8,128)(2,1)S(1)} %collective-permute-done.4.refs_5_), channel_id=1, source_target_pairs={{0,4},{1,5},{2,6},{3,7},{4,0},{5,1},{6,2},{7,3},{8,12},{9,13},{10,... | collective-permute-start | bytes 294920 | tf_op jit(solution)/shard_map/ppermute | solution.py:74
  26.1 7.7 %collective-permute-start.10 = (bf16[1152,256]{1,0:T(8,128)(2,1)S(1)}, bf16[1152,256]{1,0:T(8,128)(2,1)S(1)}, u32[]{:S(2)}, u32[]{:S(2)}) collective-permute-start(bf16[1152,256]{1,0:T(8,128)(2,1)S(1)} %pad_maximum_fusion), channel_id=1, source_target_pairs={{0,1},{1,0},{2,3},{3,2},{4,5},{5,4},{6,7},{7,6},{8,9},{9,8},{10,11... | collective-permute-start | bytes 1769480 | tf_op jit(solution)/shard_map/ppermute | solution.py:74
  27.3 4.6 %collective-permute-start.9 = (bf16[192,256]{1,0:T(8,128)(2,1)S(1)}, bf16[192,256]{1,0:T(8,128)(2,1)S(1)}, u32[]{:S(2)}, u32[]{:S(2)}) collective-permute-start(bf16[192,256]{1,0:T(8,128)(2,1)S(1)} %collective-permute-done.7.refs_8_), channel_id=1, source_target_pairs={{0,2},{1,3},{2,0},{3,1},{4,6},{5,7},{6,4},{7,5},{8,10},{9,11},{10,... | collective-permute-start | bytes 294920 | tf_op jit(solution)/shard_map/ppermute | solution.py:74
  28.9 3.2 %collective-permute-start.11 = (bf16[768,256]{1,0:T(8,128)(2,1)S(1)}, bf16[768,256]{1,0:T(8,128)(2,1)S(1)}, u32[]{:S(2)}, u32[]{:S(2)}) collective-permute-start(bf16[768,256]{1,0:T(8,128)(2,1)S(1)} %pad_maximum_fusion.1), channel_id=1, source_target_pairs={{0,1},{1,0},{2,3},{3,2},{4,5},{5,4},{6,7},{7,6},{8,9},{9,8},{10,11... | collective-permute-start | bytes 1179656 | tf_op jit(solution)/shard_map/ppermute | solution.py:74
  32.0 1.8 %collective-permute-start.12 = (bf16[768,256]{1,0:T(8,128)(2,1)S(1)}, bf16[768,256]{1,0:T(8,128)(2,1)S(1)}, u32[]{:S(2)}, u32[]{:S(2)}) collective-permute-start(bf16[768,256]{1,0:T(8,128)(2,1)S(1)} %pad_maximum_fusion.2), channel_id=1, source_target_pairs={{0,1},{1,0},{2,3},{3,2},{4,5},{5,4},{6,7},{7,6},{8,9},{9,8},{10,11... | collective-permute-start | bytes 1179656 | tf_op jit(solution)/shard_map/ppermute | solution.py:74
  37.1 2.4 %collective-permute-start.17 = (bf16[1536,256]{1,0:T(8,128)(2,1)S(1)}, bf16[1536,256]{1,0:T(8,128)(2,1)S(1)}, u32[]{:S(2)}, u32[]{:S(2)}) collective-permute-start(bf16[1536,256]{1,0:T(8,128)(2,1)S(1)} %get-tuple-element.21), channel_id=1, source_target_pairs={{0,1},{1,0},{2,3},{3,2},{4,5},{5,4},{6,7},{7,6},{8,9},{9,8},{10,11... | collective-permute-start | bytes 2359304 | tf_op jit(solution)/shard_map/ppermute | solution.py:74
  37.3 6.0 %collective-permute-start.13 = (bf16[1536,256]{1,0:T(8,128)(2,1)S(1)}, bf16[1536,256]{1,0:T(8,128)(2,1)S(1)}, u32[]{:S(2)}, u32[]{:S(2)}) collective-permute-start(bf16[1536,256]{1,0:T(8,128)(2,1)S(1)} %get-tuple-element.20), channel_id=1, source_target_pairs={{0,1},{1,0},{2,3},{3,2},{4,5},{5,4},{6,7},{7,6},{8,9},{9,8},{10,11... | collective-permute-start | bytes 2359304 | tf_op jit(solution)/shard_map/ppermute | solution.py:74
  39.6 8.7 %collective-permute-start.18 = (bf16[384,256]{1,0:T(8,128)(2,1)S(1)}, bf16[384,256]{1,0:T(8,128)(2,1)S(1)}, u32[]{:S(2)}, u32[]{:S(2)}) collective-permute-start(bf16[384,256]{1,0:T(8,128)(2,1)S(1)} %pad_maximum_fusion.8), channel_id=1, source_target_pairs={{0,6},{1,7},{2,4},{3,5},{4,2},{5,3},{6,0},{7,1},{8,14},{9,15},{10,... | collective-permute-start | bytes 589832 | tf_op jit(solution)/shard_map/ppermute | solution.py:74
  41.7 10.9 %collective-permute-start.19 = (bf16[384,256]{1,0:T(8,128)(2,1)S(1)}, bf16[384,256]{1,0:T(8,128)(2,1)S(1)}, u32[]{:S(2)}, u32[]{:S(2)}) collective-permute-start(bf16[384,256]{1,0:T(8,128)(2,1)S(1)} %pad_maximum_fusion.9), channel_id=1, source_target_pairs={{0,4},{1,5},{2,6},{3,7},{4,0},{5,1},{6,2},{7,3},{8,12},{9,13},{10,... | collective-permute-start | bytes 589832 | tf_op jit(solution)/shard_map/ppermute | solution.py:74
  42.7 9.9 %collective-permute-start.20 = (bf16[384,256]{1,0:T(8,128)(2,1)S(1)}, bf16[384,256]{1,0:T(8,128)(2,1)S(1)}, u32[]{:S(2)}, u32[]{:S(2)}) collective-permute-start(bf16[384,256]{1,0:T(8,128)(2,1)S(1)} %pad_maximum_fusion.10), channel_id=1, source_target_pairs={{0,2},{1,3},{2,0},{3,1},{4,6},{5,7},{6,4},{7,5},{8,10},{9,11},{10,... | collective-permute-start | bytes 589832 | tf_op jit(solution)/shard_map/ppermute | solution.py:74
  43.5 21.6 %copy-start.4 = (f32[192,256]{1,0:T(8,128)S(1)}, f32[192,256]{1,0:T(8,128)}, u32[]{:S(2)}) copy-start(f32[192,256]{1,0:T(8,128)} %param.11) | copy-start | bytes 589828
  43.5 21.6 %copy-start.5 = (f32[192,256]{1,0:T(8,128)S(1)}, f32[192,256]{1,0:T(8,128)}, u32[]{:S(2)}) copy-start(f32[192,256]{1,0:T(8,128)} %param.12) | copy-start | bytes 589828
  43.5 21.6 %copy-start.6 = (f32[192,256]{1,0:T(8,128)S(1)}, f32[192,256]{1,0:T(8,128)}, u32[]{:S(2)}) copy-start(f32[192,256]{1,0:T(8,128)} %param.13) | copy-start | bytes 589828
  43.5 13.3 %collective-permute-start.14 = (bf16[384,256]{1,0:T(8,128)(2,1)S(1)}, bf16[384,256]{1,0:T(8,128)(2,1)S(1)}, u32[]{:S(2)}, u32[]{:S(2)}) collective-permute-start(bf16[384,256]{1,0:T(8,128)(2,1)S(1)} %pad_maximum_fusion.5), channel_id=1, source_target_pairs={{0,6},{1,7},{2,4},{3,5},{4,2},{5,3},{6,0},{7,1},{8,14},{9,15},{10,... | collective-permute-start | bytes 589832 | tf_op jit(solution)/shard_map/ppermute | solution.py:74
  45.6 14.7 %collective-permute-start.15 = (bf16[384,256]{1,0:T(8,128)(2,1)S(1)}, bf16[384,256]{1,0:T(8,128)(2,1)S(1)}, u32[]{:S(2)}, u32[]{:S(2)}) collective-permute-start(bf16[384,256]{1,0:T(8,128)(2,1)S(1)} %pad_maximum_fusion.6), channel_id=1, source_target_pairs={{0,4},{1,5},{2,6},{3,7},{4,0},{5,1},{6,2},{7,3},{8,12},{9,13},{10,... | collective-permute-start | bytes 589832 | tf_op jit(solution)/shard_map/ppermute | solution.py:74
  48.3 12.0 %collective-permute-start.16 = (bf16[384,256]{1,0:T(8,128)(2,1)S(1)}, bf16[384,256]{1,0:T(8,128)(2,1)S(1)}, u32[]{:S(2)}, u32[]{:S(2)}) collective-permute-start(bf16[384,256]{1,0:T(8,128)(2,1)S(1)} %pad_maximum_fusion.7), channel_id=1, source_target_pairs={{0,2},{1,3},{2,0},{3,1},{4,6},{5,7},{6,4},{7,5},{8,10},{9,11},{10,... | collective-permute-start | bytes 589832 | tf_op jit(solution)/shard_map/ppermute | solution.py:74
  52.7 10.2 %collective-permute-start.21 = (bf16[192,256]{1,0:T(8,128)(2,1)S(1)}, bf16[192,256]{1,0:T(8,128)(2,1)S(1)}, u32[]{:S(2)}, u32[]{:S(2)}) collective-permute-start(bf16[192,256]{1,0:T(8,128)(2,1)S(1)} %get-tuple-element.26), channel_id=1, source_target_pairs={{0,16},{1,17},{2,18},{3,19},{4,20},{5,21},{6,22},{7,23},{8,24},{9,... | collective-permute-start | bytes 294920 | tf_op jit(solution)/shard_map/ppermute | solution.py:74
  55.3 7.7 %collective-permute-start.22 = (bf16[192,256]{1,0:T(8,128)(2,1)S(1)}, bf16[192,256]{1,0:T(8,128)(2,1)S(1)}, u32[]{:S(2)}, u32[]{:S(2)}) collective-permute-start(bf16[192,256]{1,0:T(8,128)(2,1)S(1)} %get-tuple-element.27), channel_id=1, source_target_pairs={{0,24},{1,25},{2,26},{3,27},{4,28},{5,29},{6,30},{7,31},{8,16},{9,... | collective-permute-start | bytes 294920 | tf_op jit(solution)/shard_map/ppermute | solution.py:74
  60.4 4.7 %collective-permute-start.23 = (bf16[192,256]{1,0:T(8,128)(2,1)S(1)}, bf16[192,256]{1,0:T(8,128)(2,1)S(1)}, u32[]{:S(2)}, u32[]{:S(2)}) collective-permute-start(bf16[192,256]{1,0:T(8,128)(2,1)S(1)} %fusion.4), channel_id=1, source_target_pairs={{0,8},{1,9},{2,10},{3,11},{4,12},{5,13},{6,14},{7,15},{8,0},{9,1},... | collective-permute-start | bytes 294920 | tf_op jit(solution)/shard_map/ppermute | solution.py:74

commit v3 on v2

--- a/solution.py
+++ b/solution.py
@@ -84,10 +84,10 @@
     return pl.multiple_of(lax.bitwise_xor(me, jnp.int32(offset)) * rows, rows)
 
 
-def turn_kernel(a_ref, b_ref, at_ref, bt_ref, *, step):
-    for source, target in ((a_ref, at_ref), (b_ref, bt_ref)):
-        for start in range(0, source.shape[1], step):
-            target[start : start + step, :] = source[:, start : start + step].T
+def chip_start(kz, kx, ky, rows):
+    me = lax.axis_index("grp") * 2 + lax.axis_index("rep") // 2
+    offset = (kz * 2 + kx) * 2 + ky
+    return pl.multiple_of(lax.bitwise_xor(me, jnp.int32(offset)) * (2 * rows), 2 * rows)
 
 
 def fdot(a, b, dims):
@@ -99,23 +99,51 @@
 TM = ((0,), (0,))
 
 
+def project(pieces, places, acts, cots, weights, rows, head):
+    chips = []
+    core = lax.axis_index("rep") % 2
+    for piece, place in zip(pieces, places):
+        if place[0] is None:
+            for ky in (0, 1):
+                chip = (0, 0, ky)
+                chips.append(chip)
+                offset = (chips.index(chip)) * 2 * rows
+                start = pl.multiple_of(chip_start(*chip, rows) % (4 * rows), 2 * rows)
+                weights[offset : offset + 2 * rows, :] = piece[pl.ds(start, 2 * rows), :]
+            continue
+        for index, (*chip, kc) in enumerate(place):
+            chip = tuple(chip)
+            if chip not in chips:
+                chips.append(chip)
+            offset = chips.index(chip) * 2 * rows + lax.bitwise_xor(core, jnp.int32(kc)) * rows
+            weights[pl.ds(pl.multiple_of(offset, rows), rows), :] = piece[index * rows : (index + 1) * rows, :]
+    front = back = 0.0
+    for index, chip in enumerate(chips):
+        columns = pl.ds(chip_start(*chip, rows), 2 * rows)
+        block = weights[index * 2 * rows : (index + 1) * 2 * rows, :]
+        front += fdot(acts[:, columns], block[:, : 3 * head], MM)
+        back += fdot(cots[:, columns], block[:, 3 * head :], MM)
+    return front, back
+
+
+def turn_kernel(step, source, target):
+    for start in range(0, source.shape[1], step):
+        target[start : start + step, :] = source[:, start : start + step].T
+
+
+def early_kernel(places, rows, head, *refs):
+    count = len(places)
+    acts, cots, front, back, weights = refs[count:]
+    front[...], back[...] = project(refs[:count], places, acts, cots, weights, rows, head)
+
+
 def attend_kernel(places, rows, head, grad_scale, *refs):
     count = len(places)
-    pieces = refs[:count]
-    acts, cots, docs, acts_t, cots_t = refs[count : count + 5]
-    far_ref, near_ref, left_ref, right_ref, weights = refs[count + 5 :]
-    for piece, place in zip(pieces, places):
-        for index, where in enumerate(place):
-            if where is None:
-                size = piece.shape[0]
-                start = pl.multiple_of(lax.axis_index("grp") * size, size)
-                weights[pl.ds(start, size), :] = piece[...]
-            else:
-                weights[pl.ds(block_start(*where, rows), rows), :] = piece[
-                    index * rows : (index + 1) * rows, :
-                ]
-    projected = fdot(acts[...], weights[:, : 3 * head], MM).astype(jnp.bfloat16)
-    back_context = fdot(cots[...], weights[:, 3 * head :], MM).astype(jnp.bfloat16)
+    acts, cots, docs, acts_t, cots_t, front_ref, back_ref = refs[count : count + 7]
+    far_ref, left_ref, right_ref, weights = refs[count + 7 :]
+    front, back = project(refs[:count], places, acts, cots, weights, rows, head)
+    projected = (front_ref[...] + front).astype(jnp.bfloat16)
+    back_context = (back_ref[...] + back).astype(jnp.bfloat16)
     queries = projected[:, :head]
     key_rows = projected[:, head : 2 * head]
     value_rows = projected[:, 2 * head :]
@@ -142,7 +170,6 @@
     left_ref[...] = left
     right_ref[...] = right
     write_terms(acts_t, cots_t, left, right, far_ref, FAR, 1, rows, grad_scale)
-    write_terms(acts_t, cots_t, left, right, near_ref, NEAR, 1, rows, grad_scale)
 
 
 def write_terms(acts_t, cots_t, left, right, out_ref, kzs, kc, rows, grad_scale):
@@ -153,8 +180,8 @@
         out_ref[index * rows : (index + 1) * rows, :] = (term * grad_scale).astype(out_ref.dtype)
 
 
-def mine_kernel(kzs, rows, grad_scale, acts_t, cots_t, left_ref, right_ref, out_ref):
-    write_terms(acts_t, cots_t, left_ref[...], right_ref[...], out_ref, kzs, 0, rows, grad_scale)
+def terms_kernel(kzs, kc, rows, grad_scale, acts_t, cots_t, left_ref, right_ref, out_ref):
+    write_terms(acts_t, cots_t, left_ref[...], right_ref[...], out_ref, kzs, kc, rows, grad_scale)
 
 
 def vmem(count):
@@ -174,52 +201,38 @@
     )(*args)
 
 
-def gather(weight_copy, rows, beside):
+def gather(weight_copy, rows, first, second):
     rep = lax.axis_index("rep")
     own = lax.dynamic_slice_in_dim(weight_copy, rep * rows, rows, 0)
     half = lax.dynamic_slice_in_dim(weight_copy, jnp.bitwise_xor(rep, 2) * rows, rows, 0)
     both = join(own, half)
     z2 = hop(own, 2, 0, 0, 0)
+    x0 = hop(both, 0, 1, 0, 0)
+    z2, first = lax.optimization_barrier((z2, first))
     z1 = hop(both, 1, 0, 0, 0)
-    x0 = hop(both, 0, 1, 0, 0)
-    zx = hop(both, 1, 1, 0, 0)
-    z2, *beside = lax.optimization_barrier((z2, *beside))
     z3 = hop(z2, 1, 0, 0, 0)
     x2 = hop(z2, 0, 1, 0, 0)
-    y2 = hop(z2, 0, 0, 1, 0)
+    z3, x0, x2 = lax.optimization_barrier((z3, x0, x2))
     x3 = hop(z3, 0, 1, 0, 0)
-    ya = hop(join(z3, x2), 0, 0, 1, 0)
+    ya = hop(join(z2, z3, x2), 0, 0, 1, 0)
+    zx = hop(x0, 1, 0, 0, 0)
     yb = hop(x3, 0, 0, 1, 0)
-    c0 = hop(join(z1, x0, zx), 0, 0, 0, 1)
-    c1 = hop(join(z2, z3, x2, y2), 0, 0, 0, 1)
-    c2 = hop(join(x3, ya, yb), 0, 0, 0, 1)
-    z1_at = [(1, 0, 0), (1, 0, 1)]
-    x0_at = [(0, 1, 0), (0, 1, 1)]
-    zx_at = [(1, 1, 0), (1, 1, 1)]
-    z2_at, z3_at, x2_at, y2_at = [(2, 0, 0)], [(3, 0, 0)], [(2, 1, 0)], [(2, 0, 1)]
-    x3_at, yb_at = [(3, 1, 0)], [(3, 1, 1)]
-    ya_at = [(3, 0, 1), (2, 1, 1)]
-
-    def core(kc, *lists):
-        return [(*at, kc) for one in lists for at in one]
-
-    pieces = [
-        (weight_copy, [None]),
-        (z1, core(0, z1_at)),
-        (x0, core(0, x0_at)),
-        (zx, core(0, zx_at)),
-        (z2, core(0, z2_at)),
-        (z3, core(0, z3_at)),
-        (x2, core(0, x2_at)),
-        (y2, core(0, y2_at)),
-        (x3, core(0, x3_at)),
-        (ya, core(0, ya_at)),
-        (yb, core(0, yb_at)),
-        (c0, core(1, z1_at, x0_at, zx_at)),
-        (c1, core(1, z2_at, z3_at, x2_at, y2_at)),
-        (c2, core(1, x3_at, ya_at, yb_at)),
-    ]
-    return pieces, beside
+    yb, second = lax.optimization_barrier((yb, second))
+
+    def both_cores(arrays, places):
+        other = hop(join(*arrays), 0, 0, 0, 1)
+        pieces = [(array, [(*at, 0) for at in place]) for array, place in zip(arrays, places)]
+        return pieces + [(other, [(*at, 1) for place in places for at in place])]
+
+    early = both_cores(
+        (x0, z1, z2, z3, x2),
+        ([(0, 1, 0), (0, 1, 1)], [(1, 0, 0), (1, 0, 1)], [(2, 0, 0)], [(3, 0, 0)], [(2, 1, 0)]),
+    )
+    late = both_cores(
+        (x3, zx, ya, yb),
+        ([(3, 1, 0)], [(1, 1, 0), (1, 1, 1)], [(2, 0, 1), (3, 0, 1), (2, 1, 1)], [(3, 1, 1)]),
+    )
+    return [(weight_copy, [None]), *early], late, first, second
 
 
 def plane_sum(mine, received, kzs, rows):
@@ -242,33 +255,47 @@
     rows = primary.shape[0]
     head = columns // 4
     grad_scale = 1.0 / math.sqrt(32 * tokens)
-    turned = jax.ShapeDtypeStruct((depth, tokens), jnp.bfloat16)
-    acts_t, cots_t = kernel_call(
-        functools.partial(turn_kernel, step=512), [turned, turned], "turn", (acts, cots)
-    )
-    pieces, (acts_t, cots_t) = gather(weight_copy, rows, (acts_t, cots_t))
-    places = [place for _, place in pieces]
-    side = jax.ShapeDtypeStruct((tokens, columns), jnp.bfloat16)
-    other = jax.ShapeDtypeStruct((8 * rows, columns), jnp.bfloat16)
-    far, near, left, right = kernel_call(
-        functools.partial(attend_kernel, places, rows, head, grad_scale),
-        [other, other, side, side],
+    bfloat = functools.partial(jax.ShapeDtypeStruct, dtype=jnp.bfloat16)
+    float32 = functools.partial(jax.ShapeDtypeStruct, dtype=jnp.float32)
+    flops = 4 * tokens * depth * columns
+
+    acts_t, cots_t = [
+        kernel_call(
+            functools.partial(turn_kernel, 512), [bfloat((depth, tokens))], "turn", (source,), flops=flops // 2
+        )[0]
+        for source in (acts, cots)
+    ]
+    early, late, acts_t, cots_t = gather(weight_copy, rows, acts_t, cots_t)
+    front, back = kernel_call(
+        functools.partial(early_kernel, [place for _, place in early], rows, head),
+        [float32((tokens, 3 * head)), float32((tokens, head))],
+        "early",
+        (*[piece for piece, _ in early], acts, cots),
+        scratch=[pltpu.VMEM((24 * rows, columns), jnp.bfloat16)],
+        flops=flops,
+    )
+    far, left, right = kernel_call(
+        functools.partial(attend_kernel, [place for _, place in late], rows, head, grad_scale),
+        [bfloat((8 * rows, columns))] + [bfloat((tokens, columns))] * 2,
         "attend",
-        (*[piece for piece, _ in pieces], acts, cots, documents, acts_t, cots_t),
-        scratch=[pltpu.VMEM((depth, columns), jnp.bfloat16)],
-        flops=4 * tokens * depth * columns,
-    )
+        (*[piece for piece, _ in late], acts, cots, documents, acts_t, cots_t, front, back),
+        scratch=[pltpu.VMEM((16 * rows, columns), jnp.bfloat16)],
+        flops=flops,
+    )
+
+    def terms(kzs, kc, dtype):
+        return kernel_call(
+            functools.partial(terms_kernel, kzs, kc, rows, grad_scale),
+            [dtype((4 * len(kzs) * rows, columns))],
+            "terms",
+            (acts_t, cots_t, left, right),
+            flops=flops * len(kzs) // 8,
+        )[0]
+
     totals = {}
-    for kzs, sent in ((FAR, far), (NEAR, near)):
+    for kzs, sent in ((FAR, far), (NEAR, terms(NEAR, 1, bfloat))):
         received = hop(sent, 0, 0, 0, 1)
-        (mine,) = kernel_call(
-            functools.partial(mine_kernel, kzs, rows, grad_scale),
-            [jax.ShapeDtypeStruct((8 * rows, columns), jnp.float32)],
-            "mine",
-            (acts_t, cots_t, left, right),
-            flops=tokens * depth * columns,
-        )
-        totals.update(zip(kzs, plane_sum(mine, received, kzs, rows)))
+        totals.update(zip(kzs, plane_sum(terms(kzs, 0, float32), received, kzs, rows)))
     gradient = totals[0]
     for kz in (2, 3, 1):
         gradient += hop(totals[kz].astype(jnp.bfloat16), kz, 0, 0, 0).astype(jnp.float32)

time: 73.5 us -> 68.3 us (0.929)
  waiting for transfers between devices: 25 us -> 20.6 us
  local copies, waits for them, and re-layouts: 5.07 us -> 3.47 us
  Pallas kernels: 6.13 us -> 7.1 us
    ppermute x24 -> x22, waiting for transfers between devices: 25 us -> 20.6 us  [hop(): return lax.ppermute(value, AXES, [(i, i ^ offset) for i in range(32)])]
    unnamed x15 -> x21, local copies, waits for them, and re-layouts: 4.11 us -> 2.5 us
    pallas_call x4 -> x7, Pallas kernels: 6.13 us -> 7.1 us  [kernel_call(): pl.pallas_call(body, out_shape=outs, in_specs=vmem(len(args)), out_specs=...]
    ppermute x24 -> x22, starting transfers between devices: 28.1 us -> 28 us  [hop(): return lax.ppermute(value, AXES, [(i, i ^ offset) for i in range(32)])]
  transfers between devices with their start and end apart: 24 -> 22, of which waited for: 12 -> 12; matrix products, arithmetic and copies ran while one was open for 1% -> 1% of each run, Pallas kernels for 4% -> 7%
where the time goes in v3:
time: 68.3 us; the launch traced here: 68.1 us
  starting transfers between devices  28 us (41%)
  waiting for transfers between devices  20.6 us (30%)
  Pallas kernels  7.1 us (10%)
  blocking collectives  6.47 us (9%)
  local copies, waits for them, and re-layouts  3.47 us (5%)
  other arithmetic  1.6 us (2%)
  between operations  0.92 us (1%)
    ppermute x22, starting transfers between devices, hop(): return lax.ppermute(value, AXES, [(i, i ^ offset) for i in range(32)])  28 us
    ppermute x22, waiting for transfers between devices, hop(): return lax.ppermute(value, AXES, [(i, i ^ offset) for i in range(32)])  20.6 us
    pallas_call x7, Pallas kernels, kernel_call(): pl.pallas_call(body, out_shape=outs, in_specs=vmem(len(args)), out_specs=...  7.1 us
    all_gather x1, blocking collectives, block_body(): lax.all_gather(primary_new.astype(jnp.bfloat16), 'rep', axis=0, tiled=True)  6.47 us
    unnamed x21, local copies, waits for them, and re-layouts  2.5 us
  transfers between devices with their start and end apart: 22, of which 12 were waited for; matrix products, arithmetic and copies ran while one was open for 1% of the time, Pallas kernels for 7%

profile of v3, /device:TPU:0, one launch (start us, length us, event | category | flops | bytes accessed | tf_op | source)
XLA Modules:
  0.0 68.1 jit_solution(17691186786344230970)
XLA Ops:
  0.6 1.0 %constant_dynamic-slice_fusion = (bf16[192,256]{1,0:T(8,128)(2,1)S(1)}, bf16[192,256]{1,0:T(8,128)(2,1)S(1)}) fusion(bf16[768,256]{1,0:T(8,128)(2,1)} %refs_0_.1, s32[]{:T(128)S(6)} %select_n.7, s32[]{:T(128)S(6)} %select_n.6), kind=kLoop, calls=%fused_computation.64 | loop fusion | bytes 393224 | tf_op jit(solution)/shard_map/dynamic_slice | solution.py:207
  1.6 4.1 %collective-permute-start = (bf16[192,256]{1,0:T(8,128)(2,1)S(1)}, bf16[192,256]{1,0:T(8,128)(2,1)S(1)}, u32[]{:S(2)}, u32[]{:S(2)}) collective-permute-start(bf16[192,256]{1,0:T(8,128)(2,1)S(1)} %get-tuple-element.47), channel_id=1, source_target_pairs={{0,16},{1,17},{2,18},{3,19},{4,20},{5,21},{6,22},{7,23},{8,24},{9,... | collective-permute-start | bytes 294920 | tf_op jit(solution)/shard_map/ppermute | solution.py:74
  5.7 1.6 %collective-permute-start.2 = (bf16[384,256]{1,0:T(8,128)(2,1)S(1)}, bf16[384,256]{1,0:T(8,128)(2,1)S(1)}, u32[]{:S(2)}, u32[]{:S(2)}) collective-permute-start(bf16[384,256]{1,0:T(8,128)(2,1)S(1)} %pad_maximum_fusion.2), channel_id=1, source_target_pairs={{0,4},{1,5},{2,6},{3,7},{4,0},{5,1},{6,2},{7,3},{8,12},{9,13},{10,... | collective-permute-start | bytes 589832 | tf_op jit(solution)/shard_map/ppermute | solution.py:74
  7.3 1.7 %copy-done = bf16[1,192,6144]{2,1,0:T(8,128)(2,1)S(1)} copy-done((bf16[1,192,6144]{2,1,0:T(8,128)(2,1)S(1)}, bf16[1,192,6144]{2,1,0:T(8,128)(2,1)}, u32[]{:S(2)}) %copy-start) | copy-done | bytes 2359320
  8.9 0.9 %turn.2.refs_8_.acts_t = bf16[6144,192]{1,0:T(8,128)(2,1)S(1)} custom-call(bf16[192,6144]{1,0:T(8,128)(2,1)S(1)} %bitcast.2), custom_call_target="tpu_custom_call" | custom-call | flops 603979776 | bytes 4194304 | tf_op jit(solution)/shard_map/turn/pallas_call | solution.py:192
  9.8 0.8 %collective-permute-done.refs_3_ = bf16[192,256]{1,0:T(8,128)(2,1)S(1)} collective-permute-done((bf16[192,256]{1,0:T(8,128)(2,1)S(1)}, bf16[192,256]{1,0:T(8,128)(2,1)S(1)}, u32[]{:S(2)}, u32[]{:S(2)}) %collective-permute-start) | collective-permute-done | bytes 98336 | tf_op jit(solution)/shard_map/ppermute | solution.py:74
  10.6 0.9 %collective-permute-start.1 = (bf16[192,256]{1,0:T(8,128)(2,1)S(1)}, bf16[192,256]{1,0:T(8,128)(2,1)S(1)}, u32[]{:S(2)}, u32[]{:S(2)}) collective-permute-start(bf16[192,256]{1,0:T(8,128)(2,1)S(1)} %collective-permute-done.refs_3_), channel_id=1, source_target_pairs={{0,8},{1,9},{2,10},{3,11},{4,12},{5,13},{6,14},{7,15},{8,0},{9,1},... | collective-permute-start | bytes 294920 | tf_op jit(solution)/shard_map/ppermute | solution.py:74
  11.5 1.3 %collective-permute-start.3 = (bf16[192,256]{1,0:T(8,128)(2,1)S(1)}, bf16[192,256]{1,0:T(8,128)(2,1)S(1)}, u32[]{:S(2)}, u32[]{:S(2)}) collective-permute-start(bf16[192,256]{1,0:T(8,128)(2,1)S(1)} %collective-permute-done.refs_3_), channel_id=1, source_target_pairs={{0,4},{1,5},{2,6},{3,7},{4,0},{5,1},{6,2},{7,3},{8,12},{9,13},{10,... | collective-permute-start | bytes 294920 | tf_op jit(solution)/shard_map/ppermute | solution.py:74
  12.8 1.4 %collective-permute-start.9 = (bf16[384,256]{1,0:T(8,128)(2,1)S(1)}, bf16[384,256]{1,0:T(8,128)(2,1)S(1)}, u32[]{:S(2)}, u32[]{:S(2)}) collective-permute-start(bf16[384,256]{1,0:T(8,128)(2,1)S(1)} %pad_maximum_fusion.2), channel_id=1, source_target_pairs={{0,8},{1,9},{2,10},{3,11},{4,12},{5,13},{6,14},{7,15},{8,0},{9,1},... | collective-permute-start | bytes 589832 | tf_op jit(solution)/shard_map/ppermute | solution.py:74
  14.2 0.9 %turn.3.refs_9_.cots_t = bf16[6144,192]{1,0:T(8,128)(2,1)S(1)} custom-call(bf16[192,6144]{1,0:T(8,128)(2,1)S(1)} %bitcast.5), custom_call_target="tpu_custom_call" | custom-call | flops 603979776 | bytes 4194304 | tf_op jit(solution)/shard_map/turn/pallas_call | solution.py:192
  15.1 0.0 copy-start.1
  15.1 0.0 copy-start.3
  15.1 0.5 collective-permute-done.1.refs_4_
  15.6 0.5 collective-permute-done.3.refs_5_
  16.1 1.7 %collective-permute-start.4 = (bf16[192,256]{1,0:T(8,128)(2,1)S(1)}, bf16[192,256]{1,0:T(8,128)(2,1)S(1)}, u32[]{:S(2)}, u32[]{:S(2)}) collective-permute-start(bf16[192,256]{1,0:T(8,128)(2,1)S(1)} %collective-permute-done.1.refs_4_), channel_id=1, source_target_pairs={{0,4},{1,5},{2,6},{3,7},{4,0},{5,1},{6,2},{7,3},{8,12},{9,13},{10,... | collective-permute-start | bytes 294920 | tf_op jit(solution)/shard_map/ppermute | solution.py:74
  17.8 1.6 %collective-permute-start.7 = (bf16[576,256]{1,0:T(8,128)(2,1)S(1)}, bf16[576,256]{1,0:T(8,128)(2,1)S(1)}, u32[]{:S(2)}, u32[]{:S(2)}) collective-permute-start(bf16[576,256]{1,0:T(8,128)(2,1)S(1)} %pad_maximum_fusion.1), channel_id=1, source_target_pairs={{0,2},{1,3},{2,0},{3,1},{4,6},{5,7},{6,4},{7,5},{8,10},{9,11},{10,... | collective-permute-start | bytes 884744 | tf_op jit(solution)/shard_map/ppermute | solution.py:74
  19.4 1.0 %collective-permute-start.6 = (bf16[384,256]{1,0:T(8,128)(2,1)S(1)}, bf16[384,256]{1,0:T(8,128)(2,1)S(1)}, u32[]{:S(2)}, u32[]{:S(2)}) collective-permute-start(bf16[384,256]{1,0:T(8,128)(2,1)S(1)} %collective-permute-done.2.refs_1_), channel_id=1, source_target_pairs={{0,8},{1,9},{2,10},{3,11},{4,12},{5,13},{6,14},{7,15},{8,0},{9,1},... | collective-permute-start | bytes 589832 | tf_op jit(solution)/shard_map/ppermute | solution.py:74
  20.4 0.0 collective-permute-done.9.refs_2_
  20.5 0.2 collective-permute-done.4.refs_0_
  20.7 1.5 %collective-permute-start.5 = (bf16[192,256]{1,0:T(8,128)(2,1)S(1)}, bf16[192,256]{1,0:T(8,128)(2,1)S(1)}, u32[]{:S(2)}, u32[]{:S(2)}) collective-permute-start(bf16[192,256]{1,0:T(8,128)(2,1)S(1)} %collective-permute-done.4.refs_0_), channel_id=1, source_target_pairs={{0,2},{1,3},{2,0},{3,1},{4,6},{5,7},{6,4},{7,5},{8,10},{9,11},{10,... | collective-permute-start | bytes 294920 | tf_op jit(solution)/shard_map/ppermute | solution.py:74
  22.3 0.1 collective-permute-start.10
  22.3 4.8 %collective-permute-done.5.refs_3_ = bf16[192,256]{1,0:T(8,128)(2,1)S(1)} collective-permute-done((bf16[192,256]{1,0:T(8,128)(2,1)S(1)}, bf16[192,256]{1,0:T(8,128)(2,1)S(1)}, u32[]{:S(2)}, u32[]{:S(2)}) %collective-permute-start.5) | collective-permute-done | bytes 98336 | tf_op jit(solution)/shard_map/ppermute | solution.py:74
  27.1 0.0 collective-permute-done.6.refs_1_
  27.2 0.0 collective-permute-done.7.refs_2_
  27.2 0.0 copy-start.4
  27.2 0.1 collective-permute-start.8
  27.3 0.0 collective-permute-done.10.refs_6_
  27.3 1.2 %early.1 = (f32[192,192]{1,0:T(8,128)S(1)}, f32[192,64]{1,0:T(8,128)S(1)}) custom-call(bf16[768,256]{1,0:T(8,128)(2,1)S(1)} %copy-done.3, bf16[384,256]{1,0:T(8,128)(2,1)S(1)} %collective-permute-done.2.refs_1_, bf16[384,256]{1,0:T(8,128)(2,1)S(1)} %collective-permute-done.9.refs_2_, bf16[192,256]{1,0:T(8,128)(2,1)S(1)} %collective-permute-done.refs_3_, ...), custom_call_target="tpu_custom_call" | custom-call | flops 1207959552 | bytes 4194304 | tf_op jit(solution)/shard_map/early/pallas_call | solution.py:192
  28.5 0.9 %collective-permute-done.8.refs_4_ = bf16[1344,256]{1,0:T(8,128)(2,1)S(1)} collective-permute-done((bf16[1344,256]{1,0:T(8,128)(2,1)S(1)}, bf16[1344,256]{1,0:T(8,128)(2,1)S(1)}, u32[]{:S(2)}, u32[]{:S(2)}) %collective-permute-start.8) | collective-permute-done | bytes 688160 | tf_op jit(solution)/shard_map/ppermute | solution.py:74
  29.4 2.5 %attend.1 = (bf16[1536,256]{1,0:T(8,128)(2,1)S(1)}, bf16[192,256]{1,0:T(8,128)(2,1)S(1)}, bf16[192,256]{1,0:T(8,128)(2,1)S(1)}) custom-call(bf16[192,256]{1,0:T(8,128)(2,1)S(1)} %collective-permute-done.4.refs_0_, bf16[384,256]{1,0:T(8,128)(2,1)S(1)} %collective-permute-done.6.refs_1_, bf16[576,256]{1,0:T(8,128)(2,1)S(1)} %collective-permute-done.7.refs_2_, ...), custom_call_target="tpu_custom_call" | custom-call | flops 1207959552 | bytes 4194304 | tf_op jit(solution)/shard_map/attend/pallas_call | solution.py:192
  31.9 0.2 collective-permute-start.15
  32.1 0.6 terms.4
  32.7 0.4 collective-permute-start.11
  33.1 0.6 terms.5
  33.7 0.6 terms.3
  34.3 0.0 collective-permute-done.15
  34.3 0.1 fusion.14
  34.4 1.6 %collective-permute-start.16 = (bf16[384,256]{1,0:T(8,128)(2,1)S(1)}, bf16[384,256]{1,0:T(8,128)(2,1)S(1)}, u32[]{:S(2)}, u32[]{:S(2)}) collective-permute-start(bf16[384,256]{1,0:T(8,128)(2,1)S(1)} %pad_maximum_fusion.6), channel_id=1, source_target_pairs={{0,6},{1,7},{2,4},{3,5},{4,2},{5,3},{6,0},{7,1},{8,14},{9,15},{10,... | collective-permute-start | bytes 589832 | tf_op jit(solution)/shard_map/ppermute | solution.py:74
  36.0 1.6 %collective-permute-start.17 = (bf16[384,256]{1,0:T(8,128)(2,1)S(1)}, bf16[384,256]{1,0:T(8,128)(2,1)S(1)}, u32[]{:S(2)}, u32[]{:S(2)}) collective-permute-start(bf16[384,256]{1,0:T(8,128)(2,1)S(1)} %pad_maximum_fusion.7), channel_id=1, source_target_pairs={{0,4},{1,5},{2,6},{3,7},{4,0},{5,1},{6,2},{7,3},{8,12},{9,13},{10,... | collective-permute-start | bytes 589832 | tf_op jit(solution)/shard_map/ppermute | solution.py:74
  37.6 0.6 collective-permute-start.18
  38.2 0.0 collective-permute-done.11
  38.2 0.1 fusion.24
  38.3 0.0 copy-start.5
  38.3 0.0 copy-start.6
  38.3 0.0 copy-start.7
  38.4 1.6 %collective-permute-start.12 = (bf16[384,256]{1,0:T(8,128)(2,1)S(1)}, bf16[384,256]{1,0:T(8,128)(2,1)S(1)}, u32[]{:S(2)}, u32[]{:S(2)}) collective-permute-start(bf16[384,256]{1,0:T(8,128)(2,1)S(1)} %pad_maximum_fusion.3), channel_id=1, source_target_pairs={{0,6},{1,7},{2,4},{3,5},{4,2},{5,3},{6,0},{7,1},{8,14},{9,15},{10,... | collective-permute-start | bytes 589832 | tf_op jit(solution)/shard_map/ppermute | solution.py:74
  39.9 1.6 %collective-permute-start.13 = (bf16[384,256]{1,0:T(8,128)(2,1)S(1)}, bf16[384,256]{1,0:T(8,128)(2,1)S(1)}, u32[]{:S(2)}, u32[]{:S(2)}) collective-permute-start(bf16[384,256]{1,0:T(8,128)(2,1)S(1)} %pad_maximum_fusion.4), channel_id=1, source_target_pairs={{0,4},{1,5},{2,6},{3,7},{4,0},{5,1},{6,2},{7,3},{8,12},{9,13},{10,... | collective-permute-start | bytes 589832 | tf_op jit(solution)/shard_map/ppermute | solution.py:74
  41.5 1.7 %collective-permute-done.16 = bf16[384,256]{1,0:T(8,128)(2,1)S(1)} collective-permute-done((bf16[384,256]{1,0:T(8,128)(2,1)S(1)}, bf16[384,256]{1,0:T(8,128)(2,1)S(1)}, u32[]{:S(2)}, u32[]{:S(2)}) %collective-permute-start.16) | collective-permute-done | bytes 196640 | tf_op jit(solution)/shard_map/ppermute | solution.py:74
  43.2 1.5 %collective-permute-start.14 = (bf16[384,256]{1,0:T(8,128)(2,1)S(1)}, bf16[384,256]{1,0:T(8,128)(2,1)S(1)}, u32[]{:S(2)}, u32[]{:S(2)}) collective-permute-start(bf16[384,256]{1,0:T(8,128)(2,1)S(1)} %pad_maximum_fusion.5), channel_id=1, source_target_pairs={{0,2},{1,3},{2,0},{3,1},{4,6},{5,7},{6,4},{7,5},{8,10},{9,11},{10,... | collective-permute-start | bytes 589832 | tf_op jit(solution)/shard_map/ppermute | solution.py:74
  44.7 2.7 %collective-permute-done.17 = bf16[384,256]{1,0:T(8,128)(2,1)S(1)} collective-permute-done((bf16[384,256]{1,0:T(8,128)(2,1)S(1)}, bf16[384,256]{1,0:T(8,128)(2,1)S(1)}, u32[]{:S(2)}, u32[]{:S(2)}) %collective-permute-start.17) | collective-permute-done | bytes 196640 | tf_op jit(solution)/shard_map/ppermute | solution.py:74
  47.5 0.0 collective-permute-done.18
  47.5 0.1 fusion.18
  47.6 3.4 %collective-permute-start.19 = (bf16[192,256]{1,0:T(8,128)(2,1)S(1)}, bf16[192,256]{1,0:T(8,128)(2,1)S(1)}, u32[]{:S(2)}, u32[]{:S(2)}) collective-permute-start(bf16[192,256]{1,0:T(8,128)(2,1)S(1)} %get-tuple-element.32), channel_id=1, source_target_pairs={{0,16},{1,17},{2,18},{3,19},{4,20},{5,21},{6,22},{7,23},{8,24},{9,... | collective-permute-start | bytes 294920 | tf_op jit(solution)/shard_map/ppermute | solution.py:74
  51.0 0.0 collective-permute-start.20
  51.0 0.6 collective-permute-done.12
  51.7 3.5 %collective-permute-done.13 = bf16[384,256]{1,0:T(8,128)(2,1)S(1)} collective-permute-done((bf16[384,256]{1,0:T(8,128)(2,1)S(1)}, bf16[384,256]{1,0:T(8,128)(2,1)S(1)}, u32[]{:S(2)}, u32[]{:S(2)}) %collective-permute-start.13) | collective-permute-done | bytes 196640 | tf_op jit(solution)/shard_map/ppermute | solution.py:74
  55.1 0.0 collective-permute-done.14
  55.1 0.1 fusion.4
  55.2 0.5 collective-permute-start.21
  55.7 2.2 %collective-permute-done.19 = bf16[192,256]{1,0:T(8,128)(2,1)S(1)} collective-permute-done((bf16[192,256]{1,0:T(8,128)(2,1)S(1)}, bf16[192,256]{1,0:T(8,128)(2,1)S(1)}, u32[]{:S(2)}, u32[]{:S(2)}) %collective-permute-start.19) | collective-permute-done | bytes 98336 | tf_op jit(solution)/shard_map/ppermute | solution.py:74
  57.9 2.0 %collective-permute-done.21 = bf16[192,256]{1,0:T(8,128)(2,1)S(1)} collective-permute-done((bf16[192,256]{1,0:T(8,128)(2,1)S(1)}, bf16[192,256]{1,0:T(8,128)(2,1)S(1)}, u32[]{:S(2)}, u32[]{:S(2)}) %collective-permute-start.21) | collective-permute-done | bytes 98336 | tf_op jit(solution)/shard_map/ppermute | solution.py:74
  59.9 1.0 %fusion.31 = (bf16[192,256]{1,0:T(8,128)(2,1)S(1)}, f32[192,256]{1,0:T(8,128)}, f32[192,256]{1,0:T(8,128)}, f32[192,256]{1,0:T(8,128)}) fusion(f32[192,256]{1,0:T(8,128)S(1)} %copy-done.5, f32[192,256]{1,0:T(8,128)S(1)} %copy-done.6, f32[192,256]{1,0:T(8,128)S(1)} %copy-done.7, bf16[192,256]{1,0:T(8,128)(2,1)S(1)} %collective-permute-done.21, ...), kind=kLoop, calls=%fused_computation.66 | loop fusion | flops 1474560 | bytes 2162688 | tf_op jit(solution)/shard_map/convert_element_type | solution.py:303
  60.9 6.5 %all_gather.3 = bf16[768,256]{1,0:T(8,128)(2,1)S(1)} all-gather(bf16[192,256]{1,0:T(8,128)(2,1)S(1)} %get-tuple-element.28), channel_id=1, replica_groups=mesh['grp'=8,'rep'=4] {'rep'}, dimensions={0}, use_global_device_ids=true | all-gather | bytes 491520 | tf_op jit(solution)/shard_map/all_gather | solution.py:303
  67.4 0.7 %copy.16 = bf16[768,256]{1,0:T(8,128)(2,1)} copy(bf16[768,256]{1,0:T(8,128)(2,1)S(1)} %all_gather.3) | data formatting | bytes 786432
  (25 shorter events, 0.2 us)
Async XLA Ops:
  1.6 9.0 %collective-permute-start = (bf16[192,256]{1,0:T(8,128)(2,1)S(1)}, bf16[192,256]{1,0:T(8,128)(2,1)S(1)}, u32[]{:S(2)}, u32[]{:S(2)}) collective-permute-start(bf16[192,256]{1,0:T(8,128)(2,1)S(1)} %get-tuple-element.47), channel_id=1, source_target_pairs={{0,16},{1,17},{2,18},{3,19},{4,20},{5,21},{6,22},{7,23},{8,24},{9,... | collective-permute-start | bytes 294920 | tf_op jit(solution)/shard_map/ppermute | solution.py:74
  5.7 9.4 %collective-permute-start.2 = (bf16[384,256]{1,0:T(8,128)(2,1)S(1)}, bf16[384,256]{1,0:T(8,128)(2,1)S(1)}, u32[]{:S(2)}, u32[]{:S(2)}) collective-permute-start(bf16[384,256]{1,0:T(8,128)(2,1)S(1)} %pad_maximum_fusion.2), channel_id=1, source_target_pairs={{0,4},{1,5},{2,6},{3,7},{4,0},{5,1},{6,2},{7,3},{8,12},{9,13},{10,... | collective-permute-start | bytes 589832 | tf_op jit(solution)/shard_map/ppermute | solution.py:74
  7.3 1.7 %copy-start = (bf16[1,192,6144]{2,1,0:T(8,128)(2,1)S(1)}, bf16[1,192,6144]{2,1,0:T(8,128)(2,1)}, u32[]{:S(2)}) copy-start(bf16[1,192,6144]{2,1,0:T(8,128)(2,1)} %param.7) | copy-start | bytes 7077892
  8.9 5.2 %copy-start.2 = (bf16[1,192,6144]{2,1,0:T(8,128)(2,1)S(1)}, bf16[1,192,6144]{2,1,0:T(8,128)(2,1)}, u32[]{:S(2)}) copy-start(bf16[1,192,6144]{2,1,0:T(8,128)(2,1)} %param.8) | copy-start | bytes 7077892
  10.6 5.0 %collective-permute-start.1 = (bf16[192,256]{1,0:T(8,128)(2,1)S(1)}, bf16[192,256]{1,0:T(8,128)(2,1)S(1)}, u32[]{:S(2)}, u32[]{:S(2)}) collective-permute-start(bf16[192,256]{1,0:T(8,128)(2,1)S(1)} %collective-permute-done.refs_3_), channel_id=1, source_target_pairs={{0,8},{1,9},{2,10},{3,11},{4,12},{5,13},{6,14},{7,15},{8,0},{9,1},... | collective-permute-start | bytes 294920 | tf_op jit(solution)/shard_map/ppermute | solution.py:74
  11.5 4.6 %collective-permute-start.3 = (bf16[192,256]{1,0:T(8,128)(2,1)S(1)}, bf16[192,256]{1,0:T(8,128)(2,1)S(1)}, u32[]{:S(2)}, u32[]{:S(2)}) collective-permute-start(bf16[192,256]{1,0:T(8,128)(2,1)S(1)} %collective-permute-done.refs_3_), channel_id=1, source_target_pairs={{0,4},{1,5},{2,6},{3,7},{4,0},{5,1},{6,2},{7,3},{8,12},{9,13},{10,... | collective-permute-start | bytes 294920 | tf_op jit(solution)/shard_map/ppermute | solution.py:74
  12.8 7.6 %collective-permute-start.9 = (bf16[384,256]{1,0:T(8,128)(2,1)S(1)}, bf16[384,256]{1,0:T(8,128)(2,1)S(1)}, u32[]{:S(2)}, u32[]{:S(2)}) collective-permute-start(bf16[384,256]{1,0:T(8,128)(2,1)S(1)} %pad_maximum_fusion.2), channel_id=1, source_target_pairs={{0,8},{1,9},{2,10},{3,11},{4,12},{5,13},{6,14},{7,15},{8,0},{9,1},... | collective-permute-start | bytes 589832 | tf_op jit(solution)/shard_map/ppermute | solution.py:74
  15.1 12.2 %copy-start.1 = (bf16[1,192,6144]{2,1,0:T(8,128)(2,1)S(1)}, bf16[1,192,6144]{2,1,0:T(8,128)(2,1)}, u32[]{:S(2)}) copy-start(bf16[1,192,6144]{2,1,0:T(8,128)(2,1)} %param.7) | copy-start | bytes 7077892
  15.1 12.2 %copy-start.3 = (bf16[768,256]{1,0:T(8,128)(2,1)S(1)}, bf16[768,256]{1,0:T(8,128)(2,1)}, u32[]{:S(2)}) copy-start(bf16[768,256]{1,0:T(8,128)(2,1)} %refs_0_.1) | copy-start | bytes 1179652
  16.1 4.6 %collective-permute-start.4 = (bf16[192,256]{1,0:T(8,128)(2,1)S(1)}, bf16[192,256]{1,0:T(8,128)(2,1)S(1)}, u32[]{:S(2)}, u32[]{:S(2)}) collective-permute-start(bf16[192,256]{1,0:T(8,128)(2,1)S(1)} %collective-permute-done.1.refs_4_), channel_id=1, source_target_pairs={{0,4},{1,5},{2,6},{3,7},{4,0},{5,1},{6,2},{7,3},{8,12},{9,13},{10,... | collective-permute-start | bytes 294920 | tf_op jit(solution)/shard_map/ppermute | solution.py:74
  17.8 9.3 %collective-permute-start.7 = (bf16[576,256]{1,0:T(8,128)(2,1)S(1)}, bf16[576,256]{1,0:T(8,128)(2,1)S(1)}, u32[]{:S(2)}, u32[]{:S(2)}) collective-permute-start(bf16[576,256]{1,0:T(8,128)(2,1)S(1)} %pad_maximum_fusion.1), channel_id=1, source_target_pairs={{0,2},{1,3},{2,0},{3,1},{4,6},{5,7},{6,4},{7,5},{8,10},{9,11},{10,... | collective-permute-start | bytes 884744 | tf_op jit(solution)/shard_map/ppermute | solution.py:74
  19.4 7.7 %collective-permute-start.6 = (bf16[384,256]{1,0:T(8,128)(2,1)S(1)}, bf16[384,256]{1,0:T(8,128)(2,1)S(1)}, u32[]{:S(2)}, u32[]{:S(2)}) collective-permute-start(bf16[384,256]{1,0:T(8,128)(2,1)S(1)} %collective-permute-done.2.refs_1_), channel_id=1, source_target_pairs={{0,8},{1,9},{2,10},{3,11},{4,12},{5,13},{6,14},{7,15},{8,0},{9,1},... | collective-permute-start | bytes 589832 | tf_op jit(solution)/shard_map/ppermute | solution.py:74
  20.7 6.4 %collective-permute-start.5 = (bf16[192,256]{1,0:T(8,128)(2,1)S(1)}, bf16[192,256]{1,0:T(8,128)(2,1)S(1)}, u32[]{:S(2)}, u32[]{:S(2)}) collective-permute-start(bf16[192,256]{1,0:T(8,128)(2,1)S(1)} %collective-permute-done.4.refs_0_), channel_id=1, source_target_pairs={{0,2},{1,3},{2,0},{3,1},{4,6},{5,7},{6,4},{7,5},{8,10},{9,11},{10,... | collective-permute-start | bytes 294920 | tf_op jit(solution)/shard_map/ppermute | solution.py:74
  22.3 5.0 %collective-permute-start.10 = (bf16[1344,256]{1,0:T(8,128)(2,1)S(1)}, bf16[1344,256]{1,0:T(8,128)(2,1)S(1)}, u32[]{:S(2)}, u32[]{:S(2)}) collective-permute-start(bf16[1344,256]{1,0:T(8,128)(2,1)S(1)} %constant_dynamic-update-slice_fusion), channel_id=1, source_target_pairs={{0,1},{1,0},{2,3},{3,2},{4,5},{5,4},{6,7},{7,6},{8,9},{9,8},{10,11... | collective-permute-start | bytes 2064392 | tf_op jit(solution)/shard_map/ppermute | solution.py:74
  27.2 2.2 %copy-start.4 = (s32[1,192]{1,0:T(1,128)S(1)}, s32[1,192]{1,0:T(1,128)}, u32[]{:S(2)}) copy-start(s32[1,192]{1,0:T(1,128)} %refs_7_.1) | copy-start | bytes 2308
  27.2 2.2 %collective-permute-start.8 = (bf16[1344,256]{1,0:T(8,128)(2,1)S(1)}, bf16[1344,256]{1,0:T(8,128)(2,1)S(1)}, u32[]{:S(2)}, u32[]{:S(2)}) collective-permute-start(bf16[1344,256]{1,0:T(8,128)(2,1)S(1)} %pad_maximum_fusion), channel_id=1, source_target_pairs={{0,1},{1,0},{2,3},{3,2},{4,5},{5,4},{6,7},{7,6},{8,9},{9,8},{10,11... | collective-permute-start | bytes 2064392 | tf_op jit(solution)/shard_map/ppermute | solution.py:74
  31.9 2.4 %collective-permute-start.15 = (bf16[1536,256]{1,0:T(8,128)(2,1)S(1)}, bf16[1536,256]{1,0:T(8,128)(2,1)S(1)}, u32[]{:S(2)}, u32[]{:S(2)}) collective-permute-start(bf16[1536,256]{1,0:T(8,128)(2,1)S(1)} %get-tuple-element.27), channel_id=1, source_target_pairs={{0,1},{1,0},{2,3},{3,2},{4,5},{5,4},{6,7},{7,6},{8,9},{9,8},{10,11... | collective-permute-start | bytes 2359304 | tf_op jit(solution)/shard_map/ppermute | solution.py:74
  32.7 5.5 %collective-permute-start.11 = (bf16[1536,256]{1,0:T(8,128)(2,1)S(1)}, bf16[1536,256]{1,0:T(8,128)(2,1)S(1)}, u32[]{:S(2)}, u32[]{:S(2)}) collective-permute-start(bf16[1536,256]{1,0:T(8,128)(2,1)S(1)} %terms.4), channel_id=1, source_target_pairs={{0,1},{1,0},{2,3},{3,2},{4,5},{5,4},{6,7},{7,6},{8,9},{9,8},{10,11... | collective-permute-start | bytes 2359304 | tf_op jit(solution)/shard_map/ppermute | solution.py:74
  34.4 8.7 %collective-permute-start.16 = (bf16[384,256]{1,0:T(8,128)(2,1)S(1)}, bf16[384,256]{1,0:T(8,128)(2,1)S(1)}, u32[]{:S(2)}, u32[]{:S(2)}) collective-permute-start(bf16[384,256]{1,0:T(8,128)(2,1)S(1)} %pad_maximum_fusion.6), channel_id=1, source_target_pairs={{0,6},{1,7},{2,4},{3,5},{4,2},{5,3},{6,0},{7,1},{8,14},{9,15},{10,... | collective-permute-start | bytes 589832 | tf_op jit(solution)/shard_map/ppermute | solution.py:74
  36.0 11.5 %collective-permute-start.17 = (bf16[384,256]{1,0:T(8,128)(2,1)S(1)}, bf16[384,256]{1,0:T(8,128)(2,1)S(1)}, u32[]{:S(2)}, u32[]{:S(2)}) collective-permute-start(bf16[384,256]{1,0:T(8,128)(2,1)S(1)} %pad_maximum_fusion.7), channel_id=1, source_target_pairs={{0,4},{1,5},{2,6},{3,7},{4,0},{5,1},{6,2},{7,3},{8,12},{9,13},{10,... | collective-permute-start | bytes 589832 | tf_op jit(solution)/shard_map/ppermute | solution.py:74
  37.6 9.9 %collective-permute-start.18 = (bf16[384,256]{1,0:T(8,128)(2,1)S(1)}, bf16[384,256]{1,0:T(8,128)(2,1)S(1)}, u32[]{:S(2)}, u32[]{:S(2)}) collective-permute-start(bf16[384,256]{1,0:T(8,128)(2,1)S(1)} %pad_maximum_fusion.8), channel_id=1, source_target_pairs={{0,2},{1,3},{2,0},{3,1},{4,6},{5,7},{6,4},{7,5},{8,10},{9,11},{10,... | collective-permute-start | bytes 589832 | tf_op jit(solution)/shard_map/ppermute | solution.py:74
  38.3 21.6 %copy-start.5 = (f32[192,256]{1,0:T(8,128)S(1)}, f32[192,256]{1,0:T(8,128)}, u32[]{:S(2)}) copy-start(f32[192,256]{1,0:T(8,128)} %param.11) | copy-start | bytes 589828
  38.3 21.6 %copy-start.6 = (f32[192,256]{1,0:T(8,128)S(1)}, f32[192,256]{1,0:T(8,128)}, u32[]{:S(2)}) copy-start(f32[192,256]{1,0:T(8,128)} %param.12) | copy-start | bytes 589828
  38.3 21.6 %copy-start.7 = (f32[192,256]{1,0:T(8,128)S(1)}, f32[192,256]{1,0:T(8,128)}, u32[]{:S(2)}) copy-start(f32[192,256]{1,0:T(8,128)} %param.13) | copy-start | bytes 589828
  38.4 13.3 %collective-permute-start.12 = (bf16[384,256]{1,0:T(8,128)(2,1)S(1)}, bf16[384,256]{1,0:T(8,128)(2,1)S(1)}, u32[]{:S(2)}, u32[]{:S(2)}) collective-permute-start(bf16[384,256]{1,0:T(8,128)(2,1)S(1)} %pad_maximum_fusion.3), channel_id=1, source_target_pairs={{0,6},{1,7},{2,4},{3,5},{4,2},{5,3},{6,0},{7,1},{8,14},{9,15},{10,... | collective-permute-start | bytes 589832 | tf_op jit(solution)/shard_map/ppermute | solution.py:74
  39.9 15.2 %collective-permute-start.13 = (bf16[384,256]{1,0:T(8,128)(2,1)S(1)}, bf16[384,256]{1,0:T(8,128)(2,1)S(1)}, u32[]{:S(2)}, u32[]{:S(2)}) collective-permute-start(bf16[384,256]{1,0:T(8,128)(2,1)S(1)} %pad_maximum_fusion.4), channel_id=1, source_target_pairs={{0,4},{1,5},{2,6},{3,7},{4,0},{5,1},{6,2},{7,3},{8,12},{9,13},{10,... | collective-permute-start | bytes 589832 | tf_op jit(solution)/shard_map/ppermute | solution.py:74
  43.2 11.9 %collective-permute-start.14 = (bf16[384,256]{1,0:T(8,128)(2,1)S(1)}, bf16[384,256]{1,0:T(8,128)(2,1)S(1)}, u32[]{:S(2)}, u32[]{:S(2)}) collective-permute-start(bf16[384,256]{1,0:T(8,128)(2,1)S(1)} %pad_maximum_fusion.5), channel_id=1, source_target_pairs={{0,2},{1,3},{2,0},{3,1},{4,6},{5,7},{6,4},{7,5},{8,10},{9,11},{10,... | collective-permute-start | bytes 589832 | tf_op jit(solution)/shard_map/ppermute | solution.py:74
  47.6 10.3 %collective-permute-start.19 = (bf16[192,256]{1,0:T(8,128)(2,1)S(1)}, bf16[192,256]{1,0:T(8,128)(2,1)S(1)}, u32[]{:S(2)}, u32[]{:S(2)}) collective-permute-start(bf16[192,256]{1,0:T(8,128)(2,1)S(1)} %get-tuple-element.32), channel_id=1, source_target_pairs={{0,16},{1,17},{2,18},{3,19},{4,20},{5,21},{6,22},{7,23},{8,24},{9,... | collective-permute-start | bytes 294920 | tf_op jit(solution)/shard_map/ppermute | solution.py:74
  51.0 6.9 %collective-permute-start.20 = (bf16[192,256]{1,0:T(8,128)(2,1)S(1)}, bf16[192,256]{1,0:T(8,128)(2,1)S(1)}, u32[]{:S(2)}, u32[]{:S(2)}) collective-permute-start(bf16[192,256]{1,0:T(8,128)(2,1)S(1)} %get-tuple-element.33), channel_id=1, source_target_pairs={{0,24},{1,25},{2,26},{3,27},{4,28},{5,29},{6,30},{7,31},{8,16},{9,... | collective-permute-start | bytes 294920 | tf_op jit(solution)/shard_map/ppermute | solution.py:74
  55.2 4.7 %collective-permute-start.21 = (bf16[192,256]{1,0:T(8,128)(2,1)S(1)}, bf16[192,256]{1,0:T(8,128)(2,1)S(1)}, u32[]{:S(2)}, u32[]{:S(2)}) collective-permute-start(bf16[192,256]{1,0:T(8,128)(2,1)S(1)} %fusion.4), channel_id=1, source_target_pairs={{0,8},{1,9},{2,10},{3,11},{4,12},{5,13},{6,14},{7,15},{8,0},{9,1},... | collective-permute-start | bytes 294920 | tf_op jit(solution)/shard_map/ppermute | solution.py:74

commit v4 on v3

--- a/solution.py
+++ b/solution.py
@@ -17,8 +17,6 @@
 
 AXES = ("grp", "rep")
 MIB = 1024 * 1024
-FAR = (2, 3)
-NEAR = (1, 0)
 
 
 def adam(gradient, primary, first_moment, second_moment):
@@ -137,10 +135,10 @@
     front[...], back[...] = project(refs[:count], places, acts, cots, weights, rows, head)
 
 
-def attend_kernel(places, rows, head, grad_scale, *refs):
+def attend_kernel(places, blocks, rows, head, grad_scale, *refs):
     count = len(places)
     acts, cots, docs, acts_t, cots_t, front_ref, back_ref = refs[count : count + 7]
-    far_ref, left_ref, right_ref, weights = refs[count + 7 :]
+    sent_ref, left_ref, right_ref, weights = refs[count + 7 :]
     front, back = project(refs[:count], places, acts, cots, weights, rows, head)
     projected = (front_ref[...] + front).astype(jnp.bfloat16)
     back_context = (back_ref[...] + back).astype(jnp.bfloat16)
@@ -169,19 +167,19 @@
     right = jnp.concatenate([none, none, none, context], axis=1)
     left_ref[...] = left
     right_ref[...] = right
-    write_terms(acts_t, cots_t, left, right, far_ref, FAR, 1, rows, grad_scale)
-
-
-def write_terms(acts_t, cots_t, left, right, out_ref, kzs, kc, rows, grad_scale):
-    for index, (kz, kx, ky) in enumerate((kz, kx, ky) for kz in kzs for kx in (0, 1) for ky in (0, 1)):
-        start = block_start(kz, kx, ky, kc, rows)
+    write_terms(acts_t, cots_t, left, right, sent_ref, blocks, 1, rows, grad_scale)
+
+
+def write_terms(acts_t, cots_t, left, right, out_ref, blocks, kc, rows, grad_scale):
+    for index, block in enumerate(blocks):
+        start = block_start(*block, kc, rows)
         term = fdot(acts_t[pl.ds(start, rows), :], left, MM)
         term += fdot(cots_t[pl.ds(start, rows), :], right, MM)
         out_ref[index * rows : (index + 1) * rows, :] = (term * grad_scale).astype(out_ref.dtype)
 
 
-def terms_kernel(kzs, kc, rows, grad_scale, acts_t, cots_t, left_ref, right_ref, out_ref):
-    write_terms(acts_t, cots_t, left_ref[...], right_ref[...], out_ref, kzs, kc, rows, grad_scale)
+def terms_kernel(blocks, kc, rows, grad_scale, acts_t, cots_t, left_ref, right_ref, out_ref):
+    write_terms(acts_t, cots_t, left_ref[...], right_ref[...], out_ref, blocks, kc, rows, grad_scale)
 
 
 def vmem(count):
@@ -235,17 +233,20 @@
     return [(weight_copy, [None]), *early], late, first, second
 
 
-def plane_sum(mine, received, kzs, rows):
-    def block(kz, kx, ky):
-        start = ((kzs.index(kz) * 2 + kx) * 2 + ky) * rows
-        return mine[start : start + rows] + received[start : start + rows].astype(jnp.float32)
-
-    totals = [block(kz, 0, 0) for kz in kzs]
-    for kx, ky in ((1, 1), (1, 0), (0, 1)):
-        came = hop(join(*[block(kz, kx, ky).astype(jnp.bfloat16) for kz in kzs]), 0, kx, ky, 0)
-        for index in range(len(kzs)):
-            totals[index] += came[index * rows : (index + 1) * rows].astype(jnp.float32)
-    return totals
+SIDES = ((1, 1), (1, 0), (0, 1))
+
+
+def cut(array, count):
+    size = array.shape[0] // count
+    return [array[index * size : (index + 1) * size] for index in range(count)]
+
+
+def add(*parts):
+    return sum(part.astype(jnp.float32) for part in parts)
+
+
+def low(array):
+    return array.astype(jnp.bfloat16)
 
 
 def block_body(activations, cotangent, documents, weight_copy, primary, first_moment, second_moment):
@@ -274,31 +275,42 @@
         scratch=[pltpu.VMEM((24 * rows, columns), jnp.bfloat16)],
         flops=flops,
     )
-    far, left, right = kernel_call(
-        functools.partial(attend_kernel, [place for _, place in late], rows, head, grad_scale),
-        [bfloat((8 * rows, columns))] + [bfloat((tokens, columns))] * 2,
+    far = [(kz, kx, ky) for kx, ky in (*SIDES, (0, 0)) for kz in (2, 3)]
+    near = [(kz, kx, ky) for kz in (1, 0) for kx, ky in (*SIDES, (0, 0))]
+    sent, left, right = kernel_call(
+        functools.partial(attend_kernel, [place for _, place in late], far[:2], rows, head, grad_scale),
+        [bfloat((2 * rows, columns))] + [bfloat((tokens, columns))] * 2,
         "attend",
         (*[piece for piece, _ in late], acts, cots, documents, acts_t, cots_t, front, back),
         scratch=[pltpu.VMEM((16 * rows, columns), jnp.bfloat16)],
         flops=flops,
     )
 
-    def terms(kzs, kc, dtype):
+    def terms(blocks, kc, dtype):
         return kernel_call(
-            functools.partial(terms_kernel, kzs, kc, rows, grad_scale),
-            [dtype((4 * len(kzs) * rows, columns))],
+            functools.partial(terms_kernel, blocks, kc, rows, grad_scale),
+            [dtype((len(blocks) * rows, columns))],
             "terms",
             (acts_t, cots_t, left, right),
-            flops=flops * len(kzs) // 8,
+            flops=flops * len(blocks) // 32,
         )[0]
 
-    totals = {}
-    for kzs, sent in ((FAR, far), (NEAR, terms(NEAR, 1, bfloat))):
-        received = hop(sent, 0, 0, 0, 1)
-        totals.update(zip(kzs, plane_sum(terms(kzs, 0, float32), received, kzs, rows)))
-    gradient = totals[0]
-    for kz in (2, 3, 1):
-        gradient += hop(totals[kz].astype(jnp.bfloat16), kz, 0, 0, 0).astype(jnp.float32)
+    def other_core(value):
+        return hop(value, 0, 0, 0, 1)
+
+    sent = other_core(sent)
+    rest = other_core(terms(far[2:], 1, bfloat))
+    near_other = other_core(terms(near, 1, bfloat))
+    mine = terms(far, 0, float32)
+    diagonal = add(mine[: 2 * rows], sent)
+    along_x, along_y, total = cut(add(mine[2 * rows :], rest), 3)
+    total = add(total, *[hop(low(part), 0, *side, 0) for part, side in zip((diagonal, along_x, along_y), SIDES)])
+    total_2, total_3 = cut(total, 2)
+    one, zero = cut(add(terms(near, 0, float32), near_other), 2)
+    *parts, gradient = cut(add(zero, hop(low(one), 1, 0, 0, 0)), 4)
+    arrived = [hop(low(part), 0, *side, 0) for part, side in zip(parts, SIDES)]
+    arrived += [hop(low(total_2), 2, 0, 0, 0), hop(low(total_3), 3, 0, 0, 0)]
+    gradient = add(gradient, *arrived)
     primary_new, first_new, second_new = adam(gradient, primary, first_moment, second_moment)
     copy_new = lax.all_gather(primary_new.astype(jnp.bfloat16), "rep", axis=0, tiled=True)
     return primary_new, first_new, second_new, copy_new

time: 68.3 us -> 66.6 us (0.975)
  starting transfers between devices: 28 us -> 27 us
  waiting for transfers between devices: 20.6 us -> 19.9 us
    ppermute x22 -> x23, starting transfers between devices: 28 us -> 27 us  [hop(): return lax.ppermute(value, AXES, [(i, i ^ offset) for i in range(32)])]
    ppermute x22 -> x23, waiting for transfers between devices: 20.6 us -> 19.9 us  [hop(): return lax.ppermute(value, AXES, [(i, i ^ offset) for i in range(32)])]
    pallas_call x7 -> x8, Pallas kernels: 7.1 us -> 7.23 us  [kernel_call(): pl.pallas_call(body, out_shape=outs, in_specs=vmem(len(args)), out_specs=...]
  transfers between devices with their start and end apart: 22 -> 23, of which waited for: 12 -> 11; matrix products, arithmetic and copies ran while one was open for 1% -> 1% of each run, Pallas kernels for 7% -> 7%
where the time goes in v4:
time: 66.6 us; the launch traced here: 66.4 us
  starting transfers between devices  27 us (41%)
  waiting for transfers between devices  19.9 us (30%)
  Pallas kernels  7.23 us (11%)
  blocking collectives  6.13 us (9%)
  local copies, waits for them, and re-layouts  3.57 us (5%)
  other arithmetic  1.65 us (2%)
  between operations  0.92 us (1%)
    ppermute x23, starting transfers between devices, hop(): return lax.ppermute(value, AXES, [(i, i ^ offset) for i in range(32)])  27 us
    ppermute x23, waiting for transfers between devices, hop(): return lax.ppermute(value, AXES, [(i, i ^ offset) for i in range(32)])  19.9 us
    pallas_call x8, Pallas kernels, kernel_call(): pl.pallas_call(body, out_shape=outs, in_specs=vmem(len(args)), out_specs=...  7.23 us
    all_gather x1, blocking collectives, block_body(): lax.all_gather(primary_new.astype(jnp.bfloat16), 'rep', axis=0, tiled=True)  6.13 us
    unnamed x21, local copies, waits for them, and re-layouts  2.5 us
  transfers between devices with their start and end apart: 23, of which 11 were waited for; matrix products, arithmetic and copies ran while one was open for 1% of the time, Pallas kernels for 7%

profile of v4, /device:TPU:0, one launch (start us, length us, event | category | flops | bytes accessed | tf_op | source)
XLA Modules:
  0.0 66.4 jit_solution(8847303744188034840)
XLA Ops:
  0.6 1.0 %constant_dynamic-slice_fusion = (bf16[192,256]{1,0:T(8,128)(2,1)S(1)}, bf16[192,256]{1,0:T(8,128)(2,1)S(1)}) fusion(bf16[768,256]{1,0:T(8,128)(2,1)} %refs_0_.1, s32[]{:T(128)S(6)} %select_n.7, s32[]{:T(128)S(6)} %select_n.6), kind=kLoop, calls=%fused_computation.27 | loop fusion | bytes 393224 | tf_op jit(solution)/shard_map/dynamic_slice | solution.py:205
  1.6 4.1 %collective-permute-start = (bf16[192,256]{1,0:T(8,128)(2,1)S(1)}, bf16[192,256]{1,0:T(8,128)(2,1)S(1)}, u32[]{:S(2)}, u32[]{:S(2)}) collective-permute-start(bf16[192,256]{1,0:T(8,128)(2,1)S(1)} %get-tuple-element.42), channel_id=1, source_target_pairs={{0,16},{1,17},{2,18},{3,19},{4,20},{5,21},{6,22},{7,23},{8,24},{9,... | collective-permute-start | bytes 294920 | tf_op jit(solution)/shard_map/ppermute | solution.py:72
  5.7 1.6 %collective-permute-start.2 = (bf16[384,256]{1,0:T(8,128)(2,1)S(1)}, bf16[384,256]{1,0:T(8,128)(2,1)S(1)}, u32[]{:S(2)}, u32[]{:S(2)}) collective-permute-start(bf16[384,256]{1,0:T(8,128)(2,1)S(1)} %pad_maximum_fusion.2), channel_id=1, source_target_pairs={{0,4},{1,5},{2,6},{3,7},{4,0},{5,1},{6,2},{7,3},{8,12},{9,13},{10,... | collective-permute-start | bytes 589832 | tf_op jit(solution)/shard_map/ppermute | solution.py:72
  7.3 1.7 %copy-done = bf16[1,192,6144]{2,1,0:T(8,128)(2,1)S(1)} copy-done((bf16[1,192,6144]{2,1,0:T(8,128)(2,1)S(1)}, bf16[1,192,6144]{2,1,0:T(8,128)(2,1)}, u32[]{:S(2)}) %copy-start) | copy-done | bytes 2359320
  8.9 0.9 %turn.2.refs_8_.acts_t = bf16[6144,192]{1,0:T(8,128)(2,1)S(1)} custom-call(bf16[192,6144]{1,0:T(8,128)(2,1)S(1)} %bitcast.2), custom_call_target="tpu_custom_call" | custom-call | flops 603979776 | bytes 4194304 | tf_op jit(solution)/shard_map/turn/pallas_call | solution.py:190
  9.8 0.8 %collective-permute-done.refs_3_ = bf16[192,256]{1,0:T(8,128)(2,1)S(1)} collective-permute-done((bf16[192,256]{1,0:T(8,128)(2,1)S(1)}, bf16[192,256]{1,0:T(8,128)(2,1)S(1)}, u32[]{:S(2)}, u32[]{:S(2)}) %collective-permute-start) | collective-permute-done | bytes 98336 | tf_op jit(solution)/shard_map/ppermute | solution.py:72
  10.6 0.9 %collective-permute-start.1 = (bf16[192,256]{1,0:T(8,128)(2,1)S(1)}, bf16[192,256]{1,0:T(8,128)(2,1)S(1)}, u32[]{:S(2)}, u32[]{:S(2)}) collective-permute-start(bf16[192,256]{1,0:T(8,128)(2,1)S(1)} %collective-permute-done.refs_3_), channel_id=1, source_target_pairs={{0,8},{1,9},{2,10},{3,11},{4,12},{5,13},{6,14},{7,15},{8,0},{9,1},... | collective-permute-start | bytes 294920 | tf_op jit(solution)/shard_map/ppermute | solution.py:72
  11.5 1.3 %collective-permute-start.3 = (bf16[192,256]{1,0:T(8,128)(2,1)S(1)}, bf16[192,256]{1,0:T(8,128)(2,1)S(1)}, u32[]{:S(2)}, u32[]{:S(2)}) collective-permute-start(bf16[192,256]{1,0:T(8,128)(2,1)S(1)} %collective-permute-done.refs_3_), channel_id=1, source_target_pairs={{0,4},{1,5},{2,6},{3,7},{4,0},{5,1},{6,2},{7,3},{8,12},{9,13},{10,... | collective-permute-start | bytes 294920 | tf_op jit(solution)/shard_map/ppermute | solution.py:72
  12.8 1.4 %collective-permute-start.9 = (bf16[384,256]{1,0:T(8,128)(2,1)S(1)}, bf16[384,256]{1,0:T(8,128)(2,1)S(1)}, u32[]{:S(2)}, u32[]{:S(2)}) collective-permute-start(bf16[384,256]{1,0:T(8,128)(2,1)S(1)} %pad_maximum_fusion.2), channel_id=1, source_target_pairs={{0,8},{1,9},{2,10},{3,11},{4,12},{5,13},{6,14},{7,15},{8,0},{9,1},... | collective-permute-start | bytes 589832 | tf_op jit(solution)/shard_map/ppermute | solution.py:72
  14.2 0.9 %turn.3.refs_9_.cots_t = bf16[6144,192]{1,0:T(8,128)(2,1)S(1)} custom-call(bf16[192,6144]{1,0:T(8,128)(2,1)S(1)} %bitcast.5), custom_call_target="tpu_custom_call" | custom-call | flops 603979776 | bytes 4194304 | tf_op jit(solution)/shard_map/turn/pallas_call | solution.py:190
  15.1 0.0 copy-start.1
  15.1 0.0 copy-start.3
  15.1 0.5 collective-permute-done.1.refs_4_
  15.6 0.5 collective-permute-done.3.refs_5_
  16.1 1.7 %collective-permute-start.4 = (bf16[192,256]{1,0:T(8,128)(2,1)S(1)}, bf16[192,256]{1,0:T(8,128)(2,1)S(1)}, u32[]{:S(2)}, u32[]{:S(2)}) collective-permute-start(bf16[192,256]{1,0:T(8,128)(2,1)S(1)} %collective-permute-done.1.refs_4_), channel_id=1, source_target_pairs={{0,4},{1,5},{2,6},{3,7},{4,0},{5,1},{6,2},{7,3},{8,12},{9,13},{10,... | collective-permute-start | bytes 294920 | tf_op jit(solution)/shard_map/ppermute | solution.py:72
  17.8 1.6 %collective-permute-start.7 = (bf16[576,256]{1,0:T(8,128)(2,1)S(1)}, bf16[576,256]{1,0:T(8,128)(2,1)S(1)}, u32[]{:S(2)}, u32[]{:S(2)}) collective-permute-start(bf16[576,256]{1,0:T(8,128)(2,1)S(1)} %pad_maximum_fusion.1), channel_id=1, source_target_pairs={{0,2},{1,3},{2,0},{3,1},{4,6},{5,7},{6,4},{7,5},{8,10},{9,11},{10,... | collective-permute-start | bytes 884744 | tf_op jit(solution)/shard_map/ppermute | solution.py:72
  19.4 1.0 %collective-permute-start.6 = (bf16[384,256]{1,0:T(8,128)(2,1)S(1)}, bf16[384,256]{1,0:T(8,128)(2,1)S(1)}, u32[]{:S(2)}, u32[]{:S(2)}) collective-permute-start(bf16[384,256]{1,0:T(8,128)(2,1)S(1)} %collective-permute-done.2.refs_1_), channel_id=1, source_target_pairs={{0,8},{1,9},{2,10},{3,11},{4,12},{5,13},{6,14},{7,15},{8,0},{9,1},... | collective-permute-start | bytes 589832 | tf_op jit(solution)/shard_map/ppermute | solution.py:72
  20.4 0.0 collective-permute-done.9.refs_2_
  20.5 0.2 collective-permute-done.4.refs_0_
  20.7 1.5 %collective-permute-start.5 = (bf16[192,256]{1,0:T(8,128)(2,1)S(1)}, bf16[192,256]{1,0:T(8,128)(2,1)S(1)}, u32[]{:S(2)}, u32[]{:S(2)}) collective-permute-start(bf16[192,256]{1,0:T(8,128)(2,1)S(1)} %collective-permute-done.4.refs_0_), channel_id=1, source_target_pairs={{0,2},{1,3},{2,0},{3,1},{4,6},{5,7},{6,4},{7,5},{8,10},{9,11},{10,... | collective-permute-start | bytes 294920 | tf_op jit(solution)/shard_map/ppermute | solution.py:72
  22.3 0.1 collective-permute-start.10
  22.3 4.8 %collective-permute-done.5.refs_3_ = bf16[192,256]{1,0:T(8,128)(2,1)S(1)} collective-permute-done((bf16[192,256]{1,0:T(8,128)(2,1)S(1)}, bf16[192,256]{1,0:T(8,128)(2,1)S(1)}, u32[]{:S(2)}, u32[]{:S(2)}) %collective-permute-start.5) | collective-permute-done | bytes 98336 | tf_op jit(solution)/shard_map/ppermute | solution.py:72
  27.1 0.0 collective-permute-done.6.refs_1_
  27.2 0.0 collective-permute-done.7.refs_2_
  27.2 0.0 copy-start.4
  27.2 0.1 collective-permute-start.8
  27.3 0.0 collective-permute-done.10.refs_6_
  27.3 1.2 %early.1 = (f32[192,192]{1,0:T(8,128)S(1)}, f32[192,64]{1,0:T(8,128)S(1)}) custom-call(bf16[768,256]{1,0:T(8,128)(2,1)S(1)} %copy-done.3, bf16[384,256]{1,0:T(8,128)(2,1)S(1)} %collective-permute-done.2.refs_1_, bf16[384,256]{1,0:T(8,128)(2,1)S(1)} %collective-permute-done.9.refs_2_, bf16[192,256]{1,0:T(8,128)(2,1)S(1)} %collective-permute-done.refs_3_, ...), custom_call_target="tpu_custom_call" | custom-call | flops 1207959552 | bytes 4194304 | tf_op jit(solution)/shard_map/early/pallas_call | solution.py:190
  28.5 0.9 %collective-permute-done.8.refs_4_ = bf16[1344,256]{1,0:T(8,128)(2,1)S(1)} collective-permute-done((bf16[1344,256]{1,0:T(8,128)(2,1)S(1)}, bf16[1344,256]{1,0:T(8,128)(2,1)S(1)}, u32[]{:S(2)}, u32[]{:S(2)}) %collective-permute-start.8) | collective-permute-done | bytes 688160 | tf_op jit(solution)/shard_map/ppermute | solution.py:72
  29.4 2.2 %attend.1 = (bf16[384,256]{1,0:T(8,128)(2,1)S(1)}, bf16[192,256]{1,0:T(8,128)(2,1)S(1)}, bf16[192,256]{1,0:T(8,128)(2,1)S(1)}) custom-call(bf16[192,256]{1,0:T(8,128)(2,1)S(1)} %collective-permute-done.4.refs_0_, bf16[384,256]{1,0:T(8,128)(2,1)S(1)} %collective-permute-done.6.refs_1_, bf16[576,256]{1,0:T(8,128)(2,1)S(1)} %collective-permute-done.7.refs_2_, ...), custom_call_target="tpu_custom_call" | custom-call | flops 1207959552 | bytes 4194304 | tf_op jit(solution)/shard_map/attend/pallas_call | solution.py:190
  31.6 0.5 terms.7
  32.1 0.2 collective-permute-start.16
  32.3 0.4 collective-permute-start.17
  32.6 0.6 terms.5
  33.2 0.2 collective-permute-start.11
  33.4 0.6 terms.4
  34.0 0.6 terms.6
  34.5 0.0 collective-permute-done.17
  34.5 0.1 fusion
  34.6 1.6 %collective-permute-start.18 = (bf16[384,256]{1,0:T(8,128)(2,1)S(1)}, bf16[384,256]{1,0:T(8,128)(2,1)S(1)}, u32[]{:S(2)}, u32[]{:S(2)}) collective-permute-start(bf16[384,256]{1,0:T(8,128)(2,1)S(1)} %fusion), channel_id=1, source_target_pairs={{0,6},{1,7},{2,4},{3,5},{4,2},{5,3},{6,0},{7,1},{8,14},{9,15},{10,... | collective-permute-start | bytes 589832 | tf_op jit(solution)/shard_map/ppermute | solution.py:72
  36.2 0.0 collective-permute-done.16
  36.2 0.2 fusion.12
  36.4 1.6 %collective-permute-start.19 = (bf16[384,256]{1,0:T(8,128)(2,1)S(1)}, bf16[384,256]{1,0:T(8,128)(2,1)S(1)}, u32[]{:S(2)}, u32[]{:S(2)}) collective-permute-start(bf16[384,256]{1,0:T(8,128)(2,1)S(1)} %get-tuple-element.36), channel_id=1, source_target_pairs={{0,4},{1,5},{2,6},{3,7},{4,0},{5,1},{6,2},{7,3},{8,12},{9,13},{10,... | collective-permute-start | bytes 589832 | tf_op jit(solution)/shard_map/ppermute | solution.py:72
  37.9 0.5 collective-permute-start.20
  38.5 0.2 convert_add_fusion
  38.7 0.5 collective-permute-start.12
  39.2 4.2 %collective-permute-done.18 = bf16[384,256]{1,0:T(8,128)(2,1)S(1)} collective-permute-done((bf16[384,256]{1,0:T(8,128)(2,1)S(1)}, bf16[384,256]{1,0:T(8,128)(2,1)S(1)}, u32[]{:S(2)}, u32[]{:S(2)}) %collective-permute-start.18) | collective-permute-done | bytes 196640 | tf_op jit(solution)/shard_map/ppermute | solution.py:72
  43.3 3.7 %collective-permute-done.19 = bf16[384,256]{1,0:T(8,128)(2,1)S(1)} collective-permute-done((bf16[384,256]{1,0:T(8,128)(2,1)S(1)}, bf16[384,256]{1,0:T(8,128)(2,1)S(1)}, u32[]{:S(2)}, u32[]{:S(2)}) %collective-permute-start.19) | collective-permute-done | bytes 196640 | tf_op jit(solution)/shard_map/ppermute | solution.py:72
  47.1 0.1 fusion.3
  47.2 0.0 copy-start.5
  47.2 0.0 copy-start.6
  47.2 0.0 copy-start.7
  47.2 3.4 %collective-permute-start.21 = (bf16[192,256]{1,0:T(8,128)(2,1)S(1)}, bf16[192,256]{1,0:T(8,128)(2,1)S(1)}, u32[]{:S(2)}, u32[]{:S(2)}) collective-permute-start(bf16[192,256]{1,0:T(8,128)(2,1)S(1)} %get-tuple-element.43), channel_id=1, source_target_pairs={{0,16},{1,17},{2,18},{3,19},{4,20},{5,21},{6,22},{7,23},{8,24},{9,... | collective-permute-start | bytes 294920 | tf_op jit(solution)/shard_map/ppermute | solution.py:72
  50.6 0.0 collective-permute-start.22
  50.6 0.1 fusion.11
  50.8 1.4 %collective-permute-start.13 = (bf16[192,256]{1,0:T(8,128)(2,1)S(1)}, bf16[192,256]{1,0:T(8,128)(2,1)S(1)}, u32[]{:S(2)}, u32[]{:S(2)}) collective-permute-start(bf16[192,256]{1,0:T(8,128)(2,1)S(1)} %get-tuple-element.38), channel_id=1, source_target_pairs={{0,6},{1,7},{2,4},{3,5},{4,2},{5,3},{6,0},{7,1},{8,14},{9,15},{10,... | collective-permute-start | bytes 294920 | tf_op jit(solution)/shard_map/ppermute | solution.py:72
  52.1 1.6 %collective-permute-start.14 = (bf16[192,256]{1,0:T(8,128)(2,1)S(1)}, bf16[192,256]{1,0:T(8,128)(2,1)S(1)}, u32[]{:S(2)}, u32[]{:S(2)}) collective-permute-start(bf16[192,256]{1,0:T(8,128)(2,1)S(1)} %get-tuple-element.40), channel_id=1, source_target_pairs={{0,4},{1,5},{2,6},{3,7},{4,0},{5,1},{6,2},{7,3},{8,12},{9,13},{10,... | collective-permute-start | bytes 294920 | tf_op jit(solution)/shard_map/ppermute | solution.py:72
  53.7 0.6 collective-permute-start.15
  54.3 3.7 %collective-permute-done.21 = bf16[192,256]{1,0:T(8,128)(2,1)S(1)} collective-permute-done((bf16[192,256]{1,0:T(8,128)(2,1)S(1)}, bf16[192,256]{1,0:T(8,128)(2,1)S(1)}, u32[]{:S(2)}, u32[]{:S(2)}) %collective-permute-start.21) | collective-permute-done | bytes 98336 | tf_op jit(solution)/shard_map/ppermute | solution.py:72
  58.0 0.2 collective-permute-done.14
  58.2 0.3 collective-permute-done.15
  58.6 1.0 %fusion.9 = (bf16[192,256]{1,0:T(8,128)(2,1)S(1)}, f32[192,256]{1,0:T(8,128)}, f32[192,256]{1,0:T(8,128)}, f32[192,256]{1,0:T(8,128)}) fusion(f32[192,256]{1,0:T(8,128)S(1)} %copy-done.5, f32[192,256]{1,0:T(8,128)S(1)} %copy-done.6, f32[192,256]{1,0:T(8,128)S(1)} %copy-done.7, bf16[192,256]{1,0:T(8,128)(2,1)S(1)} %collective-permute-done.22, ...), kind=kLoop, calls=%fused_computation.29 | loop fusion | flops 1277952 | bytes 1966080 | tf_op jit(solution)/shard_map/convert_element_type | solution.py:315
  59.5 6.1 %all_gather.3 = bf16[768,256]{1,0:T(8,128)(2,1)S(1)} all-gather(bf16[192,256]{1,0:T(8,128)(2,1)S(1)} %get-tuple-element.28), channel_id=1, replica_groups=mesh['grp'=8,'rep'=4] {'rep'}, dimensions={0}, use_global_device_ids=true | all-gather | bytes 491520 | tf_op jit(solution)/shard_map/all_gather | solution.py:315
  65.7 0.7 %copy.16 = bf16[768,256]{1,0:T(8,128)(2,1)} copy(bf16[768,256]{1,0:T(8,128)(2,1)S(1)} %all_gather.3) | data formatting | bytes 786432
  (27 shorter events, 0.3 us)
Async XLA Ops:
  1.6 9.0 %collective-permute-start = (bf16[192,256]{1,0:T(8,128)(2,1)S(1)}, bf16[192,256]{1,0:T(8,128)(2,1)S(1)}, u32[]{:S(2)}, u32[]{:S(2)}) collective-permute-start(bf16[192,256]{1,0:T(8,128)(2,1)S(1)} %get-tuple-element.42), channel_id=1, source_target_pairs={{0,16},{1,17},{2,18},{3,19},{4,20},{5,21},{6,22},{7,23},{8,24},{9,... | collective-permute-start | bytes 294920 | tf_op jit(solution)/shard_map/ppermute | solution.py:72
  5.7 9.4 %collective-permute-start.2 = (bf16[384,256]{1,0:T(8,128)(2,1)S(1)}, bf16[384,256]{1,0:T(8,128)(2,1)S(1)}, u32[]{:S(2)}, u32[]{:S(2)}) collective-permute-start(bf16[384,256]{1,0:T(8,128)(2,1)S(1)} %pad_maximum_fusion.2), channel_id=1, source_target_pairs={{0,4},{1,5},{2,6},{3,7},{4,0},{5,1},{6,2},{7,3},{8,12},{9,13},{10,... | collective-permute-start | bytes 589832 | tf_op jit(solution)/shard_map/ppermute | solution.py:72
  7.3 1.7 %copy-start = (bf16[1,192,6144]{2,1,0:T(8,128)(2,1)S(1)}, bf16[1,192,6144]{2,1,0:T(8,128)(2,1)}, u32[]{:S(2)}) copy-start(bf16[1,192,6144]{2,1,0:T(8,128)(2,1)} %param.7) | copy-start | bytes 7077892
  8.9 5.2 %copy-start.2 = (bf16[1,192,6144]{2,1,0:T(8,128)(2,1)S(1)}, bf16[1,192,6144]{2,1,0:T(8,128)(2,1)}, u32[]{:S(2)}) copy-start(bf16[1,192,6144]{2,1,0:T(8,128)(2,1)} %param.8) | copy-start | bytes 7077892
  10.6 5.0 %collective-permute-start.1 = (bf16[192,256]{1,0:T(8,128)(2,1)S(1)}, bf16[192,256]{1,0:T(8,128)(2,1)S(1)}, u32[]{:S(2)}, u32[]{:S(2)}) collective-permute-start(bf16[192,256]{1,0:T(8,128)(2,1)S(1)} %collective-permute-done.refs_3_), channel_id=1, source_target_pairs={{0,8},{1,9},{2,10},{3,11},{4,12},{5,13},{6,14},{7,15},{8,0},{9,1},... | collective-permute-start | bytes 294920 | tf_op jit(solution)/shard_map/ppermute | solution.py:72
  11.5 4.6 %collective-permute-start.3 = (bf16[192,256]{1,0:T(8,128)(2,1)S(1)}, bf16[192,256]{1,0:T(8,128)(2,1)S(1)}, u32[]{:S(2)}, u32[]{:S(2)}) collective-permute-start(bf16[192,256]{1,0:T(8,128)(2,1)S(1)} %collective-permute-done.refs_3_), channel_id=1, source_target_pairs={{0,4},{1,5},{2,6},{3,7},{4,0},{5,1},{6,2},{7,3},{8,12},{9,13},{10,... | collective-permute-start | bytes 294920 | tf_op jit(solution)/shard_map/ppermute | solution.py:72
  12.8 7.6 %collective-permute-start.9 = (bf16[384,256]{1,0:T(8,128)(2,1)S(1)}, bf16[384,256]{1,0:T(8,128)(2,1)S(1)}, u32[]{:S(2)}, u32[]{:S(2)}) collective-permute-start(bf16[384,256]{1,0:T(8,128)(2,1)S(1)} %pad_maximum_fusion.2), channel_id=1, source_target_pairs={{0,8},{1,9},{2,10},{3,11},{4,12},{5,13},{6,14},{7,15},{8,0},{9,1},... | collective-permute-start | bytes 589832 | tf_op jit(solution)/shard_map/ppermute | solution.py:72
  15.1 12.2 %copy-start.1 = (bf16[1,192,6144]{2,1,0:T(8,128)(2,1)S(1)}, bf16[1,192,6144]{2,1,0:T(8,128)(2,1)}, u32[]{:S(2)}) copy-start(bf16[1,192,6144]{2,1,0:T(8,128)(2,1)} %param.7) | copy-start | bytes 7077892
  15.1 12.2 %copy-start.3 = (bf16[768,256]{1,0:T(8,128)(2,1)S(1)}, bf16[768,256]{1,0:T(8,128)(2,1)}, u32[]{:S(2)}) copy-start(bf16[768,256]{1,0:T(8,128)(2,1)} %refs_0_.1) | copy-start | bytes 1179652
  16.1 4.6 %collective-permute-start.4 = (bf16[192,256]{1,0:T(8,128)(2,1)S(1)}, bf16[192,256]{1,0:T(8,128)(2,1)S(1)}, u32[]{:S(2)}, u32[]{:S(2)}) collective-permute-start(bf16[192,256]{1,0:T(8,128)(2,1)S(1)} %collective-permute-done.1.refs_4_), channel_id=1, source_target_pairs={{0,4},{1,5},{2,6},{3,7},{4,0},{5,1},{6,2},{7,3},{8,12},{9,13},{10,... | collective-permute-start | bytes 294920 | tf_op jit(solution)/shard_map/ppermute | solution.py:72
  17.8 9.3 %collective-permute-start.7 = (bf16[576,256]{1,0:T(8,128)(2,1)S(1)}, bf16[576,256]{1,0:T(8,128)(2,1)S(1)}, u32[]{:S(2)}, u32[]{:S(2)}) collective-permute-start(bf16[576,256]{1,0:T(8,128)(2,1)S(1)} %pad_maximum_fusion.1), channel_id=1, source_target_pairs={{0,2},{1,3},{2,0},{3,1},{4,6},{5,7},{6,4},{7,5},{8,10},{9,11},{10,... | collective-permute-start | bytes 884744 | tf_op jit(solution)/shard_map/ppermute | solution.py:72
  19.4 7.7 %collective-permute-start.6 = (bf16[384,256]{1,0:T(8,128)(2,1)S(1)}, bf16[384,256]{1,0:T(8,128)(2,1)S(1)}, u32[]{:S(2)}, u32[]{:S(2)}) collective-permute-start(bf16[384,256]{1,0:T(8,128)(2,1)S(1)} %collective-permute-done.2.refs_1_), channel_id=1, source_target_pairs={{0,8},{1,9},{2,10},{3,11},{4,12},{5,13},{6,14},{7,15},{8,0},{9,1},... | collective-permute-start | bytes 589832 | tf_op jit(solution)/shard_map/ppermute | solution.py:72
  20.7 6.4 %collective-permute-start.5 = (bf16[192,256]{1,0:T(8,128)(2,1)S(1)}, bf16[192,256]{1,0:T(8,128)(2,1)S(1)}, u32[]{:S(2)}, u32[]{:S(2)}) collective-permute-start(bf16[192,256]{1,0:T(8,128)(2,1)S(1)} %collective-permute-done.4.refs_0_), channel_id=1, source_target_pairs={{0,2},{1,3},{2,0},{3,1},{4,6},{5,7},{6,4},{7,5},{8,10},{9,11},{10,... | collective-permute-start | bytes 294920 | tf_op jit(solution)/shard_map/ppermute | solution.py:72
  22.3 5.0 %collective-permute-start.10 = (bf16[1344,256]{1,0:T(8,128)(2,1)S(1)}, bf16[1344,256]{1,0:T(8,128)(2,1)S(1)}, u32[]{:S(2)}, u32[]{:S(2)}) collective-permute-start(bf16[1344,256]{1,0:T(8,128)(2,1)S(1)} %constant_dynamic-update-slice_fusion), channel_id=1, source_target_pairs={{0,1},{1,0},{2,3},{3,2},{4,5},{5,4},{6,7},{7,6},{8,9},{9,8},{10,11... | collective-permute-start | bytes 2064392 | tf_op jit(solution)/shard_map/ppermute | solution.py:72
  27.2 2.2 %copy-start.4 = (s32[1,192]{1,0:T(1,128)S(1)}, s32[1,192]{1,0:T(1,128)}, u32[]{:S(2)}) copy-start(s32[1,192]{1,0:T(1,128)} %refs_7_.1) | copy-start | bytes 2308
  27.2 2.2 %collective-permute-start.8 = (bf16[1344,256]{1,0:T(8,128)(2,1)S(1)}, bf16[1344,256]{1,0:T(8,128)(2,1)S(1)}, u32[]{:S(2)}, u32[]{:S(2)}) collective-permute-start(bf16[1344,256]{1,0:T(8,128)(2,1)S(1)} %pad_maximum_fusion), channel_id=1, source_target_pairs={{0,1},{1,0},{2,3},{3,2},{4,5},{5,4},{6,7},{7,6},{8,9},{9,8},{10,11... | collective-permute-start | bytes 2064392 | tf_op jit(solution)/shard_map/ppermute | solution.py:72
  32.1 4.1 %collective-permute-start.16 = (bf16[1152,256]{1,0:T(8,128)(2,1)S(1)}, bf16[1152,256]{1,0:T(8,128)(2,1)S(1)}, u32[]{:S(2)}, u32[]{:S(2)}) collective-permute-start(bf16[1152,256]{1,0:T(8,128)(2,1)S(1)} %terms.7), channel_id=1, source_target_pairs={{0,1},{1,0},{2,3},{3,2},{4,5},{5,4},{6,7},{7,6},{8,9},{9,8},{10,11... | collective-permute-start | bytes 1769480 | tf_op jit(solution)/shard_map/ppermute | solution.py:72
  32.3 2.3 %collective-permute-start.17 = (bf16[384,256]{1,0:T(8,128)(2,1)S(1)}, bf16[384,256]{1,0:T(8,128)(2,1)S(1)}, u32[]{:S(2)}, u32[]{:S(2)}) collective-permute-start(bf16[384,256]{1,0:T(8,128)(2,1)S(1)} %get-tuple-element.27), channel_id=1, source_target_pairs={{0,1},{1,0},{2,3},{3,2},{4,5},{5,4},{6,7},{7,6},{8,9},{9,8},{10,11... | collective-permute-start | bytes 589832 | tf_op jit(solution)/shard_map/ppermute | solution.py:72
  33.2 5.3 %collective-permute-start.11 = (bf16[1536,256]{1,0:T(8,128)(2,1)S(1)}, bf16[1536,256]{1,0:T(8,128)(2,1)S(1)}, u32[]{:S(2)}, u32[]{:S(2)}) collective-permute-start(bf16[1536,256]{1,0:T(8,128)(2,1)S(1)} %terms.5), channel_id=1, source_target_pairs={{0,1},{1,0},{2,3},{3,2},{4,5},{5,4},{6,7},{7,6},{8,9},{9,8},{10,11... | collective-permute-start | bytes 2359304 | tf_op jit(solution)/shard_map/ppermute | solution.py:72
  34.6 8.7 %collective-permute-start.18 = (bf16[384,256]{1,0:T(8,128)(2,1)S(1)}, bf16[384,256]{1,0:T(8,128)(2,1)S(1)}, u32[]{:S(2)}, u32[]{:S(2)}) collective-permute-start(bf16[384,256]{1,0:T(8,128)(2,1)S(1)} %fusion), channel_id=1, source_target_pairs={{0,6},{1,7},{2,4},{3,5},{4,2},{5,3},{6,0},{7,1},{8,14},{9,15},{10,... | collective-permute-start | bytes 589832 | tf_op jit(solution)/shard_map/ppermute | solution.py:72
  36.4 10.7 %collective-permute-start.19 = (bf16[384,256]{1,0:T(8,128)(2,1)S(1)}, bf16[384,256]{1,0:T(8,128)(2,1)S(1)}, u32[]{:S(2)}, u32[]{:S(2)}) collective-permute-start(bf16[384,256]{1,0:T(8,128)(2,1)S(1)} %get-tuple-element.36), channel_id=1, source_target_pairs={{0,4},{1,5},{2,6},{3,7},{4,0},{5,1},{6,2},{7,3},{8,12},{9,13},{10,... | collective-permute-start | bytes 589832 | tf_op jit(solution)/shard_map/ppermute | solution.py:72
  37.9 9.1 %collective-permute-start.20 = (bf16[384,256]{1,0:T(8,128)(2,1)S(1)}, bf16[384,256]{1,0:T(8,128)(2,1)S(1)}, u32[]{:S(2)}, u32[]{:S(2)}) collective-permute-start(bf16[384,256]{1,0:T(8,128)(2,1)S(1)} %get-tuple-element.37), channel_id=1, source_target_pairs={{0,2},{1,3},{2,0},{3,1},{4,6},{5,7},{6,4},{7,5},{8,10},{9,11},{10,... | collective-permute-start | bytes 589832 | tf_op jit(solution)/shard_map/ppermute | solution.py:72
  38.7 11.9 %collective-permute-start.12 = (bf16[768,256]{1,0:T(8,128)(2,1)S(1)}, bf16[768,256]{1,0:T(8,128)(2,1)S(1)}, u32[]{:S(2)}, u32[]{:S(2)}) collective-permute-start(bf16[768,256]{1,0:T(8,128)(2,1)S(1)} %slice.95), channel_id=1, source_target_pairs={{0,8},{1,9},{2,10},{3,11},{4,12},{5,13},{6,14},{7,15},{8,0},{9,1},... | collective-permute-start | bytes 1179656 | tf_op jit(solution)/shard_map/ppermute | solution.py:72
  47.2 11.4 %copy-start.5 = (f32[192,256]{1,0:T(8,128)S(1)}, f32[192,256]{1,0:T(8,128)}, u32[]{:S(2)}) copy-start(f32[192,256]{1,0:T(8,128)} %param.11) | copy-start | bytes 589828
  47.2 11.4 %copy-start.6 = (f32[192,256]{1,0:T(8,128)S(1)}, f32[192,256]{1,0:T(8,128)}, u32[]{:S(2)}) copy-start(f32[192,256]{1,0:T(8,128)} %param.12) | copy-start | bytes 589828
  47.2 11.4 %copy-start.7 = (f32[192,256]{1,0:T(8,128)S(1)}, f32[192,256]{1,0:T(8,128)}, u32[]{:S(2)}) copy-start(f32[192,256]{1,0:T(8,128)} %param.13) | copy-start | bytes 589828
  47.2 10.8 %collective-permute-start.21 = (bf16[192,256]{1,0:T(8,128)(2,1)S(1)}, bf16[192,256]{1,0:T(8,128)(2,1)S(1)}, u32[]{:S(2)}, u32[]{:S(2)}) collective-permute-start(bf16[192,256]{1,0:T(8,128)(2,1)S(1)} %get-tuple-element.43), channel_id=1, source_target_pairs={{0,16},{1,17},{2,18},{3,19},{4,20},{5,21},{6,22},{7,23},{8,24},{9,... | collective-permute-start | bytes 294920 | tf_op jit(solution)/shard_map/ppermute | solution.py:72
  50.6 7.4 %collective-permute-start.22 = (bf16[192,256]{1,0:T(8,128)(2,1)S(1)}, bf16[192,256]{1,0:T(8,128)(2,1)S(1)}, u32[]{:S(2)}, u32[]{:S(2)}) collective-permute-start(bf16[192,256]{1,0:T(8,128)(2,1)S(1)} %get-tuple-element.44), channel_id=1, source_target_pairs={{0,24},{1,25},{2,26},{3,27},{4,28},{5,29},{6,30},{7,31},{8,16},{9,... | collective-permute-start | bytes 294920 | tf_op jit(solution)/shard_map/ppermute | solution.py:72
  50.8 7.3 %collective-permute-start.13 = (bf16[192,256]{1,0:T(8,128)(2,1)S(1)}, bf16[192,256]{1,0:T(8,128)(2,1)S(1)}, u32[]{:S(2)}, u32[]{:S(2)}) collective-permute-start(bf16[192,256]{1,0:T(8,128)(2,1)S(1)} %get-tuple-element.38), channel_id=1, source_target_pairs={{0,6},{1,7},{2,4},{3,5},{4,2},{5,3},{6,0},{7,1},{8,14},{9,15},{10,... | collective-permute-start | bytes 294920 | tf_op jit(solution)/shard_map/ppermute | solution.py:72
  52.1 6.1 %collective-permute-start.14 = (bf16[192,256]{1,0:T(8,128)(2,1)S(1)}, bf16[192,256]{1,0:T(8,128)(2,1)S(1)}, u32[]{:S(2)}, u32[]{:S(2)}) collective-permute-start(bf16[192,256]{1,0:T(8,128)(2,1)S(1)} %get-tuple-element.40), channel_id=1, source_target_pairs={{0,4},{1,5},{2,6},{3,7},{4,0},{5,1},{6,2},{7,3},{8,12},{9,13},{10,... | collective-permute-start | bytes 294920 | tf_op jit(solution)/shard_map/ppermute | solution.py:72
  53.7 4.9 %collective-permute-start.15 = (bf16[192,256]{1,0:T(8,128)(2,1)S(1)}, bf16[192,256]{1,0:T(8,128)(2,1)S(1)}, u32[]{:S(2)}, u32[]{:S(2)}) collective-permute-start(bf16[192,256]{1,0:T(8,128)(2,1)S(1)} %get-tuple-element.39), channel_id=1, source_target_pairs={{0,2},{1,3},{2,0},{3,1},{4,6},{5,7},{6,4},{7,5},{8,10},{9,11},{10,... | collective-permute-start | bytes 294920 | tf_op jit(solution)/shard_map/ppermute | solution.py:72

commit v5 on v4

--- a/solution.py
+++ b/solution.py
@@ -210,10 +210,12 @@
     z1 = hop(both, 1, 0, 0, 0)
     z3 = hop(z2, 1, 0, 0, 0)
     x2 = hop(z2, 0, 1, 0, 0)
+    y2 = hop(z2, 0, 0, 1, 0)
+
     z3, x0, x2 = lax.optimization_barrier((z3, x0, x2))
     x3 = hop(z3, 0, 1, 0, 0)
-    ya = hop(join(z2, z3, x2), 0, 0, 1, 0)
-    zx = hop(x0, 1, 0, 0, 0)
+    ya = hop(join(z3, x2), 0, 0, 1, 0)
+    zx = hop(z1, 0, 1, 0, 0)
     yb = hop(x3, 0, 0, 1, 0)
     yb, second = lax.optimization_barrier((yb, second))
 
@@ -222,18 +224,12 @@
         pieces = [(array, [(*at, 0) for at in place]) for array, place in zip(arrays, places)]
         return pieces + [(other, [(*at, 1) for place in places for at in place])]
 
-    early = both_cores(
-        (x0, z1, z2, z3, x2),
-        ([(0, 1, 0), (0, 1, 1)], [(1, 0, 0), (1, 0, 1)], [(2, 0, 0)], [(3, 0, 0)], [(2, 1, 0)]),
-    )
-    late = both_cores(
-        (x3, zx, ya, yb),
-        ([(3, 1, 0)], [(1, 1, 0), (1, 1, 1)], [(2, 0, 1), (3, 0, 1), (2, 1, 1)], [(3, 1, 1)]),
-    )
+    early = both_cores((x0, z2, z3, x2, y2, x3,), ([(0, 1, 0), (0, 1, 1)], [(2, 0, 0)], [(3, 0, 0)], [(2, 1, 0)], [(2, 0, 1)], [(3, 1, 0)],))
+    late = both_cores((z1, zx, ya, yb,), ([(1, 0, 0), (1, 0, 1)], [(1, 1, 0), (1, 1, 1)], [(3, 0, 1), (2, 1, 1)], [(3, 1, 1)],))
     return [(weight_copy, [None]), *early], late, first, second
 
 
-SIDES = ((1, 1), (1, 0), (0, 1))
+SIDES = ((1, 1), (0, 1), (1, 0))
 
 
 def cut(array, count):
@@ -282,7 +278,7 @@
         [bfloat((2 * rows, columns))] + [bfloat((tokens, columns))] * 2,
         "attend",
         (*[piece for piece, _ in late], acts, cots, documents, acts_t, cots_t, front, back),
-        scratch=[pltpu.VMEM((16 * rows, columns), jnp.bfloat16)],
+        scratch=[pltpu.VMEM((24 * rows, columns), jnp.bfloat16)],
         flops=flops,
     )
 

time: 66.6 us -> 65.5 us (0.983)
  waiting for transfers between devices: 19.9 us -> 18.8 us
    ppermute x23 -> x24, waiting for transfers between devices: 19.9 us -> 18.8 us  [hop(): return lax.ppermute(value, AXES, [(i, i ^ offset) for i in range(32)])]
    ppermute x23 -> x24, starting transfers between devices: 27 us -> 26.8 us  [hop(): return lax.ppermute(value, AXES, [(i, i ^ offset) for i in range(32)])]
    unnamed x21 -> x22, local copies, waits for them, and re-layouts: 2.5 us -> 2.5 us
  transfers between devices with their start and end apart: 23 -> 24, of which waited for: 11 -> 10; matrix products, arithmetic and copies ran while one was open for 1% -> 1% of each run, Pallas kernels for 7% -> 7%
where the time goes in v5:
time: 65.5 us; the launch traced here: 65.3 us
  starting transfers between devices  26.8 us (41%)
  waiting for transfers between devices  18.8 us (29%)
  Pallas kernels  7.23 us (11%)
  blocking collectives  6.26 us (10%)
  local copies, waits for them, and re-layouts  3.57 us (5%)
  other arithmetic  1.69 us (3%)
  between operations  0.91 us (1%)
    ppermute x24, starting transfers between devices, hop(): return lax.ppermute(value, AXES, [(i, i ^ offset) for i in range(32)])  26.8 us
    ppermute x24, waiting for transfers between devices, hop(): return lax.ppermute(value, AXES, [(i, i ^ offset) for i in range(32)])  18.8 us
    pallas_call x8, Pallas kernels, kernel_call(): pl.pallas_call(body, out_shape=outs, in_specs=vmem(len(args)), out_specs=...  7.23 us
    all_gather x1, blocking collectives, block_body(): lax.all_gather(primary_new.astype(jnp.bfloat16), 'rep', axis=0, tiled=True)  6.26 us
    unnamed x22, local copies, waits for them, and re-layouts  2.5 us
  transfers between devices with their start and end apart: 24, of which 10 were waited for; matrix products, arithmetic and copies ran while one was open for 1% of the time, Pallas kernels for 7%

profile of v5, /device:TPU:0, one launch (start us, length us, event | category | flops | bytes accessed | tf_op | source)
XLA Modules:
  0.0 65.3 jit_solution(10379271590025883725)
XLA Ops:
  0.6 1.0 %constant_dynamic-slice_fusion = (bf16[192,256]{1,0:T(8,128)(2,1)S(1)}, bf16[192,256]{1,0:T(8,128)(2,1)S(1)}) fusion(bf16[768,256]{1,0:T(8,128)(2,1)} %refs_0_.1, s32[]{:T(128)S(6)} %select_n.7, s32[]{:T(128)S(6)} %select_n.6), kind=kLoop, calls=%fused_computation.28 | loop fusion | bytes 393224 | tf_op jit(solution)/shard_map/dynamic_slice | solution.py:205
  1.6 4.1 %collective-permute-start = (bf16[192,256]{1,0:T(8,128)(2,1)S(1)}, bf16[192,256]{1,0:T(8,128)(2,1)S(1)}, u32[]{:S(2)}, u32[]{:S(2)}) collective-permute-start(bf16[192,256]{1,0:T(8,128)(2,1)S(1)} %get-tuple-element.42), channel_id=1, source_target_pairs={{0,16},{1,17},{2,18},{3,19},{4,20},{5,21},{6,22},{7,23},{8,24},{9,... | collective-permute-start | bytes 294920 | tf_op jit(solution)/shard_map/ppermute | solution.py:72
  5.7 1.6 %collective-permute-start.2 = (bf16[384,256]{1,0:T(8,128)(2,1)S(1)}, bf16[384,256]{1,0:T(8,128)(2,1)S(1)}, u32[]{:S(2)}, u32[]{:S(2)}) collective-permute-start(bf16[384,256]{1,0:T(8,128)(2,1)S(1)} %pad_maximum_fusion.1), channel_id=1, source_target_pairs={{0,4},{1,5},{2,6},{3,7},{4,0},{5,1},{6,2},{7,3},{8,12},{9,13},{10,... | collective-permute-start | bytes 589832 | tf_op jit(solution)/shard_map/ppermute | solution.py:72
  7.3 1.7 %copy-done = bf16[1,192,6144]{2,1,0:T(8,128)(2,1)S(1)} copy-done((bf16[1,192,6144]{2,1,0:T(8,128)(2,1)S(1)}, bf16[1,192,6144]{2,1,0:T(8,128)(2,1)}, u32[]{:S(2)}) %copy-start) | copy-done | bytes 2359320
  8.9 0.9 %turn.2.refs_8_.acts_t = bf16[6144,192]{1,0:T(8,128)(2,1)S(1)} custom-call(bf16[192,6144]{1,0:T(8,128)(2,1)S(1)} %bitcast.2), custom_call_target="tpu_custom_call" | custom-call | flops 603979776 | bytes 4194304 | tf_op jit(solution)/shard_map/turn/pallas_call | solution.py:190
  9.8 0.8 %collective-permute-done.refs_2_ = bf16[192,256]{1,0:T(8,128)(2,1)S(1)} collective-permute-done((bf16[192,256]{1,0:T(8,128)(2,1)S(1)}, bf16[192,256]{1,0:T(8,128)(2,1)S(1)}, u32[]{:S(2)}, u32[]{:S(2)}) %collective-permute-start) | collective-permute-done | bytes 98336 | tf_op jit(solution)/shard_map/ppermute | solution.py:72
  10.6 0.9 %collective-permute-start.1 = (bf16[192,256]{1,0:T(8,128)(2,1)S(1)}, bf16[192,256]{1,0:T(8,128)(2,1)S(1)}, u32[]{:S(2)}, u32[]{:S(2)}) collective-permute-start(bf16[192,256]{1,0:T(8,128)(2,1)S(1)} %collective-permute-done.refs_2_), channel_id=1, source_target_pairs={{0,8},{1,9},{2,10},{3,11},{4,12},{5,13},{6,14},{7,15},{8,0},{9,1},... | collective-permute-start | bytes 294920 | tf_op jit(solution)/shard_map/ppermute | solution.py:72
  11.5 1.3 %collective-permute-start.3 = (bf16[192,256]{1,0:T(8,128)(2,1)S(1)}, bf16[192,256]{1,0:T(8,128)(2,1)S(1)}, u32[]{:S(2)}, u32[]{:S(2)}) collective-permute-start(bf16[192,256]{1,0:T(8,128)(2,1)S(1)} %collective-permute-done.refs_2_), channel_id=1, source_target_pairs={{0,4},{1,5},{2,6},{3,7},{4,0},{5,1},{6,2},{7,3},{8,12},{9,13},{10,... | collective-permute-start | bytes 294920 | tf_op jit(solution)/shard_map/ppermute | solution.py:72
  12.8 1.4 %collective-permute-start.6 = (bf16[384,256]{1,0:T(8,128)(2,1)S(1)}, bf16[384,256]{1,0:T(8,128)(2,1)S(1)}, u32[]{:S(2)}, u32[]{:S(2)}) collective-permute-start(bf16[384,256]{1,0:T(8,128)(2,1)S(1)} %pad_maximum_fusion.1), channel_id=1, source_target_pairs={{0,8},{1,9},{2,10},{3,11},{4,12},{5,13},{6,14},{7,15},{8,0},{9,1},... | collective-permute-start | bytes 589832 | tf_op jit(solution)/shard_map/ppermute | solution.py:72
  14.2 0.9 %turn.3.refs_9_.cots_t = bf16[6144,192]{1,0:T(8,128)(2,1)S(1)} custom-call(bf16[192,6144]{1,0:T(8,128)(2,1)S(1)} %bitcast.5), custom_call_target="tpu_custom_call" | custom-call | flops 603979776 | bytes 4194304 | tf_op jit(solution)/shard_map/turn/pallas_call | solution.py:190
  15.1 0.0 copy-start.1
  15.1 0.0 copy-start.3
  15.1 1.6 %collective-permute-start.10 = (bf16[192,256]{1,0:T(8,128)(2,1)S(1)}, bf16[192,256]{1,0:T(8,128)(2,1)S(1)}, u32[]{:S(2)}, u32[]{:S(2)}) collective-permute-start(bf16[192,256]{1,0:T(8,128)(2,1)S(1)} %collective-permute-done.refs_2_), channel_id=1, source_target_pairs={{0,2},{1,3},{2,0},{3,1},{4,6},{5,7},{6,4},{7,5},{8,10},{9,11},{10,... | collective-permute-start | bytes 294920 | tf_op jit(solution)/shard_map/ppermute | solution.py:72
  16.7 0.0 collective-permute-done.1.refs_3_
  16.7 0.0 collective-permute-done.3.refs_4_
  16.7 1.2 %collective-permute-start.4 = (bf16[192,256]{1,0:T(8,128)(2,1)S(1)}, bf16[192,256]{1,0:T(8,128)(2,1)S(1)}, u32[]{:S(2)}, u32[]{:S(2)}) collective-permute-start(bf16[192,256]{1,0:T(8,128)(2,1)S(1)} %collective-permute-done.1.refs_3_), channel_id=1, source_target_pairs={{0,4},{1,5},{2,6},{3,7},{4,0},{5,1},{6,2},{7,3},{8,12},{9,13},{10,... | collective-permute-start | bytes 294920 | tf_op jit(solution)/shard_map/ppermute | solution.py:72
  17.9 1.6 %collective-permute-start.8 = (bf16[384,256]{1,0:T(8,128)(2,1)S(1)}, bf16[384,256]{1,0:T(8,128)(2,1)S(1)}, u32[]{:S(2)}, u32[]{:S(2)}) collective-permute-start(bf16[384,256]{1,0:T(8,128)(2,1)S(1)} %pad_maximum_fusion.2), channel_id=1, source_target_pairs={{0,2},{1,3},{2,0},{3,1},{4,6},{5,7},{6,4},{7,5},{8,10},{9,11},{10,... | collective-permute-start | bytes 589832 | tf_op jit(solution)/shard_map/ppermute | solution.py:72
  19.5 1.1 %collective-permute-start.7 = (bf16[384,256]{1,0:T(8,128)(2,1)S(1)}, bf16[384,256]{1,0:T(8,128)(2,1)S(1)}, u32[]{:S(2)}, u32[]{:S(2)}) collective-permute-start(bf16[384,256]{1,0:T(8,128)(2,1)S(1)} %collective-permute-done.6.refs_0_), channel_id=1, source_target_pairs={{0,4},{1,5},{2,6},{3,7},{4,0},{5,1},{6,2},{7,3},{8,12},{9,13},{10,... | collective-permute-start | bytes 589832 | tf_op jit(solution)/shard_map/ppermute | solution.py:72
  20.7 0.1 collective-permute-done.10.refs_5_
  20.8 1.2 %collective-permute-done.4.refs_6_ = bf16[192,256]{1,0:T(8,128)(2,1)S(1)} collective-permute-done((bf16[192,256]{1,0:T(8,128)(2,1)S(1)}, bf16[192,256]{1,0:T(8,128)(2,1)S(1)}, u32[]{:S(2)}, u32[]{:S(2)}) %collective-permute-start.4) | collective-permute-done | bytes 98336 | tf_op jit(solution)/shard_map/ppermute | solution.py:72
  22.0 0.4 collective-permute-start.5
  22.4 0.1 collective-permute-start.11
  22.5 4.1 %collective-permute-done.5.refs_3_ = bf16[192,256]{1,0:T(8,128)(2,1)S(1)} collective-permute-done((bf16[192,256]{1,0:T(8,128)(2,1)S(1)}, bf16[192,256]{1,0:T(8,128)(2,1)S(1)}, u32[]{:S(2)}, u32[]{:S(2)}) %collective-permute-start.5) | collective-permute-done | bytes 98336 | tf_op jit(solution)/shard_map/ppermute | solution.py:72
  26.6 0.0 copy-start.4
  26.6 0.1 collective-permute-start.9
  26.7 0.0 collective-permute-done.11.refs_7_
  26.8 1.2 %early.1 = (f32[192,192]{1,0:T(8,128)S(1)}, f32[192,64]{1,0:T(8,128)S(1)}) custom-call(bf16[768,256]{1,0:T(8,128)(2,1)S(1)} %copy-done.3, bf16[384,256]{1,0:T(8,128)(2,1)S(1)} %collective-permute-done.2.refs_1_, bf16[192,256]{1,0:T(8,128)(2,1)S(1)} %collective-permute-done.refs_2_, bf16[192,256]{1,0:T(8,128)(2,1)S(1)} %collective-permute-done.1.refs_3_, ...), custom_call_target="tpu_custom_call" | custom-call | flops 1207959552 | bytes 4194304 | tf_op jit(solution)/shard_map/early/pallas_call | solution.py:190
  27.9 0.9 %collective-permute-done.9.refs_4_ = bf16[1344,256]{1,0:T(8,128)(2,1)S(1)} collective-permute-done((bf16[1344,256]{1,0:T(8,128)(2,1)S(1)}, bf16[1344,256]{1,0:T(8,128)(2,1)S(1)}, u32[]{:S(2)}, u32[]{:S(2)}) %collective-permute-start.9) | collective-permute-done | bytes 688160 | tf_op jit(solution)/shard_map/ppermute | solution.py:72
  28.9 2.2 %attend.1 = (bf16[384,256]{1,0:T(8,128)(2,1)S(1)}, bf16[192,256]{1,0:T(8,128)(2,1)S(1)}, bf16[192,256]{1,0:T(8,128)(2,1)S(1)}) custom-call(bf16[384,256]{1,0:T(8,128)(2,1)S(1)} %collective-permute-done.6.refs_0_, bf16[384,256]{1,0:T(8,128)(2,1)S(1)} %collective-permute-done.7.refs_1_, bf16[384,256]{1,0:T(8,128)(2,1)S(1)} %collective-permute-done.8.refs_2_, ...), custom_call_target="tpu_custom_call" | custom-call | flops 1207959552 | bytes 4194304 | tf_op jit(solution)/shard_map/attend/pallas_call | solution.py:190
  31.0 0.5 terms.7
  31.5 0.2 collective-permute-start.17
  31.7 0.4 collective-permute-start.18
  32.1 0.6 terms.5
  32.6 0.2 collective-permute-start.12
  32.8 0.6 terms.4
  33.4 0.6 terms.6
  33.9 0.0 collective-permute-done.18
  34.0 2.2 %collective-permute-start.19 = (bf16[384,256]{1,0:T(8,128)(2,1)S(1)}, bf16[384,256]{1,0:T(8,128)(2,1)S(1)}, u32[]{:S(2)}, u32[]{:S(2)}) collective-permute-start(bf16[384,256]{1,0:T(8,128)(2,1)S(1)} %fusion), channel_id=1, source_target_pairs={{0,6},{1,7},{2,4},{3,5},{4,2},{5,3},{6,0},{7,1},{8,14},{9,15},{10,... | collective-permute-start | bytes 589832 | tf_op jit(solution)/shard_map/ppermute | solution.py:72
  36.2 0.0 collective-permute-done.17
  36.2 0.2 fusion.12
  36.4 0.6 collective-permute-start.20
  37.0 0.9 %collective-permute-start.21 = (bf16[384,256]{1,0:T(8,128)(2,1)S(1)}, bf16[384,256]{1,0:T(8,128)(2,1)S(1)}, u32[]{:S(2)}, u32[]{:S(2)}) collective-permute-start(bf16[384,256]{1,0:T(8,128)(2,1)S(1)} %get-tuple-element.37), channel_id=1, source_target_pairs={{0,4},{1,5},{2,6},{3,7},{4,0},{5,1},{6,2},{7,3},{8,12},{9,13},{10,... | collective-permute-start | bytes 589832 | tf_op jit(solution)/shard_map/ppermute | solution.py:72
  37.9 0.3 convert_add_fusion
  38.2 0.5 collective-permute-start.13
  38.7 4.1 %collective-permute-done.19 = bf16[384,256]{1,0:T(8,128)(2,1)S(1)} collective-permute-done((bf16[384,256]{1,0:T(8,128)(2,1)S(1)}, bf16[384,256]{1,0:T(8,128)(2,1)S(1)}, u32[]{:S(2)}, u32[]{:S(2)}) %collective-permute-start.19) | collective-permute-done | bytes 196640 | tf_op jit(solution)/shard_map/ppermute | solution.py:72
  42.8 3.6 %collective-permute-done.20 = bf16[384,256]{1,0:T(8,128)(2,1)S(1)} collective-permute-done((bf16[384,256]{1,0:T(8,128)(2,1)S(1)}, bf16[384,256]{1,0:T(8,128)(2,1)S(1)}, u32[]{:S(2)}, u32[]{:S(2)}) %collective-permute-start.20) | collective-permute-done | bytes 196640 | tf_op jit(solution)/shard_map/ppermute | solution.py:72
  46.4 0.0 collective-permute-done.21
  46.4 0.1 fusion.3
  46.5 0.0 copy-start.5
  46.5 0.0 copy-start.6
  46.5 0.0 copy-start.7
  46.5 2.7 %collective-permute-start.22 = (bf16[192,256]{1,0:T(8,128)(2,1)S(1)}, bf16[192,256]{1,0:T(8,128)(2,1)S(1)}, u32[]{:S(2)}, u32[]{:S(2)}) collective-permute-start(bf16[192,256]{1,0:T(8,128)(2,1)S(1)} %get-tuple-element.43), channel_id=1, source_target_pairs={{0,16},{1,17},{2,18},{3,19},{4,20},{5,21},{6,22},{7,23},{8,24},{9,... | collective-permute-start | bytes 294920 | tf_op jit(solution)/shard_map/ppermute | solution.py:72
  49.3 0.4 collective-permute-start.23
  49.6 0.0 collective-permute-done.13
  49.6 0.1 fusion.11
  49.7 2.1 %collective-permute-start.14 = (bf16[192,256]{1,0:T(8,128)(2,1)S(1)}, bf16[192,256]{1,0:T(8,128)(2,1)S(1)}, u32[]{:S(2)}, u32[]{:S(2)}) collective-permute-start(bf16[192,256]{1,0:T(8,128)(2,1)S(1)} %get-tuple-element.38), channel_id=1, source_target_pairs={{0,6},{1,7},{2,4},{3,5},{4,2},{5,3},{6,0},{7,1},{8,14},{9,15},{10,... | collective-permute-start | bytes 294920 | tf_op jit(solution)/shard_map/ppermute | solution.py:72
  51.8 0.8 %collective-permute-start.15 = (bf16[192,256]{1,0:T(8,128)(2,1)S(1)}, bf16[192,256]{1,0:T(8,128)(2,1)S(1)}, u32[]{:S(2)}, u32[]{:S(2)}) collective-permute-start(bf16[192,256]{1,0:T(8,128)(2,1)S(1)} %get-tuple-element.40), channel_id=1, source_target_pairs={{0,2},{1,3},{2,0},{3,1},{4,6},{5,7},{6,4},{7,5},{8,10},{9,11},{10,... | collective-permute-start | bytes 294920 | tf_op jit(solution)/shard_map/ppermute | solution.py:72
  52.6 0.7 %collective-permute-start.16 = (bf16[192,256]{1,0:T(8,128)(2,1)S(1)}, bf16[192,256]{1,0:T(8,128)(2,1)S(1)}, u32[]{:S(2)}, u32[]{:S(2)}) collective-permute-start(bf16[192,256]{1,0:T(8,128)(2,1)S(1)} %get-tuple-element.39), channel_id=1, source_target_pairs={{0,4},{1,5},{2,6},{3,7},{4,0},{5,1},{6,2},{7,3},{8,12},{9,13},{10,... | collective-permute-start | bytes 294920 | tf_op jit(solution)/shard_map/ppermute | solution.py:72
  53.3 3.8 %collective-permute-done.22 = bf16[192,256]{1,0:T(8,128)(2,1)S(1)} collective-permute-done((bf16[192,256]{1,0:T(8,128)(2,1)S(1)}, bf16[192,256]{1,0:T(8,128)(2,1)S(1)}, u32[]{:S(2)}, u32[]{:S(2)}) %collective-permute-start.22) | collective-permute-done | bytes 98336 | tf_op jit(solution)/shard_map/ppermute | solution.py:72
  57.1 0.2 collective-permute-done.15
  57.3 0.1 collective-permute-done.16
  57.4 1.0 %fusion.9 = (bf16[192,256]{1,0:T(8,128)(2,1)S(1)}, f32[192,256]{1,0:T(8,128)}, f32[192,256]{1,0:T(8,128)}, f32[192,256]{1,0:T(8,128)}) fusion(f32[192,256]{1,0:T(8,128)S(1)} %copy-done.5, f32[192,256]{1,0:T(8,128)S(1)} %copy-done.6, f32[192,256]{1,0:T(8,128)S(1)} %copy-done.7, bf16[192,256]{1,0:T(8,128)(2,1)S(1)} %collective-permute-done.23, ...), kind=kLoop, calls=%fused_computation.30 | loop fusion | flops 1277952 | bytes 1966080 | tf_op jit(solution)/shard_map/convert_element_type | solution.py:311
  58.3 6.3 %all_gather.3 = bf16[768,256]{1,0:T(8,128)(2,1)S(1)} all-gather(bf16[192,256]{1,0:T(8,128)(2,1)S(1)} %get-tuple-element.28), channel_id=1, replica_groups=mesh['grp'=8,'rep'=4] {'rep'}, dimensions={0}, use_global_device_ids=true | all-gather | bytes 491520 | tf_op jit(solution)/shard_map/all_gather | solution.py:311
  64.6 0.7 %copy.17 = bf16[768,256]{1,0:T(8,128)(2,1)} copy(bf16[768,256]{1,0:T(8,128)(2,1)S(1)} %all_gather.3) | data formatting | bytes 786432
  (30 shorter events, 0.3 us)
Async XLA Ops:
  1.6 9.0 %collective-permute-start = (bf16[192,256]{1,0:T(8,128)(2,1)S(1)}, bf16[192,256]{1,0:T(8,128)(2,1)S(1)}, u32[]{:S(2)}, u32[]{:S(2)}) collective-permute-start(bf16[192,256]{1,0:T(8,128)(2,1)S(1)} %get-tuple-element.42), channel_id=1, source_target_pairs={{0,16},{1,17},{2,18},{3,19},{4,20},{5,21},{6,22},{7,23},{8,24},{9,... | collective-permute-start | bytes 294920 | tf_op jit(solution)/shard_map/ppermute | solution.py:72
  5.7 11.0 %collective-permute-start.2 = (bf16[384,256]{1,0:T(8,128)(2,1)S(1)}, bf16[384,256]{1,0:T(8,128)(2,1)S(1)}, u32[]{:S(2)}, u32[]{:S(2)}) collective-permute-start(bf16[384,256]{1,0:T(8,128)(2,1)S(1)} %pad_maximum_fusion.1), channel_id=1, source_target_pairs={{0,4},{1,5},{2,6},{3,7},{4,0},{5,1},{6,2},{7,3},{8,12},{9,13},{10,... | collective-permute-start | bytes 589832 | tf_op jit(solution)/shard_map/ppermute | solution.py:72
  7.3 1.7 %copy-start = (bf16[1,192,6144]{2,1,0:T(8,128)(2,1)S(1)}, bf16[1,192,6144]{2,1,0:T(8,128)(2,1)}, u32[]{:S(2)}) copy-start(bf16[1,192,6144]{2,1,0:T(8,128)(2,1)} %param.7) | copy-start | bytes 7077892
  8.9 5.2 %copy-start.2 = (bf16[1,192,6144]{2,1,0:T(8,128)(2,1)S(1)}, bf16[1,192,6144]{2,1,0:T(8,128)(2,1)}, u32[]{:S(2)}) copy-start(bf16[1,192,6144]{2,1,0:T(8,128)(2,1)} %param.8) | copy-start | bytes 7077892
  10.6 6.1 %collective-permute-start.1 = (bf16[192,256]{1,0:T(8,128)(2,1)S(1)}, bf16[192,256]{1,0:T(8,128)(2,1)S(1)}, u32[]{:S(2)}, u32[]{:S(2)}) collective-permute-start(bf16[192,256]{1,0:T(8,128)(2,1)S(1)} %collective-permute-done.refs_2_), channel_id=1, source_target_pairs={{0,8},{1,9},{2,10},{3,11},{4,12},{5,13},{6,14},{7,15},{8,0},{9,1},... | collective-permute-start | bytes 294920 | tf_op jit(solution)/shard_map/ppermute | solution.py:72
  11.5 5.2 %collective-permute-start.3 = (bf16[192,256]{1,0:T(8,128)(2,1)S(1)}, bf16[192,256]{1,0:T(8,128)(2,1)S(1)}, u32[]{:S(2)}, u32[]{:S(2)}) collective-permute-start(bf16[192,256]{1,0:T(8,128)(2,1)S(1)} %collective-permute-done.refs_2_), channel_id=1, source_target_pairs={{0,4},{1,5},{2,6},{3,7},{4,0},{5,1},{6,2},{7,3},{8,12},{9,13},{10,... | collective-permute-start | bytes 294920 | tf_op jit(solution)/shard_map/ppermute | solution.py:72
  12.8 6.7 %collective-permute-start.6 = (bf16[384,256]{1,0:T(8,128)(2,1)S(1)}, bf16[384,256]{1,0:T(8,128)(2,1)S(1)}, u32[]{:S(2)}, u32[]{:S(2)}) collective-permute-start(bf16[384,256]{1,0:T(8,128)(2,1)S(1)} %pad_maximum_fusion.1), channel_id=1, source_target_pairs={{0,8},{1,9},{2,10},{3,11},{4,12},{5,13},{6,14},{7,15},{8,0},{9,1},... | collective-permute-start | bytes 589832 | tf_op jit(solution)/shard_map/ppermute | solution.py:72
  15.1 11.7 %copy-start.1 = (bf16[1,192,6144]{2,1,0:T(8,128)(2,1)S(1)}, bf16[1,192,6144]{2,1,0:T(8,128)(2,1)}, u32[]{:S(2)}) copy-start(bf16[1,192,6144]{2,1,0:T(8,128)(2,1)} %param.7) | copy-start | bytes 7077892
  15.1 11.7 %copy-start.3 = (bf16[768,256]{1,0:T(8,128)(2,1)S(1)}, bf16[768,256]{1,0:T(8,128)(2,1)}, u32[]{:S(2)}) copy-start(bf16[768,256]{1,0:T(8,128)(2,1)} %refs_0_.1) | copy-start | bytes 1179652
  15.1 5.7 %collective-permute-start.10 = (bf16[192,256]{1,0:T(8,128)(2,1)S(1)}, bf16[192,256]{1,0:T(8,128)(2,1)S(1)}, u32[]{:S(2)}, u32[]{:S(2)}) collective-permute-start(bf16[192,256]{1,0:T(8,128)(2,1)S(1)} %collective-permute-done.refs_2_), channel_id=1, source_target_pairs={{0,2},{1,3},{2,0},{3,1},{4,6},{5,7},{6,4},{7,5},{8,10},{9,11},{10,... | collective-permute-start | bytes 294920 | tf_op jit(solution)/shard_map/ppermute | solution.py:72
  16.7 5.2 %collective-permute-start.4 = (bf16[192,256]{1,0:T(8,128)(2,1)S(1)}, bf16[192,256]{1,0:T(8,128)(2,1)S(1)}, u32[]{:S(2)}, u32[]{:S(2)}) collective-permute-start(bf16[192,256]{1,0:T(8,128)(2,1)S(1)} %collective-permute-done.1.refs_3_), channel_id=1, source_target_pairs={{0,4},{1,5},{2,6},{3,7},{4,0},{5,1},{6,2},{7,3},{8,12},{9,13},{10,... | collective-permute-start | bytes 294920 | tf_op jit(solution)/shard_map/ppermute | solution.py:72
  17.9 8.7 %collective-permute-start.8 = (bf16[384,256]{1,0:T(8,128)(2,1)S(1)}, bf16[384,256]{1,0:T(8,128)(2,1)S(1)}, u32[]{:S(2)}, u32[]{:S(2)}) collective-permute-start(bf16[384,256]{1,0:T(8,128)(2,1)S(1)} %pad_maximum_fusion.2), channel_id=1, source_target_pairs={{0,2},{1,3},{2,0},{3,1},{4,6},{5,7},{6,4},{7,5},{8,10},{9,11},{10,... | collective-permute-start | bytes 589832 | tf_op jit(solution)/shard_map/ppermute | solution.py:72
  19.5 7.0 %collective-permute-start.7 = (bf16[384,256]{1,0:T(8,128)(2,1)S(1)}, bf16[384,256]{1,0:T(8,128)(2,1)S(1)}, u32[]{:S(2)}, u32[]{:S(2)}) collective-permute-start(bf16[384,256]{1,0:T(8,128)(2,1)S(1)} %collective-permute-done.6.refs_0_), channel_id=1, source_target_pairs={{0,4},{1,5},{2,6},{3,7},{4,0},{5,1},{6,2},{7,3},{8,12},{9,13},{10,... | collective-permute-start | bytes 589832 | tf_op jit(solution)/shard_map/ppermute | solution.py:72
  22.0 4.6 %collective-permute-start.5 = (bf16[192,256]{1,0:T(8,128)(2,1)S(1)}, bf16[192,256]{1,0:T(8,128)(2,1)S(1)}, u32[]{:S(2)}, u32[]{:S(2)}) collective-permute-start(bf16[192,256]{1,0:T(8,128)(2,1)S(1)} %collective-permute-done.4.refs_6_), channel_id=1, source_target_pairs={{0,2},{1,3},{2,0},{3,1},{4,6},{5,7},{6,4},{7,5},{8,10},{9,11},{10,... | collective-permute-start | bytes 294920 | tf_op jit(solution)/shard_map/ppermute | solution.py:72
  22.4 4.3 %collective-permute-start.11 = (bf16[1344,256]{1,0:T(8,128)(2,1)S(1)}, bf16[1344,256]{1,0:T(8,128)(2,1)S(1)}, u32[]{:S(2)}, u32[]{:S(2)}) collective-permute-start(bf16[1344,256]{1,0:T(8,128)(2,1)S(1)} %constant_dynamic-update-slice_fusion), channel_id=1, source_target_pairs={{0,1},{1,0},{2,3},{3,2},{4,5},{5,4},{6,7},{7,6},{8,9},{9,8},{10,11... | collective-permute-start | bytes 2064392 | tf_op jit(solution)/shard_map/ppermute | solution.py:72
  26.6 2.2 %copy-start.4 = (s32[1,192]{1,0:T(1,128)S(1)}, s32[1,192]{1,0:T(1,128)}, u32[]{:S(2)}) copy-start(s32[1,192]{1,0:T(1,128)} %refs_7_.1) | copy-start | bytes 2308
  26.6 2.2 %collective-permute-start.9 = (bf16[1344,256]{1,0:T(8,128)(2,1)S(1)}, bf16[1344,256]{1,0:T(8,128)(2,1)S(1)}, u32[]{:S(2)}, u32[]{:S(2)}) collective-permute-start(bf16[1344,256]{1,0:T(8,128)(2,1)S(1)} %pad_maximum_fusion), channel_id=1, source_target_pairs={{0,1},{1,0},{2,3},{3,2},{4,5},{5,4},{6,7},{7,6},{8,9},{9,8},{10,11... | collective-permute-start | bytes 2064392 | tf_op jit(solution)/shard_map/ppermute | solution.py:72
  31.5 4.7 %collective-permute-start.17 = (bf16[1152,256]{1,0:T(8,128)(2,1)S(1)}, bf16[1152,256]{1,0:T(8,128)(2,1)S(1)}, u32[]{:S(2)}, u32[]{:S(2)}) collective-permute-start(bf16[1152,256]{1,0:T(8,128)(2,1)S(1)} %terms.7), channel_id=1, source_target_pairs={{0,1},{1,0},{2,3},{3,2},{4,5},{5,4},{6,7},{7,6},{8,9},{9,8},{10,11... | collective-permute-start | bytes 1769480 | tf_op jit(solution)/shard_map/ppermute | solution.py:72
  31.7 2.3 %collective-permute-start.18 = (bf16[384,256]{1,0:T(8,128)(2,1)S(1)}, bf16[384,256]{1,0:T(8,128)(2,1)S(1)}, u32[]{:S(2)}, u32[]{:S(2)}) collective-permute-start(bf16[384,256]{1,0:T(8,128)(2,1)S(1)} %get-tuple-element.27), channel_id=1, source_target_pairs={{0,1},{1,0},{2,3},{3,2},{4,5},{5,4},{6,7},{7,6},{8,9},{9,8},{10,11... | collective-permute-start | bytes 589832 | tf_op jit(solution)/shard_map/ppermute | solution.py:72
  32.6 5.3 %collective-permute-start.12 = (bf16[1536,256]{1,0:T(8,128)(2,1)S(1)}, bf16[1536,256]{1,0:T(8,128)(2,1)S(1)}, u32[]{:S(2)}, u32[]{:S(2)}) collective-permute-start(bf16[1536,256]{1,0:T(8,128)(2,1)S(1)} %terms.5), channel_id=1, source_target_pairs={{0,1},{1,0},{2,3},{3,2},{4,5},{5,4},{6,7},{7,6},{8,9},{9,8},{10,11... | collective-permute-start | bytes 2359304 | tf_op jit(solution)/shard_map/ppermute | solution.py:72
  34.0 8.7 %collective-permute-start.19 = (bf16[384,256]{1,0:T(8,128)(2,1)S(1)}, bf16[384,256]{1,0:T(8,128)(2,1)S(1)}, u32[]{:S(2)}, u32[]{:S(2)}) collective-permute-start(bf16[384,256]{1,0:T(8,128)(2,1)S(1)} %fusion), channel_id=1, source_target_pairs={{0,6},{1,7},{2,4},{3,5},{4,2},{5,3},{6,0},{7,1},{8,14},{9,15},{10,... | collective-permute-start | bytes 589832 | tf_op jit(solution)/shard_map/ppermute | solution.py:72
  36.4 10.0 %collective-permute-start.20 = (bf16[384,256]{1,0:T(8,128)(2,1)S(1)}, bf16[384,256]{1,0:T(8,128)(2,1)S(1)}, u32[]{:S(2)}, u32[]{:S(2)}) collective-permute-start(bf16[384,256]{1,0:T(8,128)(2,1)S(1)} %get-tuple-element.36), channel_id=1, source_target_pairs={{0,2},{1,3},{2,0},{3,1},{4,6},{5,7},{6,4},{7,5},{8,10},{9,11},{10,... | collective-permute-start | bytes 589832 | tf_op jit(solution)/shard_map/ppermute | solution.py:72
  37.0 9.4 %collective-permute-start.21 = (bf16[384,256]{1,0:T(8,128)(2,1)S(1)}, bf16[384,256]{1,0:T(8,128)(2,1)S(1)}, u32[]{:S(2)}, u32[]{:S(2)}) collective-permute-start(bf16[384,256]{1,0:T(8,128)(2,1)S(1)} %get-tuple-element.37), channel_id=1, source_target_pairs={{0,4},{1,5},{2,6},{3,7},{4,0},{5,1},{6,2},{7,3},{8,12},{9,13},{10,... | collective-permute-start | bytes 589832 | tf_op jit(solution)/shard_map/ppermute | solution.py:72
  38.2 11.4 %collective-permute-start.13 = (bf16[768,256]{1,0:T(8,128)(2,1)S(1)}, bf16[768,256]{1,0:T(8,128)(2,1)S(1)}, u32[]{:S(2)}, u32[]{:S(2)}) collective-permute-start(bf16[768,256]{1,0:T(8,128)(2,1)S(1)} %slice.95), channel_id=1, source_target_pairs={{0,8},{1,9},{2,10},{3,11},{4,12},{5,13},{6,14},{7,15},{8,0},{9,1},... | collective-permute-start | bytes 1179656 | tf_op jit(solution)/shard_map/ppermute | solution.py:72
  46.5 10.9 %copy-start.5 = (f32[192,256]{1,0:T(8,128)S(1)}, f32[192,256]{1,0:T(8,128)}, u32[]{:S(2)}) copy-start(f32[192,256]{1,0:T(8,128)} %param.11) | copy-start | bytes 589828
  46.5 10.8 %copy-start.6 = (f32[192,256]{1,0:T(8,128)S(1)}, f32[192,256]{1,0:T(8,128)}, u32[]{:S(2)}) copy-start(f32[192,256]{1,0:T(8,128)} %param.12) | copy-start | bytes 589828
  46.5 10.8 %copy-start.7 = (f32[192,256]{1,0:T(8,128)S(1)}, f32[192,256]{1,0:T(8,128)}, u32[]{:S(2)}) copy-start(f32[192,256]{1,0:T(8,128)} %param.13) | copy-start | bytes 589828
  46.5 10.5 %collective-permute-start.22 = (bf16[192,256]{1,0:T(8,128)(2,1)S(1)}, bf16[192,256]{1,0:T(8,128)(2,1)S(1)}, u32[]{:S(2)}, u32[]{:S(2)}) collective-permute-start(bf16[192,256]{1,0:T(8,128)(2,1)S(1)} %get-tuple-element.43), channel_id=1, source_target_pairs={{0,16},{1,17},{2,18},{3,19},{4,20},{5,21},{6,22},{7,23},{8,24},{9,... | collective-permute-start | bytes 294920 | tf_op jit(solution)/shard_map/ppermute | solution.py:72
  49.3 7.8 %collective-permute-start.23 = (bf16[192,256]{1,0:T(8,128)(2,1)S(1)}, bf16[192,256]{1,0:T(8,128)(2,1)S(1)}, u32[]{:S(2)}, u32[]{:S(2)}) collective-permute-start(bf16[192,256]{1,0:T(8,128)(2,1)S(1)} %get-tuple-element.44), channel_id=1, source_target_pairs={{0,24},{1,25},{2,26},{3,27},{4,28},{5,29},{6,30},{7,31},{8,16},{9,... | collective-permute-start | bytes 294920 | tf_op jit(solution)/shard_map/ppermute | solution.py:72
  49.7 7.3 %collective-permute-start.14 = (bf16[192,256]{1,0:T(8,128)(2,1)S(1)}, bf16[192,256]{1,0:T(8,128)(2,1)S(1)}, u32[]{:S(2)}, u32[]{:S(2)}) collective-permute-start(bf16[192,256]{1,0:T(8,128)(2,1)S(1)} %get-tuple-element.38), channel_id=1, source_target_pairs={{0,6},{1,7},{2,4},{3,5},{4,2},{5,3},{6,0},{7,1},{8,14},{9,15},{10,... | collective-permute-start | bytes 294920 | tf_op jit(solution)/shard_map/ppermute | solution.py:72
  51.8 5.4 %collective-permute-start.15 = (bf16[192,256]{1,0:T(8,128)(2,1)S(1)}, bf16[192,256]{1,0:T(8,128)(2,1)S(1)}, u32[]{:S(2)}, u32[]{:S(2)}) collective-permute-start(bf16[192,256]{1,0:T(8,128)(2,1)S(1)} %get-tuple-element.40), channel_id=1, source_target_pairs={{0,2},{1,3},{2,0},{3,1},{4,6},{5,7},{6,4},{7,5},{8,10},{9,11},{10,... | collective-permute-start | bytes 294920 | tf_op jit(solution)/shard_map/ppermute | solution.py:72
  52.6 4.7 %collective-permute-start.16 = (bf16[192,256]{1,0:T(8,128)(2,1)S(1)}, bf16[192,256]{1,0:T(8,128)(2,1)S(1)}, u32[]{:S(2)}, u32[]{:S(2)}) collective-permute-start(bf16[192,256]{1,0:T(8,128)(2,1)S(1)} %get-tuple-element.39), channel_id=1, source_target_pairs={{0,4},{1,5},{2,6},{3,7},{4,0},{5,1},{6,2},{7,3},{8,12},{9,13},{10,... | collective-permute-start | bytes 294920 | tf_op jit(solution)/shard_map/ppermute | solution.py:72
